TPU v7x, 32 devices: a whole 2x2x4 slice. The times are simulated.
32 devices in a mesh: groups: 2 (over y), pix: 8 (over z, x), mem: 2 (over core).
Axes of the slice: x: 2, y: 2, z: 4, core: 2. Of those that a mesh axis runs over, the one named last changes fastest.
Arguments:
- features: bfloat16 [2, 8192, 256], P('mem', ('groups', 'pix')), parts along dimension 1, may hold values from -6 to 6
- neighbours: int32 [9, 4096], P(None, 'pix'), may hold values from -1 to 4095, as said below
- analysis_fields: float32 [8, 8192], P(None, ('groups', 'pix')), parts along dimension 1, may hold values from -14.5 to 14.5
- depth_weight: float32 [9, 256], replicated, may hold values from -2 to 2
- norm_gain: float32 [256], replicated, may hold values from 0.5 to 2
- up_weight: bfloat16 [1024, 256], P('pix'), may hold values from -0.375 to 0.375
- up_bias: float32 [1024], replicated, may hold values from -3 to 3
- down_weight: bfloat16 [1024, 256], P('pix'), may hold values from -0.1875 to 0.1875
- layer_scale: float32 [256], replicated, may hold values from 0.25 to 1
- head_matrix: bfloat16 [8, 256], replicated, may hold values from -0.375 to 0.375
Outputs:
- mean_crps: float32 [2], P('groups'), parts along dimension 0
- input_grad: bfloat16 [2, 8192, 256], P('mem', ('groups', 'pix')), parts along dimension 1
- up_grad: float32 [2048, 256], P(('groups', 'pix')), parts along dimension 0
- down_grad: float32 [2048, 256], P(('groups', 'pix')), parts along dimension 0
- depth_grad: float32 [18, 256], P('groups'), parts along dimension 0
- head_grad: float32 [16, 256], P('groups'), parts along dimension 0
There are 2 independent parts, one for each index of `groups`. A program takes and returns all parts, laid end to end along the dimension named above; an argument that names none is the same for every part. Nothing has to cross between parts.
Inputs may be any that keep to these rules, and one draw needn't show every extreme that they name: neighbours[t, p] is the pixel at tap t of pixel p; tap 4 is p itself. It lies in the same block of 512 consecutive pixels as p or in the block just before or after it. Taps mirror: wherever neighbours[t, p] = q >= 0, neighbours[8 - t, q] = p.
All inputs are finite; a program needn't handle non-finite values.
Results may differ from a plain program's by a relative error of at most 0.0095.
Values may be sent and summed in bfloat16 or wider, within the bound.
No kernel may reach another device: no remote copies, remote signals or barrier semaphores. Data moves between devices by JAX's collectives and lax.ppermute only.
A program may use at most 64 MiB of HBM per device.

v0:
```python
import math

import jax
import jax.numpy as jnp
from jax import lax
from jax.sharding import PartitionSpec as P


def with_halo(array, sides, width):
    for axis, dim in sides:
        count, length = (lax.axis_size(axis), array.shape[dim])
        up = [(i, (i + 1) % count) for i in range(count - 1)]
        down = [(j, i) for i, j in up]
        last = lax.slice_in_dim(array, length - width, length, axis=dim)
        leading = lax.slice_in_dim(array, 0, width, axis=dim)
        before = lax.ppermute(last, axis, up)
        after = lax.ppermute(leading, axis, down)
        array = jnp.concatenate([before, array, after], axis=dim)
    return array


def soft_abs(values):
    return jnp.sqrt(values * values + 0.04)


def slope_of(values):
    return values / soft_abs(values)


def gelu_value(values):
    return 0.5 * values * (1.0 + lax.erf(values * 0.7071067811865476))


def gelu_slope(values):
    return (
        0.5 * (1.0 + lax.erf(values * 0.7071067811865476))
        + values * jnp.exp(-0.5 * values * values) * 0.3989422804014327
    )


def ensemble_slopes(chosen, every, target_values):
    member_total = every.shape[0]
    direct = slope_of(chosen - target_values[None]) / member_total
    paired = jnp.sum(slope_of(chosen[:, None] - every[None, :]), axis=1) / (
        member_total * (member_total - 1.0)
    )
    return (direct - paired).astype(jnp.bfloat16)


def fair_score_total(every, target_values):
    member_total = every.shape[0]
    pair_diff = every[:, None] - every[None, :]
    offdiag = (1.0 - jnp.eye(member_total, dtype=jnp.float32))[:, :, None, None]
    skill_term = jnp.sum(soft_abs(every - target_values[None]), axis=0) / member_total
    spread = jnp.sum(soft_abs(pair_diff) * offdiag, axis=(0, 1)) / (
        2.0 * member_total * (member_total - 1)
    )
    return jnp.sum(skill_term - spread)


def normalize(mixed, norm_gain):
    channel_mean = jnp.mean(mixed, axis=-1, keepdims=True)
    centred = mixed - channel_mean
    inverse_deviation = lax.rsqrt(jnp.mean(centred * centred, axis=-1, keepdims=True) + 1e-06)
    scaled_values = centred * inverse_deviation
    return (scaled_values, inverse_deviation, (scaled_values * norm_gain).astype(jnp.bfloat16))


def norm_backward(normed_grad, scaled_values, inverse_deviation, norm_gain):
    gained = normed_grad * norm_gain
    centred = gained - jnp.mean(gained, axis=-1, keepdims=True)
    return (
        inverse_deviation
        * (centred - scaled_values * jnp.mean(gained * scaled_values, axis=-1, keepdims=True))
    ).astype(jnp.bfloat16)


def tap_rows(source, places, inside_mask, tap_number):
    return (
        jnp.take(source, places[tap_number], axis=1).astype(jnp.float32)
        * inside_mask[tap_number][None, :, None]
    )


def tap_mix(source, places, inside_mask, tap_weights):
    mixture = jnp.zeros((source.shape[0], places.shape[1], source.shape[2]), jnp.float32)
    for tap_number in range(places.shape[0]):
        mixture = mixture + tap_weights[tap_number] * tap_rows(
            source, places, inside_mask, tap_number
        )
    return mixture


def tap_products(source, places, inside_mask, grad_values):
    grad_float = grad_values.astype(jnp.float32)
    tap_terms = []
    for tap_number in range(places.shape[0]):
        tap_terms.append(
            jnp.sum(tap_rows(source, places, inside_mask, tap_number) * grad_float, axis=(0, 1))
        )
    return jnp.stack(tap_terms)


def local(
    features,
    neighbours,
    analysis_fields,
    depth_weight,
    norm_gain,
    up_weight,
    up_bias,
    down_weight,
    layer_scale,
    head_matrix,
):
    members_here, pixels_here, channels = features.shape
    hidden_units = up_weight.shape[0] * lax.axis_size("pix")
    position = lax.axis_index("pix")
    inside = neighbours >= 0
    places = jnp.where(inside, neighbours - (position - 1) * pixels_here, 0)
    inside_mask = inside.astype(jnp.float32)
    extended = with_halo(features, (("pix", 1),), pixels_here)
    mixed_rows = tap_mix(extended, places, inside_mask, depth_weight)
    scaled_values, inverse_deviation, normed = normalize(mixed_rows, norm_gain)
    normalized_rows = normed.reshape(-1, channels)
    row_count = normalized_rows.shape[0]

    def up_values(up_piece, first_unit):
        product = lax.dot_general(
            normalized_rows, up_piece, (((1,), (1,)), ((), ())), preferred_element_type=jnp.float32
        )
        return product + lax.dynamic_slice_in_dim(up_bias, first_unit, up_piece.shape[0])

    up_whole = lax.all_gather(up_weight, "pix", axis=0, tiled=True)
    down_whole = lax.all_gather(down_weight, "pix", axis=0, tiled=True)
    branch_sum = jnp.zeros((row_count, channels), jnp.float32)
    act_blocks = []
    for low_edge in range(0, hidden_units, 256):
        high_edge = min(low_edge + 256, hidden_units)
        preactivation_values = up_values(up_whole[low_edge:high_edge], low_edge)
        act_piece = gelu_value(preactivation_values).astype(jnp.bfloat16)
        act_blocks.append(act_piece)
        branch_sum = branch_sum + jnp.dot(
            act_piece, down_whole[low_edge:high_edge], preferred_element_type=jnp.float32
        )
    branch_sum, layer_activations = (branch_sum, jnp.concatenate(act_blocks, axis=1))
    carried_state = (
        features.astype(jnp.float32) + layer_scale * branch_sum.reshape(features.shape)
    ).astype(jnp.bfloat16)
    member_prediction = jnp.einsum(
        "hk,ftk->fht", head_matrix, carried_state, preferred_element_type=jnp.float32
    )
    mem_position = lax.axis_index("mem")
    half_pixels = pixels_here // lax.axis_size("mem")
    own_target = lax.dynamic_slice_in_dim(
        analysis_fields, mem_position * half_pixels, half_pixels, 1
    )
    grouped_values = lax.all_to_all(
        member_prediction, "mem", split_axis=2, concat_axis=0, tiled=True
    )
    accumulated_loss = fair_score_total(grouped_values, own_target)
    grouped_gradient = ensemble_slopes(grouped_values, grouped_values, own_target)
    prediction_gradient = lax.all_to_all(
        grouped_gradient, "mem", split_axis=0, concat_axis=2, tiled=True
    )
    state_grad = jnp.einsum(
        "rb,yrk->ykb", head_matrix, prediction_gradient, preferred_element_type=jnp.float32
    )
    head_contribution = jnp.einsum(
        "xjg,xgy->jy", prediction_gradient, carried_state, preferred_element_type=jnp.float32
    )
    branch_grad = (layer_scale * state_grad).astype(jnp.bfloat16).reshape(-1, channels)
    up_whole = lax.all_gather(up_weight, "pix", axis=0, tiled=True)
    down_whole = lax.all_gather(down_weight, "pix", axis=0, tiled=True)
    normed_grad = jnp.zeros((row_count, channels), jnp.float32)
    grad_blocks = []
    for low_edge in range(0, hidden_units, 256):
        high_edge = min(low_edge + 256, hidden_units)
        preactivation_values = up_values(up_whole[low_edge:high_edge], low_edge)
        act_grad = lax.dot_general(
            branch_grad,
            down_whole[low_edge:high_edge],
            (((1,), (1,)), ((), ())),
            preferred_element_type=jnp.float32,
        )
        grad_piece = (act_grad * gelu_slope(preactivation_values)).astype(jnp.bfloat16)
        grad_blocks.append(grad_piece)
        normed_grad = normed_grad + jnp.dot(
            grad_piece, up_whole[low_edge:high_edge], preferred_element_type=jnp.float32
        )
    normed_grad, pre_grads = (normed_grad, jnp.concatenate(grad_blocks, axis=1))
    mixed_grad = norm_backward(
        normed_grad.reshape(features.shape), scaled_values, inverse_deviation, norm_gain
    )
    grad_extended = with_halo(mixed_grad, (("pix", 1),), pixels_here)
    input_grad = (
        state_grad + tap_mix(grad_extended, places, inside_mask, depth_weight[::-1])
    ).astype(jnp.bfloat16)
    depth_term = tap_products(extended, places, inside_mask, mixed_grad)
    grad_scale = 1.0 / math.sqrt(
        pixels_here * lax.axis_size("pix") * members_here * lax.axis_size("mem")
    )
    up_part = lax.dot_general(
        pre_grads, normalized_rows, (((0,), (0,)), ((), ())), preferred_element_type=jnp.float32
    )
    down_part = lax.dot_general(
        layer_activations, branch_grad, (((0,), (0,)), ((), ())), preferred_element_type=jnp.float32
    )
    summed = lax.psum(
        (jnp.concatenate([up_part, down_part], axis=1) * grad_scale).astype(jnp.bfloat16), "mem"
    ).astype(jnp.float32)
    owned = lax.psum_scatter(summed, "pix", scatter_dimension=0, tiled=True)
    loss_total, head_total, depth_total = lax.psum(
        (accumulated_loss, head_contribution * grad_scale, depth_term * grad_scale), ("pix", "mem")
    )
    mean_crps = (
        loss_total / (pixels_here * lax.axis_size("pix") * analysis_fields.shape[0])
    ).reshape(1)
    return (
        mean_crps,
        input_grad,
        owned[:, :channels],
        owned[:, channels:],
        depth_total,
        head_total,
    )


def solution(mesh):
    return jax.shard_map(
        local,
        mesh=mesh,
        in_specs=(
            P("mem", ("groups", "pix"), None),
            P(None, "pix"),
            P(None, ("groups", "pix")),
            P(),
            P(),
            P("pix", None),
            P(),
            P("pix", None),
            P(),
            P(),
        ),
        out_specs=(
            P("groups"),
            P("mem", ("groups", "pix"), None),
            P(("groups", "pix"), None),
            P(("groups", "pix"), None),
            P("groups", None),
            P("groups", None),
        ),
        check_vma=False,
    )
```

profile of v0, /device:TPU:0, one launch (start us, length us, event | category | flops | bytes accessed | tf_op | source)
XLA Modules:
  0.0 268.3 jit_solution(5273278918821946037)
XLA Ops:
  7.2 4.9 %collective-permute-start = (bf16[1,512,256]{2,1,0:T(8,128)(2,1)}, bf16[1,512,256]{2,1,0:T(8,128)(2,1)S(1)}, u32[]{:S(2)}, u32[]{:S(2)}) collective-permute-start(bf16[1,512,256]{2,1,0:T(8,128)(2,1)} %param.12), channel_id=1, source_target_pairs={{0,2},{2,4},{4,6},{6,8},{8,10},{10,12},{12,14},{1,3},{3,5},{5,7},{... | collective-permute-start | bytes 786440 | tf_op jit(solution)/shard_map/ppermute | solution.py:16
  12.1 1.3 collective-permute-start.1
  13.4 0.8 subtract_select_fusion
  14.2 0.6 compare_and_fusion
  14.8 0.6 compare_and_fusion.1
  15.4 0.6 compare_and_fusion.4
  16.0 0.6 compare_and_fusion.6
  16.6 0.8 fusion.81
  17.4 1.4 fusion.91
  18.8 1.0 fusion.90
  20.0 34.2 %all_gather.8 = bf16[1024,256]{1,0:T(8,128)(2,1)S(1)} all-gather(bf16[128,256]{1,0:T(8,128)(2,1)} %param.17), channel_id=1, replica_groups=mesh['groups'=2,'pix'=8,'mem'=2] {'pix'}, dimensions={0}, use_global_device_ids=true | all-gather | bytes 589824 | tf_op jit(solution)/shard_map/all_gather | solution.py:134
  54.2 0.6 fusion.82
  54.8 33.4 %all_gather.9 = bf16[1024,256]{1,0:T(8,128)(2,1)} all-gather(bf16[128,256]{1,0:T(8,128)(2,1)} %param.19), channel_id=1, replica_groups=mesh['groups'=2,'pix'=8,'mem'=2] {'pix'}, dimensions={0}, use_global_device_ids=true | all-gather | bytes 589824 | tf_op jit(solution)/shard_map/all_gather | solution.py:135
  88.2 1.0 maximum_bitcast_fusion
  89.2 2.0 gather_fusion.8
  91.2 2.0 gather_fusion.7
  93.1 2.0 gather_fusion.6
  95.1 2.0 gather_fusion.5
  97.1 2.0 gather_fusion.4
  99.0 2.0 gather_fusion.3
  101.0 2.0 gather_fusion.2
  103.0 2.6 gather_fusion.1
  105.5 1.9 gather_fusion
  107.6 3.0 %fusion.86 = (f32[512]{0:T(512)S(1)}, f32[1,512,256]{2,1,0:T(8,128)S(1)}) fusion(f32[512]{0:T(512)S(1)} %bitcast.238, bf16[512,256]{1,0:T(8,128)(2,1)S(1)} %gather_fusion.8, pred[512]{0:T(512)(128)(4,1)} %get-tuple-element.107, f32[256]{0:T(256)S(1)} %bitcast.288, f32[512]{0:T(512)S(1)} %bitcast.232, bf16[512,256]{1,0:T(8,128)(2,1)S(1)} %gather_fusion.7, ...), kind=kLoop, calls=%fused_computation.219 | loop fusion | flops 5897728 | bytes 2917888 | tf_op jit(solution)/shard_map/reduce_sum | solution.py:62
  111.1 1.1 multiply_convert_fusion.1
  112.2 1.1 multiply_convert_fusion.2
  113.4 1.1 multiply_convert_fusion.3
  114.5 1.1 multiply_convert_fusion.4
  117.2 0.5 broadcast.267
  117.7 2.1 reduce.5
  119.8 1.1 reshape.487
  120.9 3.9 %all_to_all.33 = f32[2,1,2048]{2,1,0:T(1,128)S(1)} all-to-all(f32[2,1,2048]{2,1,0:T(1,128)S(1)} %reshape.487), channel_id=1, replica_groups=mesh['groups'=2,'pix'=8,'mem'=2] {'mem'}, dimensions={0} | all-to-all | bytes 32768 | tf_op jit(solution)/shard_map/all_to_all | solution.py:158
  124.8 0.7 reduce.6
  125.5 0.4 reshape.488
  126.2 3.7 %all_to_all.34 = bf16[2,8,256]{2,1,0:T(8,128)(2,1)S(1)} all-to-all(bf16[2,8,256]{2,1,0:T(8,128)(2,1)S(1)} %get-tuple-element.80), channel_id=1, replica_groups=mesh['groups'=2,'pix'=8,'mem'=2] {'mem'}, dimensions={0} | all-to-all | bytes 16384 | tf_op jit(solution)/shard_map/all_to_all | solution.py:163
  129.9 1.7 multiply_convert_fusion
  131.6 1.8 fusion.19
  133.9 0.3 fusion.8
  135.5 0.5 fusion.11
  136.0 1.3 fusion
  137.4 19.5 %all-reduce.3.cloned.1.call-done = bf16[1024,512]{0,1:T(8,128)(2,1)} async-done(((bf16[1024,512]{0,1:T(8,128)(2,1)}), bf16[1024,512]{0,1:T(8,128)(2,1)}) %all-reduce.3.cloned.1.call-update) | async-done | bytes 1048592 | tf_op jit(solution)/shard_map/psum | solution.py:209
  156.9 2.8 %convert_element_type.164 = f32[1024,512]{0,1:T(8,128)} convert(bf16[1024,512]{0,1:T(8,128)(2,1)} %all-reduce.3.cloned.1.call-done) | non-fusion elementwise | flops 524288 | bytes 3145728 | tf_op jit(solution)/shard_map/convert_element_type | solution.py:211
  160.0 1.2 convolution_add_fusion.2
  161.5 0.4 fusion.52
  162.2 3.2 %fusion.51 = (f32[256]{0:T(256)S(1)}, f32[256]{0:T(256)S(1)}, f32[256]{0:T(256)S(1)}, f32[256]{0:T(256)S(1)}, f32[256]{0:T(256)S(1)}, /*index=5*/f32[256]{0:T(256)S(1)}, bf16[1,512,256]{2,1,0:T(8,128)(2,1)S(1)}) fusion(f32[512]{0:T(512)S(1)} %bitcast.239, bf16[512,256]{1,0:T(8,128)(2,1)S(1)} %gather_fusion.8, pred[512]{0:T(512)(128)(4,1)} %get-tuple-element.107, ...), kind=kLoop, calls=%fused_computation.101 | loop fusion | flops 4979200 | bytes 2913280 | tf_op jit(solution)/shard_map/reduce_sum | solution.py:99
  165.4 1.3 collective-permute-start.3
  166.7 4.6 %collective-permute-start.2 = (bf16[1,512,256]{2,1,0:T(8,128)(2,1)S(1)}, bf16[1,512,256]{2,1,0:T(8,128)(2,1)S(1)}, u32[]{:S(2)}, u32[]{:S(2)}) collective-permute-start(bf16[1,512,256]{2,1,0:T(8,128)(2,1)S(1)} %get-tuple-element.57), channel_id=1, source_target_pairs={{0,2},{2,4},{4,6},{6,8},{8,10},{10,12},{12,14},{1,3},{3,5},{5,7},{... | collective-permute-start | bytes 786440 | tf_op jit(solution)/shard_map/ppermute | solution.py:16
  171.3 0.6 fusion.50
  172.1 0.6 subtract_reduce_fusion
  172.7 61.1 %all-reduce = (f32[]{:T(128)}, f32[9,256]{1,0:T(8,128)}, f32[8,256]{1,0:T(8,128)}) all-reduce(f32[]{:T(128)} %subtract_reduce_fusion, f32[9,256]{1,0:T(8,128)S(1)} %broadcast_multiply_fusion, f32[8,256]{1,0:T(8,128)S(1)} %convolution_multiply_fusion.4), channel_id=1, replica_groups=mesh['groups'=2,'pix'=8,'mem'=2] {'pix','mem'}, use_global_device_ids=true, to_apply=%region_5.7 | all-reduce | flops 4353 | bytes 34824 | tf_op jit(solution)/shard_map/psum | solution.py:213
  234.5 1.0 maximum_bitcast_fusion.1
  235.5 2.0 gather_fusion.17
  237.5 2.0 gather_fusion.16
  239.4 2.0 gather_fusion.15
  241.4 2.0 gather_fusion.14
  243.3 2.0 gather_fusion.13
  245.3 2.0 gather_fusion.12
  247.3 2.0 gather_fusion.11
  249.4 2.0 gather_fusion.10
  251.3 2.6 gather_fusion.9
  254.1 3.8 %fusion.55 = bf16[1,512,256]{2,1,0:T(8,128)(2,1)} fusion(f32[512,256]{1,0:T(8,128)S(1)} %copy-done.4, bf16[512,256]{1,0:T(8,128)(2,1)S(1)} %gather_fusion.17, bf16[512,256]{1,0:T(8,128)(2,1)S(1)} %gather_fusion.16, bf16[512,256]{1,0:T(8,128)(2,1)S(1)} %gather_fusion.15, bf16[512,256]{1,0:T(8,128)(2,1)S(1)} %gather_fusion.14, ...), kind=kLoop, calls=%fused_computation.108 | loop fusion | flops 6029312 | bytes 3177984 | tf_op jit(solution)/shard_map/convert_element_type | solution.py:198
  257.8 1.0 fusion.87
  258.8 0.8 copy.51
  259.6 0.8 copy.50
  (171 shorter events, 5.2 us)
Async XLA Ops:
  7.2 47.1 %copy-start = (f32[8,512]{1,0:T(8,128)S(1)}, f32[8,512]{1,0:T(8,128)}, u32[]{:S(2)}) copy-start(f32[8,512]{1,0:T(8,128)} %param.14) | copy-start | bytes 49156
  7.2 149.7 %all-reduce.3.cloned.1.call-start = ((), (), s32[]{:S(2)}) async-start(), calls=%async_computation.3 | async-start | bytes 2097152 | tf_op jit(solution)/shard_map/psum | solution.py:209
  7.2 81.0 %collective-permute-start = (bf16[1,512,256]{2,1,0:T(8,128)(2,1)}, bf16[1,512,256]{2,1,0:T(8,128)(2,1)S(1)}, u32[]{:S(2)}, u32[]{:S(2)}) collective-permute-start(bf16[1,512,256]{2,1,0:T(8,128)(2,1)} %param.12), channel_id=1, source_target_pairs={{0,2},{2,4},{4,6},{6,8},{8,10},{10,12},{12,14},{1,3},{3,5},{5,7},{... | collective-permute-start | bytes 786440 | tf_op jit(solution)/shard_map/ppermute | solution.py:16
  12.1 76.1 %collective-permute-start.1 = (bf16[1,512,256]{2,1,0:T(8,128)(2,1)}, bf16[1,512,256]{2,1,0:T(8,128)(2,1)S(1)}, u32[]{:S(2)}, u32[]{:S(2)}) collective-permute-start(bf16[1,512,256]{2,1,0:T(8,128)(2,1)} %param.12), channel_id=1, source_target_pairs={{2,0},{4,2},{6,4},{8,6},{10,8},{12,10},{14,12},{3,1},{5,3},{7,5},{... | collective-permute-start | bytes 786440 | tf_op jit(solution)/shard_map/ppermute | solution.py:17
  14.2 93.3 %copy-start.38 = (pred[512]{0:T(512)(128)(4,1)}, pred[512]{0:T(512)(128)(4,1)S(1)}, u32[]{:S(2)}) copy-start(pred[512]{0:T(512)(128)(4,1)S(1)} %compare_and_fusion.8) | copy-start | bytes 1540
  15.4 92.1 %copy-start.40 = (pred[512]{0:T(512)(128)(4,1)}, pred[512]{0:T(512)(128)(4,1)S(1)}, u32[]{:S(2)}) copy-start(pred[512]{0:T(512)(128)(4,1)S(1)} %get-tuple-element.109) | copy-start | bytes 1540
  19.8 87.8 %copy-start.22 = (f32[1,256]{1,0:T(1,128)}, f32[1,256]{1,0:T(1,128)S(1)}, u32[]{:S(2)}) copy-start(f32[1,256]{1,0:T(1,128)S(1)} %get-tuple-element.83) | copy-start | bytes 3076
  19.8 87.8 %copy-start.24 = (f32[1,256]{1,0:T(1,128)}, f32[1,256]{1,0:T(1,128)S(1)}, u32[]{:S(2)}) copy-start(f32[1,256]{1,0:T(1,128)S(1)} %get-tuple-element.84) | copy-start | bytes 3076
  19.8 87.8 %copy-start.26 = (f32[1,256]{1,0:T(1,128)}, f32[1,256]{1,0:T(1,128)S(1)}, u32[]{:S(2)}) copy-start(f32[1,256]{1,0:T(1,128)S(1)} %get-tuple-element.85) | copy-start | bytes 3076
  19.8 87.8 %copy-start.28 = (f32[1,256]{1,0:T(1,128)}, f32[1,256]{1,0:T(1,128)S(1)}, u32[]{:S(2)}) copy-start(f32[1,256]{1,0:T(1,128)S(1)} %get-tuple-element.86) | copy-start | bytes 3076
  19.8 87.8 %copy-start.30 = (f32[1,256]{1,0:T(1,128)}, f32[1,256]{1,0:T(1,128)S(1)}, u32[]{:S(2)}) copy-start(f32[1,256]{1,0:T(1,128)S(1)} %get-tuple-element.87) | copy-start | bytes 3076
  19.8 87.8 %copy-start.32 = (f32[1,256]{1,0:T(1,128)}, f32[1,256]{1,0:T(1,128)S(1)}, u32[]{:S(2)}) copy-start(f32[1,256]{1,0:T(1,128)S(1)} %get-tuple-element.88) | copy-start | bytes 3076
  19.8 87.8 %copy-start.34 = (f32[1,256]{1,0:T(1,128)}, f32[1,256]{1,0:T(1,128)S(1)}, u32[]{:S(2)}) copy-start(f32[1,256]{1,0:T(1,128)S(1)} %get-tuple-element.89) | copy-start | bytes 3076
  19.8 87.8 %copy-start.36 = (f32[1,256]{1,0:T(1,128)}, f32[1,256]{1,0:T(1,128)S(1)}, u32[]{:S(2)}) copy-start(f32[1,256]{1,0:T(1,128)S(1)} %get-tuple-element.90) | copy-start | bytes 3076
  101.0 6.6 %copy-start.1 = (bf16[512,256]{1,0:T(8,128)(2,1)}, bf16[512,256]{1,0:T(8,128)(2,1)S(1)}, u32[]{:S(2)}) copy-start(bf16[512,256]{1,0:T(8,128)(2,1)S(1)} %gather_fusion.3) | copy-start | bytes 786436
  102.9 4.7 %copy-start.2 = (bf16[512,256]{1,0:T(8,128)(2,1)}, bf16[512,256]{1,0:T(8,128)(2,1)S(1)}, u32[]{:S(2)}) copy-start(bf16[512,256]{1,0:T(8,128)(2,1)S(1)} %gather_fusion.2) | copy-start | bytes 786436
  107.5 3.4 %copy-start.51 = (f32[256]{0:T(256)S(1)}, f32[256]{0:T(256)}, u32[]{:S(2)}) copy-start(f32[256]{0:T(256)} %param.16) | copy-start | bytes 3076
  107.6 3.5 %copy-start.56 = (f32[256]{0:T(256)S(1)}, f32[256]{0:T(256)}, u32[]{:S(2)}) copy-start(f32[256]{0:T(256)} %get-tuple-element.91) | copy-start | bytes 3076
  107.6 4.6 %copy-start.55 = (f32[256]{0:T(256)S(1)}, f32[256]{0:T(256)}, u32[]{:S(2)}) copy-start(f32[256]{0:T(256)} %get-tuple-element.94) | copy-start | bytes 3076
  110.6 2.7 %copy-start.54 = (f32[256]{0:T(256)S(1)}, f32[256]{0:T(256)}, u32[]{:S(2)}) copy-start(f32[256]{0:T(256)} %get-tuple-element.92) | copy-start | bytes 3076
  110.9 3.6 %copy-start.53 = (f32[256]{0:T(256)S(1)}, f32[256]{0:T(256)}, u32[]{:S(2)}) copy-start(f32[256]{0:T(256)} %get-tuple-element.93) | copy-start | bytes 3076
  111.1 4.4 %copy-start.5 = (bf16[1024,256]{1,0:T(8,128)(2,1)S(1)}, bf16[1024,256]{1,0:T(8,128)(2,1)}, u32[]{:S(2)}) copy-start(bf16[1024,256]{1,0:T(8,128)(2,1)} %all_gather.9) | copy-start | bytes 1572868
  112.2 4.2 %copy-start.8 = (bf16[512,256]{0,1:T(8,128)(2,1)}, bf16[512,256]{0,1:T(8,128)(2,1)S(1)}, u32[]{:S(2)}) copy-start(bf16[512,256]{0,1:T(8,128)(2,1)S(1)} %get-tuple-element.101) | copy-start | bytes 786436
  113.4 2.8 %copy-start.10 = (bf16[512,256]{0,1:T(8,128)(2,1)}, bf16[512,256]{0,1:T(8,128)(2,1)S(1)}, u32[]{:S(2)}) copy-start(bf16[512,256]{0,1:T(8,128)(2,1)S(1)} %get-tuple-element.99) | copy-start | bytes 786436
  114.5 2.0 copy-start.11
  115.6 0.9 copy-start.9
  115.6 1.0 copy-start.7
  115.6 1.0 copy-start.50
  115.8 1.1 copy-start.21
  116.1 9.9 %copy-start.57 = (f32[2,2]{1,0:T(2,128)S(1)}, f32[2,2]{1,0:T(2,128)}, u32[]{:S(2)}) copy-start(f32[2,2]{1,0:T(2,128)} %fusion.82) | copy-start | bytes 52
  131.6 1.8 copy-start.6
  131.6 1.8 copy-start.12
  131.6 2.2 copy-start.13
  133.4 1.0 copy-start.14
  133.8 1.5 copy-start.16
  133.8 1.2 copy-start.15
  134.2 1.2 copy-start.18
  134.8 0.7 copy-start.20
  137.3 120.5 %reduce-scatter.2.cloned.1.call-start = ((), (), s32[]{:S(2)}) async-start(), calls=%async_computation.4 | async-start | bytes 2359296 | tf_op jit(solution)/shard_map/reduce_scatter | solution.py:212
  159.7 1.5 copy-start.19
  159.7 1.8 copy-start.17
  159.7 1.8 copy-start.52
  162.0 9.3 %copy-start.39 = (pred[512]{0:T(512)(128)(4,1)S(1)}, pred[512]{0:T(512)(128)(4,1)}, u32[]{:S(2)}) copy-start(pred[512]{0:T(512)(128)(4,1)} %copy-done.38) | copy-start | bytes 1540
  162.0 9.3 %copy-start.41 = (pred[512]{0:T(512)(128)(4,1)S(1)}, pred[512]{0:T(512)(128)(4,1)}, u32[]{:S(2)}) copy-start(pred[512]{0:T(512)(128)(4,1)} %copy-done.40) | copy-start | bytes 1540
  162.0 9.3 %copy-start.42 = (pred[512]{0:T(512)(128)(4,1)S(1)}, pred[512]{0:T(512)(128)(4,1)}, u32[]{:S(2)}) copy-start(pred[512]{0:T(512)(128)(4,1)} %get-tuple-element.110) | copy-start | bytes 1540
  165.3 69.1 %copy-start.3 = (bf16[1,512,256]{2,1,0:T(8,128)(2,1)}, bf16[1,512,256]{2,1,0:T(8,128)(2,1)S(1)}, u32[]{:S(2)}) copy-start(bf16[1,512,256]{2,1,0:T(8,128)(2,1)S(1)} %get-tuple-element.57) | copy-start | bytes 786436
  165.4 69.1 %collective-permute-start.3 = (bf16[1,512,256]{2,1,0:T(8,128)(2,1)S(1)}, bf16[1,512,256]{2,1,0:T(8,128)(2,1)S(1)}, u32[]{:S(2)}, u32[]{:S(2)}) collective-permute-start(bf16[1,512,256]{2,1,0:T(8,128)(2,1)S(1)} %get-tuple-element.57), channel_id=1, source_target_pairs={{2,0},{4,2},{6,4},{8,6},{10,8},{12,10},{14,12},{3,1},{5,3},{7,5},{... | collective-permute-start | bytes 786440 | tf_op jit(solution)/shard_map/ppermute | solution.py:17
  166.7 67.8 %collective-permute-start.2 = (bf16[1,512,256]{2,1,0:T(8,128)(2,1)S(1)}, bf16[1,512,256]{2,1,0:T(8,128)(2,1)S(1)}, u32[]{:S(2)}, u32[]{:S(2)}) collective-permute-start(bf16[1,512,256]{2,1,0:T(8,128)(2,1)S(1)} %get-tuple-element.57), channel_id=1, source_target_pairs={{0,2},{2,4},{4,6},{6,8},{8,10},{10,12},{12,14},{1,3},{3,5},{5,7},{... | collective-permute-start | bytes 786440 | tf_op jit(solution)/shard_map/ppermute | solution.py:16
  249.2 4.7 %copy-start.4 = (f32[512,256]{1,0:T(8,128)S(1)}, f32[512,256]{1,0:T(8,128)}, u32[]{:S(2)}) copy-start(f32[512,256]{1,0:T(8,128)} %get-tuple-element.104) | copy-start | bytes 1572868
  249.2 4.7 %copy-start.23 = (f32[1,256]{1,0:T(1,128)S(1)}, f32[1,256]{1,0:T(1,128)}, u32[]{:S(2)}) copy-start(f32[1,256]{1,0:T(1,128)} %copy-done.22) | copy-start | bytes 3076
  249.2 4.7 %copy-start.25 = (f32[1,256]{1,0:T(1,128)S(1)}, f32[1,256]{1,0:T(1,128)}, u32[]{:S(2)}) copy-start(f32[1,256]{1,0:T(1,128)} %copy-done.24) | copy-start | bytes 3076
  249.3 4.7 %copy-start.27 = (f32[1,256]{1,0:T(1,128)S(1)}, f32[1,256]{1,0:T(1,128)}, u32[]{:S(2)}) copy-start(f32[1,256]{1,0:T(1,128)} %copy-done.26) | copy-start | bytes 3076
  249.3 4.7 %copy-start.29 = (f32[1,256]{1,0:T(1,128)S(1)}, f32[1,256]{1,0:T(1,128)}, u32[]{:S(2)}) copy-start(f32[1,256]{1,0:T(1,128)} %copy-done.28) | copy-start | bytes 3076
  249.3 4.7 %copy-start.31 = (f32[1,256]{1,0:T(1,128)S(1)}, f32[1,256]{1,0:T(1,128)}, u32[]{:S(2)}) copy-start(f32[1,256]{1,0:T(1,128)} %copy-done.30) | copy-start | bytes 3076
  249.3 4.7 %copy-start.33 = (f32[1,256]{1,0:T(1,128)S(1)}, f32[1,256]{1,0:T(1,128)}, u32[]{:S(2)}) copy-start(f32[1,256]{1,0:T(1,128)} %copy-done.32) | copy-start | bytes 3076
  249.3 4.7 %copy-start.35 = (f32[1,256]{1,0:T(1,128)S(1)}, f32[1,256]{1,0:T(1,128)}, u32[]{:S(2)}) copy-start(f32[1,256]{1,0:T(1,128)} %copy-done.34) | copy-start | bytes 3076
  249.3 4.7 %copy-start.37 = (f32[1,256]{1,0:T(1,128)S(1)}, f32[1,256]{1,0:T(1,128)}, u32[]{:S(2)}) copy-start(f32[1,256]{1,0:T(1,128)} %copy-done.36) | copy-start | bytes 3076
  249.3 4.7 %copy-start.43 = (pred[512]{0:T(512)(128)(4,1)S(1)}, pred[512]{0:T(512)(128)(4,1)}, u32[]{:S(2)}) copy-start(pred[512]{0:T(512)(128)(4,1)} %get-tuple-element.110) | copy-start | bytes 1540
  249.3 4.7 %copy-start.44 = (pred[512]{0:T(512)(128)(4,1)S(1)}, pred[512]{0:T(512)(128)(4,1)}, u32[]{:S(2)}) copy-start(pred[512]{0:T(512)(128)(4,1)} %get-tuple-element.107) | copy-start | bytes 1540
  249.3 4.7 %copy-start.45 = (pred[512]{0:T(512)(128)(4,1)S(1)}, pred[512]{0:T(512)(128)(4,1)}, u32[]{:S(2)}) copy-start(pred[512]{0:T(512)(128)(4,1)} %get-tuple-element.108) | copy-start | bytes 1540
  249.3 4.7 %copy-start.46 = (pred[512]{0:T(512)(128)(4,1)S(1)}, pred[512]{0:T(512)(128)(4,1)}, u32[]{:S(2)}) copy-start(pred[512]{0:T(512)(128)(4,1)} %get-tuple-element.111) | copy-start | bytes 1540
  249.4 4.7 %copy-start.47 = (pred[512]{0:T(512)(128)(4,1)S(1)}, pred[512]{0:T(512)(128)(4,1)}, u32[]{:S(2)}) copy-start(pred[512]{0:T(512)(128)(4,1)} %get-tuple-element.112) | copy-start | bytes 1540
  249.4 4.7 %copy-start.48 = (pred[512]{0:T(512)(128)(4,1)S(1)}, pred[512]{0:T(512)(128)(4,1)}, u32[]{:S(2)}) copy-start(pred[512]{0:T(512)(128)(4,1)} %get-tuple-element.113) | copy-start | bytes 1540
  249.4 4.7 %copy-start.49 = (pred[512]{0:T(512)(128)(4,1)S(1)}, pred[512]{0:T(512)(128)(4,1)}, u32[]{:S(2)}) copy-start(pred[512]{0:T(512)(128)(4,1)} %get-tuple-element.114) | copy-start | bytes 1540
Sparse Core Ops, SparseCore 0:
  137.4 19.4 all-reduce.2
  160.8 73.3 reduce-scatter.1
where the time goes:
time: 270 us; the launch traced here: 268 us
  blocking collectives  136 us (50%)
  local copies, waits for them, and re-layouts  44.7 us (17%)
  other arithmetic  25.2 us (9%)
  waiting for transfers between devices  19.6 us (7%)
  between operations  17.1 us (6%)
  matrix products  13.3 us (5%)
  starting transfers between devices  12.1 us (4%)
    psum x1, blocking collectives, local(): lax.psum((accumulated_loss, head_contribution * grad_scale, depth_term *...  61.1 us
    gather x18, local copies, waits for them, and re-layouts, tap_rows(): jnp.take(source, places[tap_number], axis=1).astype(jnp.float32)  36.4 us
    all_gather x1, blocking collectives, local(): up_whole = lax.all_gather(up_weight, 'pix', axis=0, tiled=True)  34.2 us
    all_gather x1, blocking collectives, local(): down_whole = lax.all_gather(down_weight, 'pix', axis=0, tiled=True)  33.4 us
    psum x1, waiting for transfers between devices, local(): lax.psum((jnp.concatenate([up_part, down_part], axis=1) * grad_scale).ast...  19.5 us
    ppermute x2, starting transfers between devices, with_halo(): before = lax.ppermute(last, axis, up)  9.42 us
  transfers between devices with their start and end apart: 6, of which 1 were waited for; matrix products, arithmetic and copies ran while one was open for 14% of the time, Pallas kernels for 0%

commit v1 on v0

v1 whole, which is shorter than its diff:
```python
import math

import jax
import jax.numpy as jnp
from jax import lax
from jax.experimental import pallas as pl
from jax.experimental.pallas import tpu as pltpu
from jax.sharding import PartitionSpec as P

F32 = jnp.float32
BF16 = jnp.bfloat16
LANES = 128
EXTRA = 48
NN = (((1,), (0,)), ((), ()))
NT = (((1,), (1,)), ((), ()))
TN = (((0,), (0,)), ((), ()))


def mul(a, b, dims=NN):
    return lax.dot_general(a, b, dims, preferred_element_type=F32)


def params(mib):
    return pltpu.CompilerParams(vmem_limit_bytes=mib * 2**20)


def halves(values):
    high = values.astype(BF16)
    return high, (values - high.astype(F32)).astype(BF16)


def tap_rows(places, extended, tap):
    rows, count = places.shape[0], extended.shape[0]
    column = lax.broadcasted_iota(jnp.int32, (rows, count), 1)
    chosen = (column == places[:, tap : tap + 1]).astype(F32).astype(BF16)
    return mul(chosen, extended)


def row_mean(values):
    return jnp.mean(values, axis=-1, keepdims=True)


def mix_kernel(before, own, after, places, weights, gain, taken, mixed_out, normed_out):
    extended = jnp.concatenate([before[...], own[...], after[...]], axis=0)
    where = places[...]
    mixed = jnp.zeros(own.shape, F32)
    for tap in range(weights.shape[0]):
        rows = tap_rows(where, extended, tap)
        taken[tap] = rows.astype(BF16)
        mixed = mixed + weights[tap : tap + 1, :] * rows
    mixed_out[...] = mixed
    centred = mixed - row_mean(mixed)
    inverse = lax.rsqrt(row_mean(centred * centred) + 1e-06)
    normed_out[...] = (centred * inverse * gain[...]).astype(BF16)


def forward_kernel(
    normed, up, bias, down, scale, head, features, act_out, slope_out, reach_out, forecast_out
):
    weighed = head[...].astype(F32) * scale[...]
    high, low = halves(weighed)
    reach = mul(jnp.concatenate([high, low], axis=0), down[...], NT)
    reach = reach[:8] + reach[8:]
    high, low = halves(reach)
    both = jnp.concatenate([high, low], axis=0)
    reach_out[...] = both
    rows = normed[...]
    total = mul(head[...], features[...], NT)
    hidden = up.shape[0]
    for low_edge in range(0, hidden, 256):
        piece = slice(low_edge, low_edge + 256)
        pre = mul(rows, up[piece, :], NT) + bias[:, piece]
        phi = 0.5 + 0.5 * lax.erf(pre * 0.7071067811865476)
        act = (pre * phi).astype(BF16)
        act_out[:, piece] = act
        slope_out[:, piece] = phi + pre * jnp.exp(-0.5 * pre * pre) * 0.3989422804014327
        part = mul(both[:, piece], act, NT)
        total = total + part[:8] + part[8:]
    forecast_out[...] = total


def soft_abs(values):
    return jnp.sqrt(values * values + 0.04)


def backward_kernel(
    mine, other, target, reach, slope, up, mixed, gain, mixed_grad, pre_out, grad_out, loss_out
):
    apart = mine[...] - target[...]
    spread = mine[...] - other[...]
    apart_abs, spread_abs = soft_abs(apart), soft_abs(spread)
    grad = (0.5 * (apart / apart_abs) - 0.5 * (spread / spread_abs)).astype(BF16)
    grad_out[...] = grad
    loss = jnp.sum(0.5 * apart_abs - 0.25 * spread_abs)
    loss_out[...] = jnp.full(loss_out.shape, loss, F32)
    twice = jnp.concatenate([grad.astype(F32), grad.astype(F32)], axis=0).T.astype(BF16)
    normed_grad = jnp.zeros(mixed.shape, F32)
    for low_edge in range(0, up.shape[0], 256):
        piece = slice(low_edge, low_edge + 256)
        act_grad = mul(twice, reach[:, piece])
        pre = (act_grad * slope[:, piece]).astype(BF16)
        pre_out[:, piece] = pre
        normed_grad = normed_grad + mul(pre, up[piece, :])
    values = mixed[...]
    centred = values - row_mean(values)
    inverse = lax.rsqrt(row_mean(centred * centred) + 1e-06)
    z = centred * inverse
    gained = normed_grad * gain[...]
    mixed_grad[...] = (
        inverse * (gained - row_mean(gained) - z * row_mean(gained * z))
    ).astype(BF16)


def weights_kernel(
    pre_grad, normed, act, grad, features, down, scale, taken, mixed_grad, loss, pay
):
    blocks = pay.shape[1]
    normed_t = normed[...].astype(F32).T.astype(BF16)
    summed = mul(grad[...], act[...])
    high, low = halves(summed)
    through = mul(jnp.concatenate([high, low], axis=0), down[...])
    head_part = mul(grad[...], features[...]) + scale[...] * (through[:8] + through[8:])
    flow = mixed_grad[...].astype(F32)
    depth = [
        jnp.sum(taken[tap].astype(F32) * flow, axis=0, keepdims=True)
        for tap in range(taken.shape[0])
    ]
    small = jnp.concatenate([head_part] + depth, axis=0)
    for block in range(blocks):
        lanes = slice(block * LANES, (block + 1) * LANES)
        up_part = mul(normed_t, pre_grad[:, lanes])
        for half in range(2):
            pay[half, block, :LANES, :] = up_part[half * LANES : (half + 1) * LANES].astype(BF16)
            extra = jnp.concatenate(
                [
                    small[:, half * LANES : (half + 1) * LANES],
                    loss[...],
                    summed[4 * half : 4 * half + 4, lanes],
                    jnp.zeros((2, LANES), F32),
                ],
                axis=0,
            )
            high, low = halves(extra)
            pay[half, block, LANES:, :] = jnp.concatenate([high, low], axis=0)


def input_kernel(before, own, after, places, weights, grad, head, out):
    extended = jnp.concatenate([before[...], own[...], after[...]], axis=0)
    where = places[...]
    taps = weights.shape[0]
    total = mul(grad[...].astype(F32).T.astype(BF16), head[...])
    for tap in range(taps):
        total = total + weights[taps - 1 - tap : taps - tap, :] * tap_rows(where, extended, tap)
    out[...] = total.astype(BF16)


def call(kernel, outs, mib, *operands):
    return pl.pallas_call(
        kernel,
        out_shape=tuple(jax.ShapeDtypeStruct(shape, dtype) for shape, dtype in outs),
        compiler_params=params(mib),
    )(*operands)


def neighbour_blocks(array):
    count = lax.axis_size("pix")
    up = [(i, i + 1) for i in range(count - 1)]
    down = [(j, i) for i, j in up]
    return lax.ppermute(array, "pix", up), lax.ppermute(array, "pix", down)


def swap(array):
    return lax.ppermute(array, "mem", [(0, 1), (1, 0)])


def gather_weights(up_weight, down_weight, member):
    count, rows = lax.axis_size("pix"), up_weight.shape[0]
    if rows % 32 != 0:
        return (
            lax.all_gather(up_weight, "pix", axis=0, tiled=True),
            lax.all_gather(down_weight, "pix", axis=0, tiled=True),
        )
    both = jnp.stack([up_weight, down_weight])
    half = rows // 2
    mine = lax.dynamic_slice_in_dim(both, member * half, half, 1)
    mine = jnp.broadcast_to(mine[None], (count,) + mine.shape)
    mine = lax.all_to_all(mine, "pix", split_axis=0, concat_axis=0)
    other = swap(mine)
    first = jnp.where(member == 0, mine, other)
    second = jnp.where(member == 0, other, mine)
    whole = jnp.stack([first, second], axis=2)
    return whole[:, 0].reshape(count * rows, -1), whole[:, 1].reshape(count * rows, -1)


def local(
    features,
    neighbours,
    analysis_fields,
    depth_weight,
    norm_gain,
    up_weight,
    up_bias,
    down_weight,
    layer_scale,
    head_matrix,
):
    pixels, channels = features.shape[1:]
    count = lax.axis_size("pix")
    owned_rows = up_weight.shape[0]
    hidden = owned_rows * count
    taps = neighbours.shape[0]
    position, member = lax.axis_index("pix"), lax.axis_index("mem")
    own = features[0]
    gain, scale, bias = norm_gain[None], layer_scale[None], up_bias[None]
    places = jnp.where(neighbours >= 0, neighbours - (position - 1) * pixels, -1).T

    before, after = neighbour_blocks(own)
    up, down = gather_weights(up_weight, down_weight, member)
    taken, mixed, normed = call(
        mix_kernel,
        [((taps, pixels, channels), BF16), ((pixels, channels), F32), ((pixels, channels), BF16)],
        40,
        before, own, after, places, depth_weight, gain,
    )
    act, slope, reach, forecast = call(
        forward_kernel,
        [((pixels, hidden), BF16), ((pixels, hidden), F32), ((16, hidden), BF16), ((8, pixels), F32)],
        40,
        normed, up, bias, down, scale, head_matrix, own,
    )
    other = swap(forecast)
    mixed_grad, pre_grad, grad, loss = call(
        backward_kernel,
        [((pixels, channels), BF16), ((pixels, hidden), BF16), ((8, pixels), BF16), ((1, LANES), F32)],
        40,
        forecast, other, analysis_fields, reach, slope, up, mixed, gain,
    )
    grad_before, grad_after = neighbour_blocks(mixed_grad)
    (pay,) = call(
        weights_kernel,
        [((2, hidden // LANES, LANES + EXTRA, LANES), BF16)],
        40,
        pre_grad, normed, act, grad, own, down, scale, taken, mixed_grad, loss,
    )
    (input_grad,) = call(
        input_kernel,
        [((pixels, channels), BF16)],
        40,
        grad_before, mixed_grad, grad_after, places, depth_weight, grad, head_matrix,
    )
    grad_scale = 1.0 / math.sqrt(pixels * count * 2)
    keep = lax.dynamic_index_in_dim(pay, member, 0, keepdims=False)
    send = lax.dynamic_index_in_dim(pay, 1 - member, 0, keepdims=False)
    block_rows = EXTRA // 2
    joined = (keep.astype(F32) + swap(send).astype(F32))
    fine = joined[:, LANES : LANES + block_rows] + joined[:, LANES + block_rows :]
    if owned_rows == LANES:
        high, low = halves(fine)
        joined = jnp.concatenate([joined[:, :LANES].astype(BF16), high, low], axis=1)
        joined = lax.all_to_all(joined, "pix", split_axis=0, concat_axis=0)
        total = jnp.sum(joined.astype(F32), axis=0)
        total = jnp.concatenate(
            [total[:LANES], total[LANES : LANES + block_rows] + total[LANES + block_rows :]], axis=0
        )
        ours, theirs = total, swap(total)
        first = jnp.where(member == 0, ours, theirs)
        second = jnp.where(member == 0, theirs, ours)
        up_grad = jnp.concatenate([first[:LANES], second[:LANES]], axis=0).T
        small = jnp.concatenate([first[LANES:], second[LANES:]], axis=1)
        summed = jnp.concatenate([first[LANES + 18 : LANES + 22], second[LANES + 18 : LANES + 22]])
    else:
        pair = jnp.stack([joined[:, :LANES], swap(joined[:, :LANES])])
        pair = jnp.where(member == 0, pair, pair[::-1])
        rows = jnp.transpose(pair, (1, 3, 0, 2)).reshape(hidden, channels)
        up_grad = lax.psum_scatter(rows, "pix", scatter_dimension=0, tiled=True)
        fine_pair = jnp.stack([fine, swap(fine)])
        fine_pair = jnp.where(member == 0, fine_pair, fine_pair[::-1])
        small = jnp.transpose(fine_pair[:, 0], (1, 0, 2)).reshape(block_rows, channels)
        small = lax.psum(small, "pix")
        summed = jnp.transpose(fine_pair[:, :, 18:22], (1, 3, 0, 2)).reshape(hidden, 8)
        summed = lax.psum_scatter(summed, "pix", scatter_dimension=0, tiled=True).T
    down_grad = layer_scale * lax.dot_general(
        summed, head_matrix.astype(F32), TN, precision=lax.Precision.HIGHEST
    )
    mean_crps = (small[17, 0] / (pixels * count * 8)).reshape(1)
    return (
        mean_crps,
        input_grad[None],
        up_grad * grad_scale,
        down_grad * grad_scale,
        small[8 : 8 + taps] * grad_scale,
        small[:8] * grad_scale,
    )


def solution(mesh):
    return jax.shard_map(
        local,
        mesh=mesh,
        in_specs=(
            P("mem", ("groups", "pix"), None),
            P(None, "pix"),
            P(None, ("groups", "pix")),
            P(),
            P(),
            P("pix", None),
            P(),
            P("pix", None),
            P(),
            P(),
        ),
        out_specs=(
            P("groups"),
            P("mem", ("groups", "pix"), None),
            P(("groups", "pix"), None),
            P(("groups", "pix"), None),
            P("groups", None),
            P("groups", None),
        ),
        check_vma=False,
    )
```

time: 270 us -> 81.6 us (0.30)
  the two profiles are of different devices: /device:TPU:0 before, /device:TPU:16 now
where the time goes in v1:
time: 81.6 us; the launch traced here: 81 us
  waiting for transfers between devices  27.1 us (33%)
  starting transfers between devices  24.6 us (30%)
  Pallas kernels  12.3 us (15%)
  local copies, waits for them, and re-layouts  7.13 us (9%)
  other arithmetic  6.14 us (8%)
  between operations  2.73 us (3%)
  matrix products  0.92 us (1%)
    ppermute x4, waiting for transfers between devices, neighbour_blocks(): return (lax.ppermute(array, 'pix', up), lax.ppermute(array, 'pix', down))  16.5 us
    ppermute x4, starting transfers between devices, neighbour_blocks(): return (lax.ppermute(array, 'pix', up), lax.ppermute(array, 'pix', down))  13.6 us
    pallas_call x5, Pallas kernels, call(): pl.pallas_call(kernel, out_shape=tuple((jax.ShapeDtypeStruct(shape, dtype...  12.3 us
    all_to_all x1, starting transfers between devices, gather_weights(): mine = lax.all_to_all(mine, 'pix', split_axis=0, concat_axis=0)  6.14 us
    all_to_all x1, waiting for transfers between devices, gather_weights(): mine = lax.all_to_all(mine, 'pix', split_axis=0, concat_axis=0)  5.92 us
    unnamed x27, local copies, waits for them, and re-layouts  5.25 us
    all_to_all x1, starting transfers between devices, local(): joined = lax.all_to_all(joined, 'pix', split_axis=0, concat_axis=0)  4.5 us
    ppermute x4, waiting for transfers between devices, swap(): return lax.ppermute(array, 'mem', [(0, 1), (1, 0)])  2.7 us
  transfers between devices with their start and end apart: 10, of which 8 were waited for; matrix products, arithmetic and copies ran while one was open for 2% of the time, Pallas kernels for 11%

profile of v1, /device:TPU:16, one launch (start us, length us, event | category | flops | bytes accessed | tf_op | source)
XLA Modules:
  0.0 81.0 jit_solution(12532583678553001353)
XLA Ops:
  0.6 0.0 copy-start
  0.6 0.0 copy-start.12
  0.7 0.0 copy-start.7
  0.7 0.8 %fusion.3 = bf16[2,64,256]{2,1,0:T(8,128)(2,1)S(1)} fusion(s32[]{:T(128)S(6)} %select_n.41, bf16[1,128,256]{2,1,0:T(8,128)(2,1)} %bitcast.39, bf16[1,128,256]{2,1,0:T(8,128)(2,1)} %bitcast.40), kind=kLoop, calls=%fused_computation.21 | loop fusion | flops 131072 | bytes 196612 | tf_op jit(solution)/shard_map/stack | solution.py:183
  1.5 0.9 %broadcast_in_dim.25 = bf16[8,2,64,256]{3,2,1,0:T(8,128)(2,1)} broadcast(bf16[2,64,256]{2,1,0:T(8,128)(2,1)S(1)} %fusion.3), dimensions={1,2,3} | broadcast | bytes 589824 | tf_op jit(solution)/shard_map/broadcast_in_dim | solution.py:186
  2.4 6.1 %all-to-all-start = ((bf16[8,2,64,256]{3,2,1,0:T(8,128)(2,1)}), bf16[8,2,64,256]{3,2,1,0:T(8,128)(2,1)S(1)}, u32[]{:S(2)}, u32[]{:S(2)}) async-start(bf16[8,2,64,256]{3,2,1,0:T(8,128)(2,1)} %broadcast_in_dim.25), calls=%async_computation | async-start | bytes 1048576 | tf_op jit(solution)/shard_map/all_to_all | solution.py:187
  8.5 3.4 %collective-permute-start = (bf16[512,256]{1,0:T(8,128)(2,1)}, bf16[512,256]{1,0:T(8,128)(2,1)S(1)}, u32[]{:S(2)}, u32[]{:S(2)}) collective-permute-start(bf16[512,256]{1,0:T(8,128)(2,1)} %bitcast.28), channel_id=1, source_target_pairs={{0,2},{2,4},{4,6},{6,8},{8,10},{10,12},{12,14},{1,3},{3,5},{5,7},{... | collective-permute-start | bytes 786440 | tf_op jit(solution)/shard_map/ppermute | solution.py:169
  11.9 3.4 %collective-permute-start.1 = (bf16[512,256]{1,0:T(8,128)(2,1)}, bf16[512,256]{1,0:T(8,128)(2,1)S(1)}, u32[]{:S(2)}, u32[]{:S(2)}) collective-permute-start(bf16[512,256]{1,0:T(8,128)(2,1)} %bitcast.29), channel_id=1, source_target_pairs={{2,0},{4,2},{6,4},{8,6},{10,8},{12,10},{14,12},{3,1},{5,3},{7,5},{... | collective-permute-start | bytes 786440 | tf_op jit(solution)/shard_map/ppermute | solution.py:169
  15.2 5.9 %all-to-all-done = bf16[8,2,64,256]{3,2,1,0:T(8,128)(2,1)S(1)} async-done(((bf16[8,2,64,256]{3,2,1,0:T(8,128)(2,1)}), bf16[8,2,64,256]{3,2,1,0:T(8,128)(2,1)S(1)}, u32[]{:S(2)}, u32[]{:S(2)}) %all-to-all-start) | async-done | bytes 524320 | tf_op jit(solution)/shard_map/all_to_all | solution.py:187
  21.2 0.0 collective-permute-start.2
  21.2 0.8 broadcast_subtract_fusion
  21.9 0.8 broadcast_compare_fusion
  22.7 0.1 copy.30
  22.8 0.2 copy.29
  23.1 4.2 %collective-permute-done.before = bf16[512,256]{1,0:T(8,128)(2,1)S(1)} collective-permute-done((bf16[512,256]{1,0:T(8,128)(2,1)}, bf16[512,256]{1,0:T(8,128)(2,1)S(1)}, u32[]{:S(2)}, u32[]{:S(2)}) %collective-permute-start) | collective-permute-done | bytes 262176 | tf_op jit(solution)/shard_map/ppermute | solution.py:169
  27.3 1.6 %collective-permute-done.1.after = bf16[512,256]{1,0:T(8,128)(2,1)S(1)} collective-permute-done((bf16[512,256]{1,0:T(8,128)(2,1)}, bf16[512,256]{1,0:T(8,128)(2,1)S(1)}, u32[]{:S(2)}, u32[]{:S(2)}) %collective-permute-start.1) | collective-permute-done | bytes 262176 | tf_op jit(solution)/shard_map/ppermute | solution.py:169
  28.9 0.0 copy-done
  28.9 0.0 copy-done.12
  28.9 0.0 copy-done.7
  28.9 4.1 %shard_map.145 = (bf16[9,512,256]{2,1,0:T(8,128)(2,1)S(1)}, f32[512,256]{1,0:T(8,128)S(1)}, bf16[512,256]{1,0:T(8,128)(2,1)S(1)}) custom-call(bf16[512,256]{1,0:T(8,128)(2,1)S(1)} %collective-permute-done.before, bf16[512,256]{1,0:T(8,128)(2,1)S(1)} %bitcast.30, bf16[512,256]{1,0:T(8,128)(2,1)S(1)} %collective-permute-done.1.after, ...), custom_call_target="tpu_custom_call" | custom-call | tf_op jit(solution)/shard_map/pallas_call | solution.py:158
  33.0 0.0 copy-start.1
  33.0 0.0 copy-start.5
  33.1 0.0 collective-permute-done.2
  33.1 1.5 %select_bitcast_fusion = (bf16[8,2,1,64,256]{4,3,1,0,2:T(8,128)(2,1)S(1)}, bf16[8,2,1,64,256]{4,3,1,0,2:T(8,128)(2,1)S(1)}) fusion(bf16[8,2,64,256]{3,2,1,0:T(8,128)(2,1)} %collective-permute-done.2, bf16[8,2,64,256]{3,2,1,0:T(8,128)(2,1)S(1)} %all-to-all-done, pred[]{:T(512)S(6)} %eq.2), kind=kLoop, calls=%fused_computation.9 | loop fusion | flops 524288 | bytes 2097153 | tf_op jit(solution)/shard_map/stack | solution.py:191
  34.6 0.0 copy-start.8
  34.6 0.0 copy-start.10
  34.6 0.0 copy-start.11
  34.6 0.1 pad_maximum_fusion
  34.7 0.0 copy-start.9
  34.8 0.0 copy-done.1
  34.8 0.0 copy-done.5
  34.8 0.4 copy-done.8
  35.3 0.0 copy-done.10
  35.3 0.0 copy-done.11
  35.3 1.4 %shard_map.146 = (bf16[512,1024]{1,0:T(8,128)(2,1)S(1)}, f32[512,1024]{1,0:T(8,128)S(1)}, bf16[16,1024]{1,0:T(8,128)(2,1)S(1)}, f32[8,512]{1,0:T(8,128)S(1)}) custom-call(bf16[512,256]{1,0:T(8,128)(2,1)S(1)} %get-tuple-element.17.normed, bf16[1024,256]{1,0:T(8,128)(2,1)S(1)} %bitcast.26, f32[1,1024]{1,0:T(1,128)S(1)} %bitcast.35, ...), custom_call_target="tpu_custom_call" | custom-call | tf_op jit(solution)/shard_map/pallas_call | solution.py:158
  36.7 0.0 copy-start.3
  36.7 1.3 %copy-done.3 = f32[512,1024]{1,0:T(8,128)} copy-done((f32[512,1024]{1,0:T(8,128)}, f32[512,1024]{1,0:T(8,128)S(1)}, u32[]{:S(2)}) %copy-start.3) | copy-done | bytes 2097176
  38.1 0.0 collective-permute-start.3
  38.1 1.2 %collective-permute-done.3.other = f32[8,512]{1,0:T(8,128)S(1)} collective-permute-done((f32[8,512]{1,0:T(8,128)S(1)}, f32[8,512]{1,0:T(8,128)S(1)}, u32[]{:S(2)}, u32[]{:S(2)}) %collective-permute-start.3) | collective-permute-done | bytes 16416 | tf_op jit(solution)/shard_map/ppermute | solution.py:173
  39.3 0.0 copy-done.9
  39.3 1.6 %copy-done.4 = f32[512,1024]{1,0:T(8,128)S(1)} copy-done((f32[512,1024]{1,0:T(8,128)S(1)}, f32[512,1024]{1,0:T(8,128)}, u32[]{:S(2)}) %copy-start.4) | copy-done | bytes 2097176
  40.9 1.0 %copy-done.6 = f32[512,256]{1,0:T(8,128)S(1)} copy-done((f32[512,256]{1,0:T(8,128)S(1)}, f32[512,256]{1,0:T(8,128)}, u32[]{:S(2)}) %copy-start.6) | copy-done | bytes 524312
  41.9 1.0 %shard_map.147 = (bf16[512,256]{1,0:T(8,128)(2,1)S(1)}, bf16[512,1024]{1,0:T(8,128)(2,1)S(1)}, bf16[8,512]{1,0:T(8,128)(2,1)S(1)}, f32[1,128]{1,0:T(1,128)S(1)}) custom-call(f32[8,512]{1,0:T(8,128)S(1)} %get-tuple-element.18.mine, f32[8,512]{1,0:T(8,128)S(1)} %collective-permute-done.3.other, f32[8,512]{1,0:T(8,128)S(1)} %copy-done.9, ...), custom_call_target="tpu_custom_call" | custom-call | tf_op jit(solution)/shard_map/pallas_call | solution.py:158
  42.9 0.0 copy-done.2
  42.9 1.1 %shard_map.148 = bf16[2,8,176,128]{3,2,1,0:T(8,128)(2,1)S(1)} custom-call(bf16[512,1024]{1,0:T(8,128)(2,1)S(1)} %get-tuple-element.22.pre_grad, bf16[512,256]{1,0:T(8,128)(2,1)S(1)} %get-tuple-element.17.normed, bf16[512,1024]{1,0:T(8,128)(2,1)S(1)} %get-tuple-element.23.act, bf16[8,512]{1,0:T(8,128)(2,1)S(1)} %get-tuple-element.24.grad, ...), custom_call_target="tpu_custom_call" | custom-call | tf_op jit(solution)/shard_map/pallas_call | solution.py:158
  44.1 0.2 collective-permute-start.4
  44.3 1.5 %collective-permute-done.4 = bf16[8,176,128]{2,1,0:T(8,128)(2,1)S(1)} collective-permute-done((bf16[8,176,128]{2,1,0:T(8,128)(2,1)S(1)}, bf16[8,176,128]{2,1,0:T(8,128)(2,1)S(1)}, u32[]{:S(2)}, u32[]{:S(2)}) %collective-permute-start.4) | collective-permute-done | bytes 360480 | tf_op jit(solution)/shard_map/ppermute | solution.py:173
  45.8 0.1 convert_add_fusion
  46.0 0.8 pad_maximum_fusion.1
  46.7 4.5 %all-to-all-start.1 = ((bf16[8,176,128]{2,1,0:T(8,128)(2,1)}), bf16[8,176,128]{2,1,0:T(8,128)(2,1)S(1)}, u32[]{:S(2)}, u32[]{:S(2)}) async-start(bf16[8,176,128]{2,1,0:T(8,128)(2,1)} %pad_maximum_fusion.1), calls=%async_computation.1 | async-start | bytes 720896 | tf_op jit(solution)/shard_map/all_to_all | solution.py:260
  51.2 3.4 %collective-permute-start.6 = (bf16[512,256]{1,0:T(8,128)(2,1)S(1)}, bf16[512,256]{1,0:T(8,128)(2,1)S(1)}, u32[]{:S(2)}, u32[]{:S(2)}) collective-permute-start(bf16[512,256]{1,0:T(8,128)(2,1)S(1)} %get-tuple-element.26.mixed_grad.own), channel_id=1, source_target_pairs={{0,2},{2,4},{4,6},{6,8},{8,10},{10,12},{12,14},{1,3},{3,5},{5,7},{... | collective-permute-start | bytes 786440 | tf_op jit(solution)/shard_map/ppermute | solution.py:169
  54.6 3.6 %collective-permute-start.7 = (bf16[512,256]{1,0:T(8,128)(2,1)S(1)}, bf16[512,256]{1,0:T(8,128)(2,1)S(1)}, u32[]{:S(2)}, u32[]{:S(2)}) collective-permute-start(bf16[512,256]{1,0:T(8,128)(2,1)S(1)} %get-tuple-element.26.mixed_grad.own), channel_id=1, source_target_pairs={{2,0},{4,2},{6,4},{8,6},{10,8},{12,10},{14,12},{3,1},{5,3},{7,5},{... | collective-permute-start | bytes 786440 | tf_op jit(solution)/shard_map/ppermute | solution.py:169
  58.1 2.1 %all-to-all-done.1 = bf16[8,176,128]{2,1,0:T(8,128)(2,1)S(1)} async-done(((bf16[8,176,128]{2,1,0:T(8,128)(2,1)}), bf16[8,176,128]{2,1,0:T(8,128)(2,1)S(1)}, u32[]{:S(2)}, u32[]{:S(2)}) %all-to-all-start.1) | async-done | bytes 360480 | tf_op jit(solution)/shard_map/all_to_all | solution.py:260
  60.2 0.1 convert_reduce_fusion
  60.3 0.1 collective-permute-start.5
  60.4 6.4 %collective-permute-done.6.before = bf16[512,256]{1,0:T(8,128)(2,1)S(1)} collective-permute-done((bf16[512,256]{1,0:T(8,128)(2,1)S(1)}, bf16[512,256]{1,0:T(8,128)(2,1)S(1)}, u32[]{:S(2)}, u32[]{:S(2)}) %collective-permute-start.6) | collective-permute-done | bytes 262176 | tf_op jit(solution)/shard_map/ppermute | solution.py:169
  66.8 4.2 %collective-permute-done.7.after = bf16[512,256]{1,0:T(8,128)(2,1)S(1)} collective-permute-done((bf16[512,256]{1,0:T(8,128)(2,1)S(1)}, bf16[512,256]{1,0:T(8,128)(2,1)S(1)}, u32[]{:S(2)}, u32[]{:S(2)}) %collective-permute-start.7) | collective-permute-done | bytes 262176 | tf_op jit(solution)/shard_map/ppermute | solution.py:169
  71.0 4.7 %shard_map.149 = bf16[512,256]{1,0:T(8,128)(2,1)} custom-call(bf16[512,256]{1,0:T(8,128)(2,1)S(1)} %collective-permute-done.6.before, bf16[512,256]{1,0:T(8,128)(2,1)S(1)} %get-tuple-element.26.mixed_grad.own, bf16[512,256]{1,0:T(8,128)(2,1)S(1)} %collective-permute-done.7.after, s32[512,9]{1,0:T(8,128)S(1)} %select_bitcast_fusion.2.places, ...), custom_call_target="tpu_custom_call" | custom-call | tf_op jit(solution)/shard_map/pallas_call | solution.py:158
  75.7 0.0 collective-permute-done.5
  75.7 0.6 fusion.7
  76.3 0.6 fusion.6
  77.0 0.5 slice.78
  77.5 0.8 copy.33
  78.3 0.9 %fusion = f32[128,256]{1,0:T(8,128)} fusion(bf16[8,256]{1,0:T(8,128)(2,1)S(1)} %copy-done.8, f32[256]{0:T(256)S(1)} %copy-done.10, f32[4,128]{1,0:T(4,128)S(1)} %slice.82, f32[4,128]{1,0:T(4,128)S(1)} %slice.81), kind=kOutput, calls=%fused_computation.1 | convolution fusion | flops 3212288 | bytes 140288 | tf_op jit(solution)/shard_map/dot_general | solution.py:282
  (20 shorter events, 0.3 us)
Async XLA Ops:
  0.6 28.3 %copy-start = (bf16[1,512,256]{2,1,0:T(8,128)(2,1)S(1)}, bf16[1,512,256]{2,1,0:T(8,128)(2,1)}, u32[]{:S(2)}) copy-start(bf16[1,512,256]{2,1,0:T(8,128)(2,1)} %param.10) | copy-start | bytes 786436
  0.6 28.3 %copy-start.12 = (f32[256]{0:T(256)S(1)}, f32[256]{0:T(256)}, u32[]{:S(2)}) copy-start(f32[256]{0:T(256)} %param.14) | copy-start | bytes 3076
  0.7 28.2 %copy-start.7 = (f32[9,256]{1,0:T(8,128)S(1)}, f32[9,256]{1,0:T(8,128)}, u32[]{:S(2)}) copy-start(f32[9,256]{1,0:T(8,128)} %weights.3) | copy-start | bytes 27652
  2.4 18.8 %all-to-all-start = ((bf16[8,2,64,256]{3,2,1,0:T(8,128)(2,1)}), bf16[8,2,64,256]{3,2,1,0:T(8,128)(2,1)S(1)}, u32[]{:S(2)}, u32[]{:S(2)}) async-start(bf16[8,2,64,256]{3,2,1,0:T(8,128)(2,1)} %broadcast_in_dim.25), calls=%async_computation | async-start | bytes 1048576 | tf_op jit(solution)/shard_map/all_to_all | solution.py:187
  8.5 18.8 %collective-permute-start = (bf16[512,256]{1,0:T(8,128)(2,1)}, bf16[512,256]{1,0:T(8,128)(2,1)S(1)}, u32[]{:S(2)}, u32[]{:S(2)}) collective-permute-start(bf16[512,256]{1,0:T(8,128)(2,1)} %bitcast.28), channel_id=1, source_target_pairs={{0,2},{2,4},{4,6},{6,8},{8,10},{10,12},{12,14},{1,3},{3,5},{5,7},{... | collective-permute-start | bytes 786440 | tf_op jit(solution)/shard_map/ppermute | solution.py:169
  11.9 17.0 %collective-permute-start.1 = (bf16[512,256]{1,0:T(8,128)(2,1)}, bf16[512,256]{1,0:T(8,128)(2,1)S(1)}, u32[]{:S(2)}, u32[]{:S(2)}) collective-permute-start(bf16[512,256]{1,0:T(8,128)(2,1)} %bitcast.29), channel_id=1, source_target_pairs={{2,0},{4,2},{6,4},{8,6},{10,8},{12,10},{14,12},{3,1},{5,3},{7,5},{... | collective-permute-start | bytes 786440 | tf_op jit(solution)/shard_map/ppermute | solution.py:169
  21.2 11.9 %collective-permute-start.2 = (bf16[8,2,64,256]{3,2,1,0:T(8,128)(2,1)S(1)}, bf16[8,2,64,256]{3,2,1,0:T(8,128)(2,1)}, u32[]{:S(2)}, u32[]{:S(2)}) collective-permute-start(bf16[8,2,64,256]{3,2,1,0:T(8,128)(2,1)S(1)} %all-to-all-done), channel_id=1, source_target_pairs={{0,1},{1,0},{2,3},{3,2},{4,5},{5,4},{6,7},{7,6},{8,9},{9,8},{10,11... | collective-permute-start | bytes 1572872 | tf_op jit(solution)/shard_map/ppermute | solution.py:173
  33.0 1.7 %copy-start.1 = (bf16[9,512,256]{2,1,0:T(8,128)(2,1)}, bf16[9,512,256]{2,1,0:T(8,128)(2,1)S(1)}, u32[]{:S(2)}) copy-start(bf16[9,512,256]{2,1,0:T(8,128)(2,1)S(1)} %get-tuple-element.25.taken) | copy-start | bytes 7077892
  33.0 1.7 %copy-start.5 = (f32[512,256]{1,0:T(8,128)}, f32[512,256]{1,0:T(8,128)S(1)}, u32[]{:S(2)}) copy-start(f32[512,256]{1,0:T(8,128)S(1)} %get-tuple-element.21.mixed) | copy-start | bytes 1572868
  34.6 0.7 copy-start.8
  34.6 0.7 copy-start.10
  34.6 0.7 copy-start.11
  34.7 4.6 %copy-start.9 = (f32[8,512]{1,0:T(8,128)S(1)}, f32[8,512]{1,0:T(8,128)}, u32[]{:S(2)}) copy-start(f32[8,512]{1,0:T(8,128)} %target.1) | copy-start | bytes 49156
  36.7 1.3 %copy-start.3 = (f32[512,1024]{1,0:T(8,128)}, f32[512,1024]{1,0:T(8,128)S(1)}, u32[]{:S(2)}) copy-start(f32[512,1024]{1,0:T(8,128)S(1)} %get-tuple-element.20.slope) | copy-start | bytes 6291460
  38.1 1.2 %collective-permute-start.3 = (f32[8,512]{1,0:T(8,128)S(1)}, f32[8,512]{1,0:T(8,128)S(1)}, u32[]{:S(2)}, u32[]{:S(2)}) collective-permute-start(f32[8,512]{1,0:T(8,128)S(1)} %get-tuple-element.18.mine), channel_id=1, source_target_pairs={{0,1},{1,0},{2,3},{3,2},{4,5},{5,4},{6,7},{7,6},{8,9},{9,8},{10,11... | collective-permute-start | bytes 49160 | tf_op jit(solution)/shard_map/ppermute | solution.py:173
  38.1 4.8 %copy-start.2 = (bf16[9,512,256]{2,1,0:T(8,128)(2,1)S(1)}, bf16[9,512,256]{2,1,0:T(8,128)(2,1)}, u32[]{:S(2)}) copy-start(bf16[9,512,256]{2,1,0:T(8,128)(2,1)} %copy-done.1) | copy-start | bytes 7077892
  39.3 1.6 %copy-start.4 = (f32[512,1024]{1,0:T(8,128)S(1)}, f32[512,1024]{1,0:T(8,128)}, u32[]{:S(2)}) copy-start(f32[512,1024]{1,0:T(8,128)} %copy-done.3) | copy-start | bytes 6291460
  40.9 1.0 %copy-start.6 = (f32[512,256]{1,0:T(8,128)S(1)}, f32[512,256]{1,0:T(8,128)}, u32[]{:S(2)}) copy-start(f32[512,256]{1,0:T(8,128)} %copy-done.5) | copy-start | bytes 1572868
  44.1 1.7 %collective-permute-start.4 = (bf16[8,176,128]{2,1,0:T(8,128)(2,1)S(1)}, bf16[8,176,128]{2,1,0:T(8,128)(2,1)S(1)}, u32[]{:S(2)}, u32[]{:S(2)}) collective-permute-start(bf16[8,176,128]{2,1,0:T(8,128)(2,1)S(1)} %dynamic-slice_bitcast_fusion), channel_id=1, source_target_pairs={{0,1},{1,0},{2,3},{3,2},{4,5},{5,4},{6,7},{7,6},{8,9},{9,8},{10,11... | collective-permute-start | bytes 1081352 | tf_op jit(solution)/shard_map/ppermute | solution.py:173
  46.7 13.5 %all-to-all-start.1 = ((bf16[8,176,128]{2,1,0:T(8,128)(2,1)}), bf16[8,176,128]{2,1,0:T(8,128)(2,1)S(1)}, u32[]{:S(2)}, u32[]{:S(2)}) async-start(bf16[8,176,128]{2,1,0:T(8,128)(2,1)} %pad_maximum_fusion.1), calls=%async_computation.1 | async-start | bytes 720896 | tf_op jit(solution)/shard_map/all_to_all | solution.py:260
  51.2 15.6 %collective-permute-start.6 = (bf16[512,256]{1,0:T(8,128)(2,1)S(1)}, bf16[512,256]{1,0:T(8,128)(2,1)S(1)}, u32[]{:S(2)}, u32[]{:S(2)}) collective-permute-start(bf16[512,256]{1,0:T(8,128)(2,1)S(1)} %get-tuple-element.26.mixed_grad.own), channel_id=1, source_target_pairs={{0,2},{2,4},{4,6},{6,8},{8,10},{10,12},{12,14},{1,3},{3,5},{5,7},{... | collective-permute-start | bytes 786440 | tf_op jit(solution)/shard_map/ppermute | solution.py:169
  54.6 16.4 %collective-permute-start.7 = (bf16[512,256]{1,0:T(8,128)(2,1)S(1)}, bf16[512,256]{1,0:T(8,128)(2,1)S(1)}, u32[]{:S(2)}, u32[]{:S(2)}) collective-permute-start(bf16[512,256]{1,0:T(8,128)(2,1)S(1)} %get-tuple-element.26.mixed_grad.own), channel_id=1, source_target_pairs={{2,0},{4,2},{6,4},{8,6},{10,8},{12,10},{14,12},{3,1},{5,3},{7,5},{... | collective-permute-start | bytes 786440 | tf_op jit(solution)/shard_map/ppermute | solution.py:169
  60.3 15.4 %collective-permute-start.5 = (f32[152,128]{1,0:T(8,128)S(1)}, f32[152,128]{1,0:T(8,128)S(1)}, u32[]{:S(2)}, u32[]{:S(2)}) collective-permute-start(f32[152,128]{1,0:T(8,128)S(1)} %pad_maximum_fusion.2), channel_id=1, source_target_pairs={{0,1},{1,0},{2,3},{3,2},{4,5},{5,4},{6,7},{7,6},{8,9},{9,8},{10,11... | collective-permute-start | bytes 233480 | tf_op jit(solution)/shard_map/ppermute | solution.py:173

commit v2 on v1

v2 whole, which is shorter than its diff:
```python
import functools
import math

import jax
import jax.numpy as jnp
from jax import lax
from jax.experimental import pallas as pl
from jax.experimental.pallas import tpu as pltpu
from jax.sharding import PartitionSpec as P

F32 = jnp.float32
BF16 = jnp.bfloat16
LANES = 128
EXTRA = 48
CENTRE = 4
NN = (((1,), (0,)), ((), ()))
NT = (((1,), (1,)), ((), ()))
TN = (((0,), (0,)), ((), ()))
FAR = -1e6
NEAR = 50 * 10**9
OWN = 8 * 10**9


def mul(a, b, dims=NN):
    return lax.dot_general(a, b, dims, preferred_element_type=F32)


def halves(values):
    high = values.astype(BF16)
    return high, (values - high.astype(F32)).astype(BF16)


def row_mean(values):
    return jnp.mean(values, axis=-1, keepdims=True)


def soft_abs(values):
    return jnp.sqrt(values * values + 0.04)


def turned(values):
    return values.astype(F32).T.astype(BF16)


def relative_places(info, neighbours):
    table = neighbours[...]
    relative = jnp.where(table >= 0, (table - info[0]).astype(F32), FAR)
    fill = jnp.full((16 - table.shape[0], table.shape[1]), FAR, F32)
    return jnp.concatenate([relative, fill], axis=0).T


def pair_places(info, neighbours):
    pixels = neighbours.shape[1]
    return relative_places(info, neighbours) + jnp.where(info[1] == 0, -pixels, pixels).astype(F32)


def side_places(info, neighbours):
    pixels = neighbours.shape[1]
    return relative_places(info, neighbours) + jnp.where(info[1] == 0, pixels, -pixels).astype(F32)


def tap_rows(places, source, tap):
    column = lax.broadcasted_iota(jnp.int32, (places.shape[0], source.shape[0]), 1).astype(F32)
    chosen = jnp.where(column == places[:, tap : tap + 1], 1.0, 0.0).astype(BF16)
    return mul(chosen, source)


def load(pairs, sems):
    copies = [pltpu.make_async_copy(src, dst, sems.at[k]) for k, (src, dst) in enumerate(pairs)]
    for copy in copies:
        copy.start()
    for copy in copies:
        copy.wait()


def spread_kernel(rows, out):
    for owner in range(out.shape[0]):
        out[owner] = rows[...]


def mix_own_kernel(
    info, own_hbm, neighbours_hbm, weights_hbm, head_hbm, scale_hbm, gain_hbm, bias_hbm, target_hbm,
    own, weights, head, scale, gain, bias, target,
    neighbours, taken, mixed_out, base_out, sems,
):
    load(
        [(own_hbm, own), (neighbours_hbm, neighbours), (weights_hbm, weights), (head_hbm, head),
         (scale_hbm, scale), (gain_hbm, gain), (bias_hbm, bias), (target_hbm, target)],
        sems,
    )
    source = own[...]
    places = relative_places(info, neighbours)
    base_out[...] = mul(head[...], source, NT)
    mixed = weights[CENTRE : CENTRE + 1, :] * source.astype(F32)
    for tap in range(weights.shape[0]):
        if tap != CENTRE:
            rows = tap_rows(places, source, tap)
            taken[tap - (tap > CENTRE)] = rows.astype(BF16)
            mixed = mixed + weights[tap : tap + 1, :] * rows
    mixed_out[...] = mixed


def mix(where, tile, weights, mixed_in, taken, mixed_out):
    source = tile[...]
    mixed = mixed_in[...]
    for tap in range(weights.shape[0]):
        if tap != CENTRE:
            rows = tap_rows(where, source, tap)
            taken[tap - (tap > CENTRE)] = rows.astype(BF16)
            mixed = mixed + weights[tap : tap + 1, :] * rows
    mixed_out[...] = mixed


def mix_pair_kernel(info, tile, neighbours, weights, mixed_in, taken, mixed_out):
    mix(pair_places(info, neighbours), tile, weights, mixed_in, taken, mixed_out)


def mix_side_kernel(
    info, tile, neighbours, weights, gain, mixed_in, taken, mixed_out, normed_out
):
    mix(side_places(info, neighbours), tile, weights, mixed_in, taken, mixed_out)
    mixed = mixed_out[...]
    centred = mixed - row_mean(mixed)
    inverse = lax.rsqrt(row_mean(centred * centred) + 1e-06)
    normed_out[...] = (centred * inverse * gain[...]).astype(BF16)


def forward_kernel(
    info, normed, mine, other, bias, base, head, scale,
    act_out, slope_out, forecast_out, up, down, reach,
):
    owners = mine.shape[0]
    half = mine.shape[1] // 2
    for owner in range(owners):
        for side in range(2):
            rows = slice((2 * owner + side) * half, (2 * owner + side + 1) * half)
            up[rows, :] = jnp.where(info[2] == side, mine[owner, :half], other[owner, :half])
            down[rows, :] = jnp.where(info[2] == side, mine[owner, half:], other[owner, half:])
    high, low = halves(head[...].astype(F32) * scale[...])
    product = mul(jnp.concatenate([high, low], axis=0), down[...], NT)
    high, low = halves(product[:8] + product[8:])
    reach[...] = jnp.concatenate([high, low], axis=0)
    forward(normed, up, reach, bias, base, act_out, slope_out, forecast_out)


def forward(normed, up, reach, bias, base, act_out, slope_out, forecast_out):
    rows = normed[...]
    total = base[...]
    for low_edge in range(0, up.shape[0], 256):
        piece = slice(low_edge, low_edge + 256)
        pre = mul(rows, up[piece, :], NT) + bias[:, piece]
        phi = 0.5 + 0.5 * lax.erf(pre * 0.7071067811865476)
        act = (pre * phi).astype(BF16)
        act_out[:, piece] = act
        slope_out[:, piece] = phi + pre * jnp.exp(-0.5 * pre * pre) * 0.3989422804014327
        part = mul(reach[:, piece], act, NT)
        total = total + part[:8] + part[8:]
    forecast_out[...] = total


def backward_kernel(
    mine, other, target, reach, slope, up, mixed, gain, mixed_grad, pre_out, grad_out, loss_out
):
    apart = mine[...] - target[...]
    spread = mine[...] - other[...]
    apart_abs, spread_abs = soft_abs(apart), soft_abs(spread)
    grad = (0.5 * (apart / apart_abs) - 0.5 * (spread / spread_abs)).astype(BF16)
    grad_out[...] = grad
    loss_out[...] = jnp.full(loss_out.shape, jnp.sum(0.5 * apart_abs - 0.25 * spread_abs), F32)
    twice = turned(jnp.concatenate([grad, grad], axis=0))
    normed_grad = jnp.zeros(mixed.shape, F32)
    for low_edge in range(0, up.shape[0], 256):
        piece = slice(low_edge, low_edge + 256)
        pre = (mul(twice, reach[:, piece]) * slope[:, piece]).astype(BF16)
        pre_out[:, piece] = pre
        normed_grad = normed_grad + mul(pre, up[piece, :])
    values = mixed[...]
    centred = values - row_mean(values)
    inverse = lax.rsqrt(row_mean(centred * centred) + 1e-06)
    z = centred * inverse
    gained = normed_grad * gain[...]
    mixed_grad[...] = (
        inverse * (gained - row_mean(gained) - z * row_mean(gained * z))
    ).astype(BF16)


def weights_kernel(
    info, pre_grad, normed, act, grad, features, down, scale, a, b, c, mixed_grad, loss,
    keep, send, small,
):
    normed_t = turned(normed[...])
    summed = mul(grad[...], act[...])
    high, low = halves(summed)
    through = mul(jnp.concatenate([high, low], axis=0), down[...])
    head_part = mul(grad[...], features[...]) + scale[...] * (through[:8] + through[8:])
    flow = mixed_grad[...].astype(F32)
    depth = [
        jnp.sum((a[k] + b[k] + c[k]).astype(F32) * flow, axis=0, keepdims=True)
        for k in range(a.shape[0])
    ]
    depth.insert(CENTRE, jnp.sum(features[...].astype(F32) * flow, axis=0, keepdims=True))
    small[...] = jnp.concatenate([head_part] + depth + [loss[...]], axis=0)
    first = info[2] == 0
    for block in range(keep.shape[0]):
        lanes = slice(block * LANES, (block + 1) * LANES)
        up_part = mul(normed_t, pre_grad[:, lanes])
        lower, higher = up_part[:LANES], up_part[LANES:]
        keep[block, :LANES, :] = jnp.where(first, lower, higher).astype(BF16)
        send[block, :, :] = jnp.where(first, higher, lower).astype(BF16)
        extra = [small[:, :LANES], small[:, LANES:], summed[:, lanes], jnp.zeros((4, LANES), F32)]
        keep[block, LANES:, :] = jnp.concatenate(extra, axis=0).astype(BF16)


def join_kernel(keep, came, joined):
    for block in range(keep.shape[0]):
        main = keep[block, :LANES, :].astype(F32) + came[block].astype(F32)
        joined[block, :LANES, :] = main.astype(BF16)
        joined[block, LANES:, :] = keep[block, LANES:, :]


def sum_kernel(parts, total):
    value = parts[0].astype(F32)
    for part in range(1, parts.shape[0]):
        value = value + parts[part].astype(F32)
    total[...] = value


def final_kernel(factors, info, ours, theirs, head, scale, mean, up, down, depth, head_out):
    loss_factor, factor = factors
    mine, other = ours[:LANES, :], theirs[:LANES, :]
    up[:, :LANES] = jnp.where(info[2] == 0, mine, other).T * factor
    up[:, LANES:] = jnp.where(info[2] == 0, other, mine).T * factor
    extra = ours[LANES:, :] + theirs[LANES:, :]
    small = jnp.concatenate([extra[:18], extra[18:36]], axis=1)
    head_out[...] = small[:8] * factor
    depth[...] = small[8:17] * factor
    mean[0] = jnp.sum(small[17:18, :1]) * loss_factor
    high, low = halves(extra[36:44])
    turn = jnp.concatenate([high, low], axis=0).astype(F32).T.astype(BF16)
    down[...] = mul(turn, jnp.concatenate([head[...], head[...]], axis=0)) * (scale[...] * factor)


def back_taps(total, source, places, weights):
    last = weights.shape[0] - 1
    for tap in range(last + 1):
        if tap != CENTRE:
            total = total + weights[last - tap : last - tap + 1, :] * tap_rows(places, source, tap)
    return total


def input_own_kernel(info, own, neighbours, weights, grad, head, out):
    source = own[...]
    centre = weights.shape[0] - 1 - CENTRE
    total = mul(turned(grad[...]), head[...])
    total = total + weights[centre : centre + 1, :] * source.astype(F32)
    out[...] = back_taps(total, source, relative_places(info, neighbours), weights)


def input_pair_kernel(info, tile, neighbours, weights, partial, out):
    out[...] = back_taps(partial[...], tile[...], pair_places(info, neighbours), weights)


def input_side_kernel(info, tile, neighbours, weights, partial, out):
    total = back_taps(partial[...], tile[...], side_places(info, neighbours), weights)
    out[...] = total.astype(BF16)


def call(
    kernel, outs, scalars, *operands, hbm=0, scratch=(), aliases=None, flops=2000000000, mib=8, smem_outs=(), last=False
):
    smem = pl.BlockSpec(memory_space=pltpu.SMEM)
    out_spec = pl.BlockSpec() if last else pl.BlockSpec(memory_space=pltpu.VMEM)
    kinds = [smem] * scalars + [pl.BlockSpec(memory_space=pltpu.HBM)] * hbm
    kinds = kinds + [pl.BlockSpec()] * (len(operands) - len(kinds))
    return pl.pallas_call(
        kernel,
        out_shape=tuple(jax.ShapeDtypeStruct(shape, dtype) for shape, dtype in outs),
        in_specs=kinds,
        out_specs=tuple(smem if k in smem_outs else out_spec for k in range(len(outs))),
        scratch_shapes=list(scratch),
        input_output_aliases=aliases or {},
        compiler_params=pltpu.CompilerParams(vmem_limit_bytes=mib * 2**20),
        cost_estimate=pl.CostEstimate(flops=flops, bytes_accessed=0, transcendentals=0),
    )(*operands)


def pair_tiles(array):
    count = lax.axis_size("pix")
    inner = [(i, i ^ 1) for i in range(count)]
    outer = [(i, i + 1) for i in range(1, count - 1, 2)]
    outer = outer + [(j, i) for i, j in outer]
    return lax.ppermute(array, "pix", inner), lax.ppermute(array, "pix", outer)


def swap(array):
    return lax.ppermute(array, "mem", [(0, 1), (1, 0)])


def local(
    features,
    neighbours,
    analysis_fields,
    depth_weight,
    norm_gain,
    up_weight,
    up_bias,
    down_weight,
    layer_scale,
    head_matrix,
):
    pixels, channels = features.shape[1:]
    count = lax.axis_size("pix")
    owned_rows = up_weight.shape[0]
    hidden = owned_rows * count
    taps = neighbours.shape[0]
    position, member = lax.axis_index("pix"), lax.axis_index("mem")
    info = jnp.stack([position * pixels, position % 2, member]).astype(jnp.int32)
    own = features[0]
    gain, scale, bias = norm_gain[None], layer_scale[None], up_bias[None]
    by_blocks = owned_rows == LANES
    exact = lax.Precision.HIGHEST
    tile, many = (pixels, channels), (taps - 1, pixels, channels)

    def everywhere(array):
        return lax.all_to_all(array, "pix", split_axis=0, concat_axis=0)

    pair, side = pair_tiles(own)
    if by_blocks:
        half = owned_rows // 2
        rows = jnp.stack([up_weight, down_weight])
        rows = lax.dynamic_slice_in_dim(rows, member * half, half, 1)
        (rows,) = call(
            spread_kernel,
            [((count, owned_rows, channels), BF16)],
            0,
            rows.reshape(owned_rows, channels),
            flops=OWN,
        )
        mine = everywhere(rows)
    else:
        up = lax.all_gather(up_weight, "pix", axis=0, tiled=True)
        down = lax.all_gather(down_weight, "pix", axis=0, tiled=True)
        reach = lax.dot_general(
            head_matrix.astype(F32) * layer_scale, down.astype(F32), NT, precision=exact
        )
        reach = jnp.concatenate(halves(reach), axis=0)
    own, weights, head, scale, gain, bias, target, places, taken, mixed, base = call(
        mix_own_kernel,
        [(tile, BF16), (depth_weight.shape, F32), (head_matrix.shape, BF16),
         ((1, channels), F32), ((1, channels), F32), ((1, hidden), F32), ((8, pixels), F32),
         (neighbours.shape, jnp.int32), (many, BF16), (tile, F32), ((8, pixels), F32)],
        1,
        info, own, neighbours, depth_weight, head_matrix, scale, gain, bias, analysis_fields,
        hbm=8,
        scratch=[pltpu.SemaphoreType.DMA((8,))],
        flops=OWN,
    )
    taken_pair, mixed = call(
        mix_pair_kernel,
        [(many, BF16), (tile, F32)],
        1,
        info, pair, places, weights, mixed,
        flops=NEAR,
    )
    taken_side, mixed, normed = call(
        mix_side_kernel,
        [(many, BF16), (tile, F32), (tile, BF16)],
        1,
        info, side, places, weights, gain, mixed,
        flops=NEAR,
    )
    outs = [((pixels, hidden), BF16), ((pixels, hidden), F32), ((8, pixels), F32)]
    if by_blocks:
        mine, normed = lax.optimization_barrier((mine, normed))
        other = swap(mine)
        whole = ((hidden, channels), BF16)
        act, slope, forecast, up, down, reach = call(
            forward_kernel,
            outs + [whole, whole, ((16, hidden), BF16)],
            1,
            info, normed, mine, other, bias, base, head, scale,
        )
    else:
        act, slope, forecast = call(forward, outs, 0, normed, up, reach, bias, base)
    mixed_grad, pre_grad, grad, loss = call(
        backward_kernel,
        [(tile, BF16), ((pixels, hidden), BF16), ((8, pixels), BF16), ((1, channels), F32)],
        0,
        forecast, swap(forecast), target, reach, slope, up, mixed, gain,
    )
    blocks = hidden // LANES
    full = ((blocks, LANES + EXTRA, LANES), BF16)
    keep, send, small = call(
        weights_kernel,
        [full, ((blocks, LANES, LANES), BF16), ((18, channels), F32)],
        1,
        info, pre_grad, normed, act, grad, own, down, scale, taken, taken_pair, taken_side,
        mixed_grad, loss,
        flops=NEAR,
    )
    came = swap(send)
    grad_pair, grad_side = pair_tiles(mixed_grad)
    (joined,) = call(join_kernel, [full], 0, keep, came)
    source, joined = lax.optimization_barrier((mixed_grad, joined))
    (partial,) = call(
        input_own_kernel, [(tile, F32)], 1, info, source, places, weights, grad, head, flops=OWN
    )
    (partial,) = call(
        input_pair_kernel,
        [(tile, F32)],
        1,
        info, grad_pair, places, weights, partial,
        flops=NEAR,
    )
    (input_grad,) = call(
        input_side_kernel,
        [(tile, BF16)],
        1,
        info, grad_side, places, weights, partial,
        flops=NEAR,
        last=True,
    )
    grad_scale = 1.0 / math.sqrt(pixels * count * 2)
    loss_scale = 1.0 / (pixels * count * 8)
    if by_blocks:
        parts, input_grad = lax.optimization_barrier((everywhere(joined), input_grad))
        (total,) = call(sum_kernel, [((LANES + EXTRA, LANES), F32)], 0, parts)
        mean_crps, up_grad, down_grad, depth_grad, head_grad = call(
            functools.partial(final_kernel, (loss_scale, grad_scale)),
            [((1,), F32), ((LANES, channels), F32), ((LANES, channels), F32),
             ((taps, channels), F32), ((8, channels), F32)],
            1,
            info, total, swap(total), head, scale,
            smem_outs=(0,),
            last=True,
        )
        return mean_crps, input_grad[None], up_grad, down_grad, depth_grad, head_grad

    main = joined[:, :LANES].astype(F32)
    main = jnp.stack([main, swap(main)])
    main = jnp.where(member == 0, main, main[::-1])
    rows = jnp.transpose(main, (1, 3, 0, 2)).reshape(hidden, channels)
    up_grad = lax.psum_scatter(rows, "pix", scatter_dimension=0, tiled=True)
    summed = keep[:, LANES + 36 : LANES + 44].astype(F32)
    summed = jnp.transpose(summed + swap(summed), (0, 2, 1)).reshape(hidden, 8)
    summed = lax.psum_scatter(summed, "pix", scatter_dimension=0, tiled=True)
    down_grad = layer_scale * jnp.dot(summed, head_matrix.astype(F32), precision=exact)
    small = lax.psum(small, ("pix", "mem"))
    return (
        small[17, :1] * loss_scale,
        input_grad[None],
        up_grad * grad_scale,
        down_grad * grad_scale,
        small[8:17] * grad_scale,
        small[:8] * grad_scale,
    )


def solution(mesh):
    return jax.shard_map(
        local,
        mesh=mesh,
        in_specs=(
            P("mem", ("groups", "pix"), None),
            P(None, "pix"),
            P(None, ("groups", "pix")),
            P(),
            P(),
            P("pix", None),
            P(),
            P("pix", None),
            P(),
            P(),
        ),
        out_specs=(
            P("groups"),
            P("mem", ("groups", "pix"), None),
            P(("groups", "pix"), None),
            P(("groups", "pix"), None),
            P("groups", None),
            P("groups", None),
        ),
        check_vma=False,
    )
```

time: 81.6 us -> 62.3 us (0.76)
  the two profiles are of different devices: /device:TPU:16 before, /device:TPU:0 now
where the time goes in v2:
time: 62.3 us; the launch traced here: 61.2 us
  Pallas kernels  22.2 us (36%)
  starting transfers between devices  20.3 us (33%)
  waiting for transfers between devices  11 us (18%)
  local copies, waits for them, and re-layouts  5.9 us (9%)
  between operations  1.02 us (2%)
  other arithmetic  0.86 us (1%)
    pallas_call x13, Pallas kernels, call(): pl.pallas_call(kernel, out_shape=tuple((jax.ShapeDtypeStruct(shape, dtype...  22.2 us
    all_to_all x2, starting transfers between devices, everywhere(): return lax.all_to_all(array, 'pix', split_axis=0, concat_axis=0)  14.1 us
    unnamed x28, local copies, waits for them, and re-layouts  5.9 us
    ppermute x2, starting transfers between devices, pair_tiles(): lax.ppermute(array, 'pix', inner)  4.42 us
    ppermute x4, waiting for transfers between devices, swap(): return lax.ppermute(array, 'mem', [(0, 1), (1, 0)])  4.23 us
    ppermute x2, waiting for transfers between devices, pair_tiles(): lax.ppermute(array, 'pix', inner)  4.08 us
    all_to_all x2, waiting for transfers between devices, everywhere(): return lax.all_to_all(array, 'pix', split_axis=0, concat_axis=0)  2.69 us
    ppermute x2, starting transfers between devices, pair_tiles(): lax.ppermute(array, 'pix', outer)  1.33 us
  transfers between devices with their start and end apart: 10, of which 5 were waited for; matrix products, arithmetic and copies ran while one was open for 1% of the time, Pallas kernels for 26%

profile of v2, /device:TPU:0, one launch (start us, length us, event | category | flops | bytes accessed | tf_op | source)
XLA Modules:
  0.0 61.2 jit_solution(7724156234284184643)
XLA Ops:
  0.6 3.0 %collective-permute-start.1 = (bf16[512,256]{1,0:T(8,128)(2,1)}, bf16[512,256]{1,0:T(8,128)(2,1)S(1)}, u32[]{:S(2)}, u32[]{:S(2)}) collective-permute-start(bf16[512,256]{1,0:T(8,128)(2,1)} %bitcast.12), channel_id=1, source_target_pairs={{0,2},{2,0},{4,6},{6,4},{8,10},{10,8},{12,14},{14,12},{1,3},{3,1},... | collective-permute-start | bytes 786440 | tf_op jit(solution)/shard_map/ppermute | solution.py:292
  3.6 0.7 %collective-permute-start = (bf16[512,256]{1,0:T(8,128)(2,1)}, bf16[512,256]{1,0:T(8,128)(2,1)S(1)}, u32[]{:S(2)}, u32[]{:S(2)}) collective-permute-start(bf16[512,256]{1,0:T(8,128)(2,1)} %bitcast.13), channel_id=1, source_target_pairs={{2,4},{6,8},{10,12},{4,2},{8,6},{12,10},{3,5},{7,9},{11,13},{5,3},... | collective-permute-start | bytes 786440 | tf_op jit(solution)/shard_map/ppermute | solution.py:292
  4.3 0.8 %fusion = bf16[2,64,256]{2,1,0:T(8,128)(2,1)S(1)} fusion(s32[]{:T(128)S(6)} %select_n.11, bf16[1,128,256]{2,1,0:T(8,128)(2,1)} %bitcast.18, bf16[1,128,256]{2,1,0:T(8,128)(2,1)} %bitcast.19), kind=kLoop, calls=%fused_computation.2 | loop fusion | flops 131072 | bytes 196612 | tf_op jit(solution)/shard_map/stack | solution.py:330
  5.1 0.0 copy-start
  5.1 0.0 copy-start.1
  5.1 0.0 copy-start.2
  5.1 0.0 copy-start.3
  5.1 0.0 copy-start.4
  5.1 0.0 copy-start.5
  5.2 0.0 copy-start.6
  5.2 0.0 copy-start.7
  5.2 0.9 %shard_map.145 = bf16[8,128,256]{2,1,0:T(8,128)(2,1)} custom-call(bf16[128,256]{1,0:T(8,128)(2,1)S(1)} %bitcast.11), custom_call_target="tpu_custom_call" | custom-call | flops 8000000000 | tf_op jit(solution)/shard_map/pallas_call | solution.py:275
  6.0 7.6 %all-to-all-start = ((bf16[8,128,256]{2,1,0:T(8,128)(2,1)}), bf16[8,128,256]{2,1,0:T(8,128)(2,1)S(1)}, u32[]{:S(2)}, u32[]{:S(2)}) async-start(bf16[8,128,256]{2,1,0:T(8,128)(2,1)} %shard_map.145), calls=%async_computation | async-start | bytes 1048576 | tf_op jit(solution)/shard_map/all_to_all | solution.py:325
  13.6 0.1 pad_add_fusion.info
  13.7 0.0 copy-done
  13.7 0.0 copy-done.1
  13.7 0.0 copy-done.2
  13.7 0.0 copy-done.3
  13.7 0.0 copy-done.4
  13.7 0.0 copy-done.5
  13.7 0.0 copy-done.6
  13.7 0.0 copy-done.7
  13.7 2.5 %shard_map.146 = (bf16[512,256]{1,0:T(8,128)(2,1)S(1)}, f32[9,256]{1,0:T(8,128)S(1)}, bf16[8,256]{1,0:T(8,128)(2,1)S(1)}, f32[1,256]{1,0:T(1,128)S(1)}, f32[1,25...) custom-call(s32[3]{0:T(128)S(1)} %pad_add_fusion.info, ...), custom_call_target="tpu_custom_call" | custom-call | flops 8000000000 | tf_op jit(solution)/shard_map/pallas_call | solution.py:275
  16.3 0.0 copy-start.8
  16.3 1.4 %copy-done.8 = bf16[8,512,256]{2,1,0:T(8,128)(2,1)} copy-done((bf16[8,512,256]{2,1,0:T(8,128)(2,1)}, bf16[8,512,256]{2,1,0:T(8,128)(2,1)S(1)}, u32[]{:S(2)}) %copy-start.8) | copy-done | bytes 2097176
  17.6 0.0 collective-permute-done.1.tile
  17.6 2.2 %shard_map.147 = (bf16[8,512,256]{2,1,0:T(8,128)(2,1)S(1)}, f32[512,256]{1,0:T(8,128)S(1)}) custom-call(s32[3]{0:T(128)S(1)} %pad_add_fusion.info, bf16[512,256]{1,0:T(8,128)(2,1)S(1)} %collective-permute-done.1.tile, s32[9,512]{1,0:T(8,128)S(1)} %get-tuple-element.45.neighbours, f32[9,256]{1,0:T(8,128)S(1)} %get-tuple-element.46.weights, ...), custom_call_target="tpu_custom_call" | custom-call | flops 49999998976 | tf_op jit(solution)/shard_map/pallas_call | solution.py:275
  19.8 0.0 copy-start.10
  19.8 1.3 %copy-done.10 = bf16[8,512,256]{2,1,0:T(8,128)(2,1)} copy-done((bf16[8,512,256]{2,1,0:T(8,128)(2,1)}, bf16[8,512,256]{2,1,0:T(8,128)(2,1)S(1)}, u32[]{:S(2)}) %copy-start.10) | copy-done | bytes 2097176
  21.1 0.0 collective-permute-done.tile
  21.1 2.4 %shard_map.148 = (bf16[8,512,256]{2,1,0:T(8,128)(2,1)S(1)}, f32[512,256]{1,0:T(8,128)S(1)}, bf16[512,256]{1,0:T(8,128)(2,1)S(1)}) custom-call(s32[3]{0:T(128)S(1)} %pad_add_fusion.info, bf16[512,256]{1,0:T(8,128)(2,1)S(1)} %collective-permute-done.tile, s32[9,512]{1,0:T(8,128)S(1)} %get-tuple-element.45.neighbours, f32[9,256]{1,0:T(8,128)S(1)} %get-tuple-element.46.weights, ...), custom_call_target="tpu_custom_call" | custom-call | flops 49999998976 | tf_op jit(solution)/shard_map/pallas_call | solution.py:275
  23.5 0.0 copy-start.12
  23.5 1.4 %copy-done.12 = bf16[8,512,256]{2,1,0:T(8,128)(2,1)} copy-done((bf16[8,512,256]{2,1,0:T(8,128)(2,1)}, bf16[8,512,256]{2,1,0:T(8,128)(2,1)S(1)}, u32[]{:S(2)}) %copy-start.12) | copy-done | bytes 2097176
  24.9 2.7 %all-to-all-done.mine = bf16[8,128,256]{2,1,0:T(8,128)(2,1)S(1)} async-done(((bf16[8,128,256]{2,1,0:T(8,128)(2,1)}), bf16[8,128,256]{2,1,0:T(8,128)(2,1)S(1)}, u32[]{:S(2)}, u32[]{:S(2)}) %all-to-all-start) | async-done | bytes 524320 | tf_op jit(solution)/shard_map/all_to_all | solution.py:325
  27.6 0.0 collective-permute-start.2
  27.6 1.9 %collective-permute-done.2.other = bf16[8,128,256]{2,1,0:T(8,128)(2,1)S(1)} collective-permute-done((bf16[8,128,256]{2,1,0:T(8,128)(2,1)S(1)}, bf16[8,128,256]{2,1,0:T(8,128)(2,1)S(1)}, u32[]{:S(2)}, u32[]{:S(2)}) %collective-permute-start.2) | collective-permute-done | bytes 524320 | tf_op jit(solution)/shard_map/ppermute | solution.py:296
  29.5 2.0 %shard_map.149 = (bf16[512,1024]{1,0:T(8,128)(2,1)S(1)}, f32[512,1024]{1,0:T(8,128)S(1)}, f32[8,512]{1,0:T(8,128)S(1)}, bf16[1024,256]{1,0:T(8,128)(2,1)S(1)}, b...) custom-call(s32[3]{0:T(128)S(1)} %pad_add_fusion.info, bf16[512,256]{1,0:T(8,128)(2,1)S(1)} %get-tuple-element.51.normed, ...), custom_call_target="tpu_custom_call" | custom-call | flops 2000000000 | tf_op jit(solution)/shard_map/pallas_call | solution.py:275
  31.5 0.1 collective-permute-start.3
  31.6 1.0 %collective-permute-done.3.other = f32[8,512]{1,0:T(8,128)S(1)} collective-permute-done((f32[8,512]{1,0:T(8,128)S(1)}, f32[8,512]{1,0:T(8,128)S(1)}, u32[]{:S(2)}, u32[]{:S(2)}) %collective-permute-start.3) | collective-permute-done | bytes 16416 | tf_op jit(solution)/shard_map/ppermute | solution.py:296
  32.7 0.0 copy-start.9
  32.7 0.0 copy-start.11
  32.7 0.0 copy-start.13
  32.7 1.0 %shard_map.150 = (bf16[512,256]{1,0:T(8,128)(2,1)S(1)}, bf16[512,1024]{1,0:T(8,128)(2,1)S(1)}, bf16[8,512]{1,0:T(8,128)(2,1)S(1)}, f32[1,256]{1,0:T(1,128)S(1)}) custom-call(f32[8,512]{1,0:T(8,128)S(1)} %get-tuple-element.57.mine, f32[8,512]{1,0:T(8,128)S(1)} %collective-permute-done.3.other, f32[8,512]{1,0:T(8,128)S(1)} %get-tuple-element.58.target, ...), custom_call_target="tpu_custom_call" | custom-call | flops 2000000000 | tf_op jit(solution)/shard_map/pallas_call | solution.py:275
  33.7 0.6 copy-done.9
  34.3 0.6 %copy-done.11 = bf16[8,512,256]{2,1,0:T(8,128)(2,1)S(1)} copy-done((bf16[8,512,256]{2,1,0:T(8,128)(2,1)S(1)}, bf16[8,512,256]{2,1,0:T(8,128)(2,1)}, u32[]{:S(2)}) %copy-start.11) | copy-done | bytes 2097176
  34.9 0.6 %copy-done.13 = bf16[8,512,256]{2,1,0:T(8,128)(2,1)S(1)} copy-done((bf16[8,512,256]{2,1,0:T(8,128)(2,1)S(1)}, bf16[8,512,256]{2,1,0:T(8,128)(2,1)}, u32[]{:S(2)}) %copy-start.13) | copy-done | bytes 2097176
  35.5 1.9 %shard_map.151 = (bf16[8,176,128]{2,1,0:T(8,128)(2,1)S(1)}, bf16[8,128,128]{2,1,0:T(8,128)(2,1)S(1)}, f32[18,256]{1,0:T(8,128)}) custom-call(s32[3]{0:T(128)S(1)} %pad_add_fusion.info, bf16[512,1024]{1,0:T(8,128)(2,1)S(1)} %get-tuple-element.64.pre_grad, bf16[512,256]{1,0:T(8,128)(2,1)S(1)} %get-tuple-element.51.normed, ...), custom_call_target="tpu_custom_call" | custom-call | flops 49999998976 | tf_op jit(solution)/shard_map/pallas_call | solution.py:275
  37.5 0.2 collective-permute-start.4
  37.6 1.4 %collective-permute-start.6 = (bf16[512,256]{1,0:T(8,128)(2,1)S(1)}, bf16[512,256]{1,0:T(8,128)(2,1)S(1)}, u32[]{:S(2)}, u32[]{:S(2)}) collective-permute-start(bf16[512,256]{1,0:T(8,128)(2,1)S(1)} %get-tuple-element.76.mixed_grad.own), channel_id=1, source_target_pairs={{0,2},{2,0},{4,6},{6,4},{8,10},{10,8},{12,14},{14,12},{1,3},{3,1},... | collective-permute-start | bytes 786440 | tf_op jit(solution)/shard_map/ppermute | solution.py:292
  39.1 0.7 %collective-permute-start.5 = (bf16[512,256]{1,0:T(8,128)(2,1)S(1)}, bf16[512,256]{1,0:T(8,128)(2,1)S(1)}, u32[]{:S(2)}, u32[]{:S(2)}) collective-permute-start(bf16[512,256]{1,0:T(8,128)(2,1)S(1)} %get-tuple-element.76.mixed_grad.own), channel_id=1, source_target_pairs={{2,4},{6,8},{10,12},{4,2},{8,6},{12,10},{3,5},{7,9},{11,13},{5,3},... | collective-permute-start | bytes 786440 | tf_op jit(solution)/shard_map/ppermute | solution.py:292
  39.7 0.0 collective-permute-done.4.came
  39.8 0.8 %shard_map.152 = bf16[8,176,128]{2,1,0:T(8,128)(2,1)} custom-call(bf16[8,176,128]{2,1,0:T(8,128)(2,1)S(1)} %get-tuple-element.73.keep, bf16[8,128,128]{2,1,0:T(8,128)(2,1)S(1)} %collective-permute-done.4.came), custom_call_target="tpu_custom_call" | custom-call | flops 2000000000 | tf_op jit(solution)/shard_map/pallas_call | solution.py:275
  40.6 6.6 %all-to-all-start.1 = ((bf16[8,176,128]{2,1,0:T(8,128)(2,1)}), bf16[8,176,128]{2,1,0:T(8,128)(2,1)S(1)}, u32[]{:S(2)}, u32[]{:S(2)}) async-start(bf16[8,176,128]{2,1,0:T(8,128)(2,1)} %shard_map.152), calls=%async_computation.1 | async-start | bytes 720896 | tf_op jit(solution)/shard_map/all_to_all | solution.py:325
  47.1 2.1 %shard_map.153.partial = f32[512,256]{1,0:T(8,128)S(1)} custom-call(s32[3]{0:T(128)S(1)} %pad_add_fusion.info, bf16[512,256]{1,0:T(8,128)(2,1)S(1)} %get-tuple-element.76.mixed_grad.own, s32[9,512]{1,0:T(8,128)S(1)} %get-tuple-element.45.neighbours, f32[9,256]{1,0:T(8,128)S(1)} %get-tuple-element.46.weights, bf16[8,512]{1,0:T(8,128)(2,1)S(1)} %get-tuple-element.66.grad, ...), custom_call_target="tpu_custom_call" | custom-call | flops 8000000000 | tf_op jit(solution)/shard_map/pallas_call | solution.py:275
  49.2 4.1 %collective-permute-done.6.tile = bf16[512,256]{1,0:T(8,128)(2,1)S(1)} collective-permute-done((bf16[512,256]{1,0:T(8,128)(2,1)S(1)}, bf16[512,256]{1,0:T(8,128)(2,1)S(1)}, u32[]{:S(2)}, u32[]{:S(2)}) %collective-permute-start.6) | collective-permute-done | bytes 262176 | tf_op jit(solution)/shard_map/ppermute | solution.py:292
  53.3 2.1 %shard_map.154.partial = f32[512,256]{1,0:T(8,128)S(1)} custom-call(s32[3]{0:T(128)S(1)} %pad_add_fusion.info, bf16[512,256]{1,0:T(8,128)(2,1)S(1)} %collective-permute-done.6.tile, s32[9,512]{1,0:T(8,128)S(1)} %get-tuple-element.45.neighbours, f32[9,256]{1,0:T(8,128)S(1)} %get-tuple-element.46.weights, f32[512,256]{1,0:T(8,128)S(1)} %shard_map.153.partial), custom_call_target="tpu_custom_call" | custom-call | flops 49999998976 | tf_op jit(solution)/shard_map/pallas_call | solution.py:275
  55.4 0.0 collective-permute-done.5.tile
  55.4 2.8 %shard_map.155 = bf16[512,256]{1,0:T(8,128)(2,1)} custom-call(s32[3]{0:T(128)S(1)} %pad_add_fusion.info, bf16[512,256]{1,0:T(8,128)(2,1)S(1)} %collective-permute-done.5.tile, s32[9,512]{1,0:T(8,128)S(1)} %get-tuple-element.45.neighbours, f32[9,256]{1,0:T(8,128)S(1)} %get-tuple-element.46.weights, f32[512,256]{1,0:T(8,128)S(1)} %shard_map.154.partial), custom_call_target="tpu_custom_call" | custom-call | flops 49999998976 | tf_op jit(solution)/shard_map/pallas_call | solution.py:275
  58.2 0.0 all-to-all-done.1.parts
  58.3 0.1 collective-permute-start.7
  58.4 1.3 %collective-permute-done.7.theirs = f32[176,128]{1,0:T(8,128)S(1)} collective-permute-done((f32[176,128]{1,0:T(8,128)S(1)}, f32[176,128]{1,0:T(8,128)S(1)}, u32[]{:S(2)}, u32[]{:S(2)}) %collective-permute-start.7) | collective-permute-done | bytes 90144 | tf_op jit(solution)/shard_map/ppermute | solution.py:296
  59.6 1.4 %shard_map.157 = (f32[1]{0:T(128)}, f32[128,256]{1,0:T(8,128)}, f32[128,256]{1,0:T(8,128)}, f32[9,256]{1,0:T(8,128)}, f32[8,256]{1,0:T(8,128)}) custom-call(s32[3]{0:T(128)S(1)} %pad_add_fusion.info, f32[176,128]{1,0:T(8,128)S(1)} %shard_map.156.ours, f32[176,128]{1,0:T(8,128)S(1)} %collective-permute-done.7.theirs, ...), custom_call_target="tpu_custom_call" | custom-call | flops 2000000000 | tf_op jit(solution)/shard_map/pallas_call | solution.py:275
  (1 shorter events, 0.0 us)
Async XLA Ops:
  0.6 17.0 %collective-permute-start.1 = (bf16[512,256]{1,0:T(8,128)(2,1)}, bf16[512,256]{1,0:T(8,128)(2,1)S(1)}, u32[]{:S(2)}, u32[]{:S(2)}) collective-permute-start(bf16[512,256]{1,0:T(8,128)(2,1)} %bitcast.12), channel_id=1, source_target_pairs={{0,2},{2,0},{4,6},{6,4},{8,10},{10,8},{12,14},{14,12},{1,3},{3,1},... | collective-permute-start | bytes 786440 | tf_op jit(solution)/shard_map/ppermute | solution.py:292
  3.6 17.5 %collective-permute-start = (bf16[512,256]{1,0:T(8,128)(2,1)}, bf16[512,256]{1,0:T(8,128)(2,1)S(1)}, u32[]{:S(2)}, u32[]{:S(2)}) collective-permute-start(bf16[512,256]{1,0:T(8,128)(2,1)} %bitcast.13), channel_id=1, source_target_pairs={{2,4},{6,8},{10,12},{4,2},{8,6},{12,10},{3,5},{7,9},{11,13},{5,3},... | collective-permute-start | bytes 786440 | tf_op jit(solution)/shard_map/ppermute | solution.py:292
  5.1 8.6 %copy-start = (bf16[1,512,256]{2,1,0:T(8,128)(2,1)S(1)}, bf16[1,512,256]{2,1,0:T(8,128)(2,1)}, u32[]{:S(2)}) copy-start(bf16[1,512,256]{2,1,0:T(8,128)(2,1)} %param.10) | copy-start | bytes 786436
  5.1 8.6 %copy-start.1 = (s32[9,512]{1,0:T(8,128)S(1)}, s32[9,512]{1,0:T(8,128)}, u32[]{:S(2)}) copy-start(s32[9,512]{1,0:T(8,128)} %neighbours_hbm.1) | copy-start | bytes 55300
  5.1 8.6 %copy-start.2 = (f32[9,256]{1,0:T(8,128)S(1)}, f32[9,256]{1,0:T(8,128)}, u32[]{:S(2)}) copy-start(f32[9,256]{1,0:T(8,128)} %weights_hbm.1) | copy-start | bytes 27652
  5.1 8.6 %copy-start.3 = (f32[8,512]{1,0:T(8,128)S(1)}, f32[8,512]{1,0:T(8,128)}, u32[]{:S(2)}) copy-start(f32[8,512]{1,0:T(8,128)} %target_hbm.1) | copy-start | bytes 49156
  5.1 8.6 %copy-start.4 = (bf16[8,256]{1,0:T(8,128)(2,1)S(1)}, bf16[8,256]{1,0:T(8,128)(2,1)}, u32[]{:S(2)}) copy-start(bf16[8,256]{1,0:T(8,128)(2,1)} %head_hbm.1) | copy-start | bytes 12292
  5.1 8.6 %copy-start.5 = (f32[1024]{0:T(1024)S(1)}, f32[1024]{0:T(1024)}, u32[]{:S(2)}) copy-start(f32[1024]{0:T(1024)} %param.16) | copy-start | bytes 12292
  5.2 8.6 %copy-start.6 = (f32[256]{0:T(256)S(1)}, f32[256]{0:T(256)}, u32[]{:S(2)}) copy-start(f32[256]{0:T(256)} %param.18) | copy-start | bytes 3076
  5.2 8.6 %copy-start.7 = (f32[256]{0:T(256)S(1)}, f32[256]{0:T(256)}, u32[]{:S(2)}) copy-start(f32[256]{0:T(256)} %param.14) | copy-start | bytes 3076
  6.0 21.5 %all-to-all-start = ((bf16[8,128,256]{2,1,0:T(8,128)(2,1)}), bf16[8,128,256]{2,1,0:T(8,128)(2,1)S(1)}, u32[]{:S(2)}, u32[]{:S(2)}) async-start(bf16[8,128,256]{2,1,0:T(8,128)(2,1)} %shard_map.145), calls=%async_computation | async-start | bytes 1048576 | tf_op jit(solution)/shard_map/all_to_all | solution.py:325
  16.3 1.4 %copy-start.8 = (bf16[8,512,256]{2,1,0:T(8,128)(2,1)}, bf16[8,512,256]{2,1,0:T(8,128)(2,1)S(1)}, u32[]{:S(2)}) copy-start(bf16[8,512,256]{2,1,0:T(8,128)(2,1)S(1)} %get-tuple-element.69.a) | copy-start | bytes 6291460
  19.8 1.3 %copy-start.10 = (bf16[8,512,256]{2,1,0:T(8,128)(2,1)}, bf16[8,512,256]{2,1,0:T(8,128)(2,1)S(1)}, u32[]{:S(2)}) copy-start(bf16[8,512,256]{2,1,0:T(8,128)(2,1)S(1)} %get-tuple-element.70.b) | copy-start | bytes 6291460
  23.5 1.4 %copy-start.12 = (bf16[8,512,256]{2,1,0:T(8,128)(2,1)}, bf16[8,512,256]{2,1,0:T(8,128)(2,1)S(1)}, u32[]{:S(2)}) copy-start(bf16[8,512,256]{2,1,0:T(8,128)(2,1)S(1)} %get-tuple-element.71.c) | copy-start | bytes 6291460
  27.6 1.9 %collective-permute-start.2 = (bf16[8,128,256]{2,1,0:T(8,128)(2,1)S(1)}, bf16[8,128,256]{2,1,0:T(8,128)(2,1)S(1)}, u32[]{:S(2)}, u32[]{:S(2)}) collective-permute-start(bf16[8,128,256]{2,1,0:T(8,128)(2,1)S(1)} %all-to-all-done.mine), channel_id=1, source_target_pairs={{0,1},{1,0},{2,3},{3,2},{4,5},{5,4},{6,7},{7,6},{8,9},{9,8},{10,11... | collective-permute-start | bytes 1572872 | tf_op jit(solution)/shard_map/ppermute | solution.py:296
  31.5 1.2 %collective-permute-start.3 = (f32[8,512]{1,0:T(8,128)S(1)}, f32[8,512]{1,0:T(8,128)S(1)}, u32[]{:S(2)}, u32[]{:S(2)}) collective-permute-start(f32[8,512]{1,0:T(8,128)S(1)} %get-tuple-element.57.mine), channel_id=1, source_target_pairs={{0,1},{1,0},{2,3},{3,2},{4,5},{5,4},{6,7},{7,6},{8,9},{9,8},{10,11... | collective-permute-start | bytes 49160 | tf_op jit(solution)/shard_map/ppermute | solution.py:296
  32.7 1.6 %copy-start.9 = (bf16[8,512,256]{2,1,0:T(8,128)(2,1)S(1)}, bf16[8,512,256]{2,1,0:T(8,128)(2,1)}, u32[]{:S(2)}) copy-start(bf16[8,512,256]{2,1,0:T(8,128)(2,1)} %copy-done.8) | copy-start | bytes 6291460
  32.7 2.2 %copy-start.11 = (bf16[8,512,256]{2,1,0:T(8,128)(2,1)S(1)}, bf16[8,512,256]{2,1,0:T(8,128)(2,1)}, u32[]{:S(2)}) copy-start(bf16[8,512,256]{2,1,0:T(8,128)(2,1)} %copy-done.10) | copy-start | bytes 6291460
  32.7 2.9 %copy-start.13 = (bf16[8,512,256]{2,1,0:T(8,128)(2,1)S(1)}, bf16[8,512,256]{2,1,0:T(8,128)(2,1)}, u32[]{:S(2)}) copy-start(bf16[8,512,256]{2,1,0:T(8,128)(2,1)} %copy-done.12) | copy-start | bytes 6291460
  37.5 2.3 %collective-permute-start.4 = (bf16[8,128,128]{2,1,0:T(8,128)(2,1)S(1)}, bf16[8,128,128]{2,1,0:T(8,128)(2,1)S(1)}, u32[]{:S(2)}, u32[]{:S(2)}) collective-permute-start(bf16[8,128,128]{2,1,0:T(8,128)(2,1)S(1)} %get-tuple-element.74), channel_id=1, source_target_pairs={{0,1},{1,0},{2,3},{3,2},{4,5},{5,4},{6,7},{7,6},{8,9},{9,8},{10,11... | collective-permute-start | bytes 786440 | tf_op jit(solution)/shard_map/ppermute | solution.py:296
  37.6 15.7 %collective-permute-start.6 = (bf16[512,256]{1,0:T(8,128)(2,1)S(1)}, bf16[512,256]{1,0:T(8,128)(2,1)S(1)}, u32[]{:S(2)}, u32[]{:S(2)}) collective-permute-start(bf16[512,256]{1,0:T(8,128)(2,1)S(1)} %get-tuple-element.76.mixed_grad.own), channel_id=1, source_target_pairs={{0,2},{2,0},{4,6},{6,4},{8,10},{10,8},{12,14},{14,12},{1,3},{3,1},... | collective-permute-start | bytes 786440 | tf_op jit(solution)/shard_map/ppermute | solution.py:292
  39.1 16.4 %collective-permute-start.5 = (bf16[512,256]{1,0:T(8,128)(2,1)S(1)}, bf16[512,256]{1,0:T(8,128)(2,1)S(1)}, u32[]{:S(2)}, u32[]{:S(2)}) collective-permute-start(bf16[512,256]{1,0:T(8,128)(2,1)S(1)} %get-tuple-element.76.mixed_grad.own), channel_id=1, source_target_pairs={{2,4},{6,8},{10,12},{4,2},{8,6},{12,10},{3,5},{7,9},{11,13},{5,3},... | collective-permute-start | bytes 786440 | tf_op jit(solution)/shard_map/ppermute | solution.py:292
  40.6 17.7 %all-to-all-start.1 = ((bf16[8,176,128]{2,1,0:T(8,128)(2,1)}), bf16[8,176,128]{2,1,0:T(8,128)(2,1)S(1)}, u32[]{:S(2)}, u32[]{:S(2)}) async-start(bf16[8,176,128]{2,1,0:T(8,128)(2,1)} %shard_map.152), calls=%async_computation.1 | async-start | bytes 720896 | tf_op jit(solution)/shard_map/all_to_all | solution.py:325
  58.3 1.4 %collective-permute-start.7 = (f32[176,128]{1,0:T(8,128)S(1)}, f32[176,128]{1,0:T(8,128)S(1)}, u32[]{:S(2)}, u32[]{:S(2)}) collective-permute-start(f32[176,128]{1,0:T(8,128)S(1)} %shard_map.156.ours), channel_id=1, source_target_pairs={{0,1},{1,0},{2,3},{3,2},{4,5},{5,4},{6,7},{7,6},{8,9},{9,8},{10,11... | collective-permute-start | bytes 270344 | tf_op jit(solution)/shard_map/ppermute | solution.py:296

commit v3 on v2

--- a/solution.py
+++ b/solution.py
@@ -100,25 +100,26 @@
     mixed_out[...] = mixed
 
 
-def mix(where, tile, weights, mixed_in, taken, mixed_out):
+def mix(where, tile, weights, taken_in, mixed_in, taken, mixed_out):
     source = tile[...]
     mixed = mixed_in[...]
     for tap in range(weights.shape[0]):
         if tap != CENTRE:
             rows = tap_rows(where, source, tap)
-            taken[tap - (tap > CENTRE)] = rows.astype(BF16)
+            slot = tap - (tap > CENTRE)
+            taken[slot] = taken_in[slot] + rows.astype(BF16)
             mixed = mixed + weights[tap : tap + 1, :] * rows
     mixed_out[...] = mixed
 
 
-def mix_pair_kernel(info, tile, neighbours, weights, mixed_in, taken, mixed_out):
-    mix(pair_places(info, neighbours), tile, weights, mixed_in, taken, mixed_out)
+def mix_pair_kernel(info, tile, neighbours, weights, taken_in, mixed_in, taken, mixed_out):
+    mix(pair_places(info, neighbours), tile, weights, taken_in, mixed_in, taken, mixed_out)
 
 
 def mix_side_kernel(
-    info, tile, neighbours, weights, gain, mixed_in, taken, mixed_out, normed_out
-):
-    mix(side_places(info, neighbours), tile, weights, mixed_in, taken, mixed_out)
+    info, tile, neighbours, weights, gain, taken_in, mixed_in, taken, mixed_out, normed_out
+):
+    mix(side_places(info, neighbours), tile, weights, taken_in, mixed_in, taken, mixed_out)
     mixed = mixed_out[...]
     centred = mixed - row_mean(mixed)
     inverse = lax.rsqrt(row_mean(centred * centred) + 1e-06)
@@ -185,7 +186,7 @@
 
 
 def weights_kernel(
-    info, pre_grad, normed, act, grad, features, down, scale, a, b, c, mixed_grad, loss,
+    info, pre_grad, normed, act, grad, features, down, scale, taken, mixed_grad, loss,
     keep, send, small,
 ):
     normed_t = turned(normed[...])
@@ -195,8 +196,8 @@
     head_part = mul(grad[...], features[...]) + scale[...] * (through[:8] + through[8:])
     flow = mixed_grad[...].astype(F32)
     depth = [
-        jnp.sum((a[k] + b[k] + c[k]).astype(F32) * flow, axis=0, keepdims=True)
-        for k in range(a.shape[0])
+        jnp.sum(taken[k].astype(F32) * flow, axis=0, keepdims=True)
+        for k in range(taken.shape[0])
     ]
     depth.insert(CENTRE, jnp.sum(features[...].astype(F32) * flow, axis=0, keepdims=True))
     small[...] = jnp.concatenate([head_part] + depth + [loss[...]], axis=0)
@@ -209,6 +210,19 @@
         send[block, :, :] = jnp.where(first, higher, lower).astype(BF16)
         extra = [small[:, :LANES], small[:, LANES:], summed[:, lanes], jnp.zeros((4, LANES), F32)]
         keep[block, LANES:, :] = jnp.concatenate(extra, axis=0).astype(BF16)
+
+
+def back_kernel(
+    info, mine, other, target, reach, slope, up, mixed, gain, normed, act, features, down, scale, taken,
+    mixed_grad, grad, keep, send, pre_grad, loss, small,
+):
+    backward_kernel(
+        mine, other, target, reach, slope, up, mixed, gain, mixed_grad, pre_grad, grad, loss
+    )
+    weights_kernel(
+        info, pre_grad, normed, act, grad, features, down, scale, taken, mixed_grad, loss,
+        keep, send, small,
+    )
 
 
 def join_kernel(keep, came, joined):
@@ -355,18 +369,20 @@
         scratch=[pltpu.SemaphoreType.DMA((8,))],
         flops=OWN,
     )
-    taken_pair, mixed = call(
+    taken, mixed = call(
         mix_pair_kernel,
         [(many, BF16), (tile, F32)],
         1,
-        info, pair, places, weights, mixed,
+        info, pair, places, weights, taken, mixed,
+        aliases={4: 0, 5: 1},
         flops=NEAR,
     )
-    taken_side, mixed, normed = call(
+    taken, mixed, normed = call(
         mix_side_kernel,
         [(many, BF16), (tile, F32), (tile, BF16)],
         1,
-        info, side, places, weights, gain, mixed,
+        info, side, places, weights, gain, taken, mixed,
+        aliases={5: 0, 6: 1},
         flops=NEAR,
     )
     outs = [((pixels, hidden), BF16), ((pixels, hidden), F32), ((8, pixels), F32)]
@@ -382,20 +398,16 @@
         )
     else:
         act, slope, forecast = call(forward, outs, 0, normed, up, reach, bias, base)
-    mixed_grad, pre_grad, grad, loss = call(
-        backward_kernel,
-        [(tile, BF16), ((pixels, hidden), BF16), ((8, pixels), BF16), ((1, channels), F32)],
-        0,
-        forecast, swap(forecast), target, reach, slope, up, mixed, gain,
-    )
     blocks = hidden // LANES
     full = ((blocks, LANES + EXTRA, LANES), BF16)
-    keep, send, small = call(
-        weights_kernel,
-        [full, ((blocks, LANES, LANES), BF16), ((18, channels), F32)],
-        1,
-        info, pre_grad, normed, act, grad, own, down, scale, taken, taken_pair, taken_side,
-        mixed_grad, loss,
+    mixed_grad, grad, keep, send = call(
+        back_kernel,
+        [(tile, BF16), ((8, pixels), BF16), full, ((blocks, LANES, LANES), BF16)],
+        1,
+        info, forecast, swap(forecast), target, reach, slope, up, mixed, gain,
+        normed, act, own, down, scale, taken,
+        scratch=[pltpu.VMEM((pixels, hidden), BF16), pltpu.VMEM((1, channels), F32),
+                 pltpu.VMEM((18, channels), F32)],
         flops=NEAR,
     )
     came = swap(send)
@@ -445,6 +457,8 @@
     summed = jnp.transpose(summed + swap(summed), (0, 2, 1)).reshape(hidden, 8)
     summed = lax.psum_scatter(summed, "pix", scatter_dimension=0, tiled=True)
     down_grad = layer_scale * jnp.dot(summed, head_matrix.astype(F32), precision=exact)
+    small = keep[0, LANES : LANES + 36].astype(F32).reshape(2, 18, LANES)
+    small = jnp.transpose(small, (1, 0, 2)).reshape(18, channels)
     small = lax.psum(small, ("pix", "mem"))
     return (
         small[17, :1] * loss_scale,

time: 62.3 us -> 59.7 us (0.958); the launches traced: 61.2 us -> 59.3 us
  local copies, waits for them, and re-layouts: 5.9 us -> 1.58 us
  waiting for transfers between devices: 11 us -> 13.2 us
  Pallas kernels: 22.2 us -> 22.9 us
    unnamed x28 -> x36, local copies, waits for them, and re-layouts: 5.9 us -> 1.58 us
    all_to_all x2, waiting for transfers between devices: 2.69 us -> 4 us  [everywhere(): return lax.all_to_all(array, 'pix', split_axis=0, concat_axis=0)]
    ppermute x2, waiting for transfers between devices: 4.08 us -> 4.98 us  [pair_tiles(): lax.ppermute(array, 'pix', inner)]
    pallas_call x13 -> x12, Pallas kernels: 22.2 us -> 22.9 us  [call(): pl.pallas_call(kernel, out_shape=tuple((jax.ShapeDtypeStruct(shape, dtype...]
    all_to_all x2, starting transfers between devices: 14.1 us -> 13.5 us  [everywhere(): return lax.all_to_all(array, 'pix', split_axis=0, concat_axis=0)]
  transfers between devices with their start and end apart: 10 -> 10, of which waited for: 5 -> 5; matrix products, arithmetic and copies ran while one was open for 1% -> 1% of each run, Pallas kernels for 26% -> 28%
where the time goes in v3:
time: 59.7 us; the launch traced here: 59.3 us
  Pallas kernels  22.9 us (38%)
  starting transfers between devices  19.7 us (33%)
  waiting for transfers between devices  13.2 us (22%)
  local copies, waits for them, and re-layouts  1.58 us (3%)
  between operations  1.07 us (2%)
  other arithmetic  0.86 us (1%)
    pallas_call x12, Pallas kernels, call(): pl.pallas_call(kernel, out_shape=tuple((jax.ShapeDtypeStruct(shape, dtype...  22.9 us
    all_to_all x2, starting transfers between devices, everywhere(): return lax.all_to_all(array, 'pix', split_axis=0, concat_axis=0)  13.5 us
    ppermute x2, waiting for transfers between devices, pair_tiles(): lax.ppermute(array, 'pix', inner)  4.98 us
    ppermute x2, starting transfers between devices, pair_tiles(): lax.ppermute(array, 'pix', inner)  4.42 us
    ppermute x4, waiting for transfers between devices, swap(): return lax.ppermute(array, 'mem', [(0, 1), (1, 0)])  4.24 us
    all_to_all x2, waiting for transfers between devices, everywhere(): return lax.all_to_all(array, 'pix', split_axis=0, concat_axis=0)  4 us
    unnamed x36, local copies, waits for them, and re-layouts  1.58 us
    ppermute x2, starting transfers between devices, pair_tiles(): lax.ppermute(array, 'pix', outer)  1.33 us
  transfers between devices with their start and end apart: 10, of which 5 were waited for; matrix products, arithmetic and copies ran while one was open for 1% of the time, Pallas kernels for 28%

profile of v3, /device:TPU:0, one launch (start us, length us, event | category | flops | bytes accessed | tf_op | source)
XLA Modules:
  0.0 59.3 jit_solution(14545029861082283568)
XLA Ops:
  0.6 3.0 %collective-permute-start.1 = (bf16[512,256]{1,0:T(8,128)(2,1)}, bf16[512,256]{1,0:T(8,128)(2,1)S(1)}, u32[]{:S(2)}, u32[]{:S(2)}) collective-permute-start(bf16[512,256]{1,0:T(8,128)(2,1)} %bitcast.12), channel_id=1, source_target_pairs={{0,2},{2,0},{4,6},{6,4},{8,10},{10,8},{12,14},{14,12},{1,3},{3,1},... | collective-permute-start | bytes 786440 | tf_op jit(solution)/shard_map/ppermute | solution.py:306
  3.6 0.7 %collective-permute-start = (bf16[512,256]{1,0:T(8,128)(2,1)}, bf16[512,256]{1,0:T(8,128)(2,1)S(1)}, u32[]{:S(2)}, u32[]{:S(2)}) collective-permute-start(bf16[512,256]{1,0:T(8,128)(2,1)} %bitcast.13), channel_id=1, source_target_pairs={{2,4},{6,8},{10,12},{4,2},{8,6},{12,10},{3,5},{7,9},{11,13},{5,3},... | collective-permute-start | bytes 786440 | tf_op jit(solution)/shard_map/ppermute | solution.py:306
  4.3 0.8 %fusion = bf16[2,64,256]{2,1,0:T(8,128)(2,1)S(1)} fusion(s32[]{:T(128)S(6)} %select_n.11, bf16[1,128,256]{2,1,0:T(8,128)(2,1)} %bitcast.18, bf16[1,128,256]{2,1,0:T(8,128)(2,1)} %bitcast.19), kind=kLoop, calls=%fused_computation.2 | loop fusion | flops 131072 | bytes 196612 | tf_op jit(solution)/shard_map/stack | solution.py:344
  5.1 0.0 copy-start
  5.1 0.0 copy-start.1
  5.1 0.0 copy-start.2
  5.1 0.0 copy-start.3
  5.1 0.0 copy-start.4
  5.1 0.0 copy-start.5
  5.2 0.0 copy-start.6
  5.2 0.0 copy-start.7
  5.2 0.8 %shard_map.145 = bf16[8,128,256]{2,1,0:T(8,128)(2,1)} custom-call(bf16[128,256]{1,0:T(8,128)(2,1)S(1)} %bitcast.11), custom_call_target="tpu_custom_call" | custom-call | flops 8000000000 | tf_op jit(solution)/shard_map/pallas_call | solution.py:289
  6.0 7.6 %all-to-all-start = ((bf16[8,128,256]{2,1,0:T(8,128)(2,1)}), bf16[8,128,256]{2,1,0:T(8,128)(2,1)S(1)}, u32[]{:S(2)}, u32[]{:S(2)}) async-start(bf16[8,128,256]{2,1,0:T(8,128)(2,1)} %shard_map.145), calls=%async_computation | async-start | bytes 1048576 | tf_op jit(solution)/shard_map/all_to_all | solution.py:339
  13.6 0.1 pad_add_fusion.info
  13.6 0.0 copy-done
  13.7 0.0 copy-done.1
  13.7 0.0 copy-done.2
  13.7 0.0 copy-done.3
  13.7 0.0 copy-done.4
  13.7 0.0 copy-done.5
  13.7 0.0 copy-done.6
  13.7 0.0 copy-done.7
  13.7 2.5 %shard_map.146 = (bf16[512,256]{1,0:T(8,128)(2,1)S(1)}, f32[9,256]{1,0:T(8,128)S(1)}, bf16[8,256]{1,0:T(8,128)(2,1)S(1)}, f32[1,256]{1,0:T(1,128)S(1)}, f32[1,25...) custom-call(s32[3]{0:T(128)S(1)} %pad_add_fusion.info, ...), custom_call_target="tpu_custom_call" | custom-call | flops 8000000000 | tf_op jit(solution)/shard_map/pallas_call | solution.py:289
  16.2 0.0 copy-start.10
  16.2 0.7 %copy-done.10 = bf16[512,256]{1,0:T(8,128)(2,1)} copy-done((bf16[512,256]{1,0:T(8,128)(2,1)}, bf16[512,256]{1,0:T(8,128)(2,1)S(1)}, u32[]{:S(2)}) %copy-start.10) | copy-done | bytes 262168
  16.9 0.0 copy-start.14
  16.9 0.0 copy-start.12
  16.9 0.0 collective-permute-done.1.tile
  16.9 2.8 %shard_map.147 = (bf16[8,512,256]{2,1,0:T(8,128)(2,1)S(1)}, f32[512,256]{1,0:T(8,128)S(1)}) custom-call(s32[3]{0:T(128)S(1)} %pad_add_fusion.info, bf16[512,256]{1,0:T(8,128)(2,1)S(1)} %collective-permute-done.1.tile, s32[9,512]{1,0:T(8,128)S(1)} %get-tuple-element.43.neighbours, ...), custom_call_target="tpu_custom_call", output_to_operand_aliasing={{0}: (4, {}), {1}: (5, {})} | custom-call | flops 49999998976 | tf_op jit(solution)/shard_map/pallas_call | solution.py:289
  19.7 0.0 copy-done.14
  19.7 0.0 collective-permute-done.tile
  19.7 0.0 copy-done.12
  19.7 0.0 copy-done.16
  19.7 3.0 %shard_map.148 = (bf16[8,512,256]{2,1,0:T(8,128)(2,1)S(1)}, f32[512,256]{1,0:T(8,128)S(1)}, bf16[512,256]{1,0:T(8,128)(2,1)S(1)}) custom-call(s32[3]{0:T(128)S(1)} %pad_add_fusion.info, bf16[512,256]{1,0:T(8,128)(2,1)S(1)} %collective-permute-done.tile, s32[9,512]{1,0:T(8,128)S(1)} %get-tuple-element.43.neighbours, ...), custom_call_target="tpu_custom_call", output_to_operand_aliasing={{0}: (5, {}), {1}: (6, {})} | custom-call | flops 49999998976 | tf_op jit(solution)/shard_map/pallas_call | solution.py:289
  22.7 0.0 copy-start.8
  22.7 0.8 %copy-done.8 = f32[512,256]{1,0:T(8,128)} copy-done((f32[512,256]{1,0:T(8,128)}, f32[512,256]{1,0:T(8,128)S(1)}, u32[]{:S(2)}) %copy-start.8) | copy-done | bytes 524312
  23.5 4.0 %all-to-all-done.mine = bf16[8,128,256]{2,1,0:T(8,128)(2,1)S(1)} async-done(((bf16[8,128,256]{2,1,0:T(8,128)(2,1)}), bf16[8,128,256]{2,1,0:T(8,128)(2,1)S(1)}, u32[]{:S(2)}, u32[]{:S(2)}) %all-to-all-start) | async-done | bytes 524320 | tf_op jit(solution)/shard_map/all_to_all | solution.py:339
  27.5 0.0 collective-permute-start.2
  27.5 1.9 %collective-permute-done.2.other = bf16[8,128,256]{2,1,0:T(8,128)(2,1)S(1)} collective-permute-done((bf16[8,128,256]{2,1,0:T(8,128)(2,1)S(1)}, bf16[8,128,256]{2,1,0:T(8,128)(2,1)S(1)}, u32[]{:S(2)}, u32[]{:S(2)}) %collective-permute-start.2) | collective-permute-done | bytes 524320 | tf_op jit(solution)/shard_map/ppermute | solution.py:310
  29.5 2.0 %shard_map.149 = (bf16[512,1024]{1,0:T(8,128)(2,1)S(1)}, f32[512,1024]{1,0:T(8,128)S(1)}, f32[8,512]{1,0:T(8,128)S(1)}, bf16[1024,256]{1,0:T(8,128)(2,1)S(1)}, b...) custom-call(s32[3]{0:T(128)S(1)} %pad_add_fusion.info, bf16[512,256]{1,0:T(8,128)(2,1)S(1)} %get-tuple-element.51.normed, ...), custom_call_target="tpu_custom_call" | custom-call | flops 2000000000 | tf_op jit(solution)/shard_map/pallas_call | solution.py:289
  31.5 0.1 collective-permute-start.3
  31.6 1.1 %collective-permute-done.3.other = f32[8,512]{1,0:T(8,128)S(1)} collective-permute-done((f32[8,512]{1,0:T(8,128)S(1)}, f32[8,512]{1,0:T(8,128)S(1)}, u32[]{:S(2)}, u32[]{:S(2)}) %collective-permute-start.3) | collective-permute-done | bytes 16416 | tf_op jit(solution)/shard_map/ppermute | solution.py:310
  32.7 0.0 copy-done.9
  32.7 0.0 copy-done.11
  32.7 0.0 copy-done.15
  32.7 0.0 copy-done.17
  32.7 2.5 %shard_map.150 = (bf16[512,256]{1,0:T(8,128)(2,1)S(1)}, bf16[8,512]{1,0:T(8,128)(2,1)S(1)}, bf16[8,176,128]{2,1,0:T(8,128)(2,1)S(1)}, bf16[8,128,128]{2,1,0:T(8,128)(2,1)S(1)}) custom-call(s32[3]{0:T(128)S(1)} %pad_add_fusion.info, f32[8,512]{1,0:T(8,128)S(1)} %get-tuple-element.57.mine, f32[8,512]{1,0:T(8,128)S(1)} %collective-permute-done.3.other, ...), custom_call_target="tpu_custom_call" | custom-call | flops 49999998976 | tf_op jit(solution)/shard_map/pallas_call | solution.py:289
  35.2 0.2 collective-permute-start.4
  35.4 1.4 %collective-permute-start.6 = (bf16[512,256]{1,0:T(8,128)(2,1)S(1)}, bf16[512,256]{1,0:T(8,128)(2,1)S(1)}, u32[]{:S(2)}, u32[]{:S(2)}) collective-permute-start(bf16[512,256]{1,0:T(8,128)(2,1)S(1)} %get-tuple-element.71.own), channel_id=1, source_target_pairs={{0,2},{2,0},{4,6},{6,4},{8,10},{10,8},{12,14},{14,12},{1,3},{3,1},... | collective-permute-start | bytes 786440 | tf_op jit(solution)/shard_map/ppermute | solution.py:306
  36.8 0.7 %collective-permute-start.5 = (bf16[512,256]{1,0:T(8,128)(2,1)S(1)}, bf16[512,256]{1,0:T(8,128)(2,1)S(1)}, u32[]{:S(2)}, u32[]{:S(2)}) collective-permute-start(bf16[512,256]{1,0:T(8,128)(2,1)S(1)} %get-tuple-element.71.own), channel_id=1, source_target_pairs={{2,4},{6,8},{10,12},{4,2},{8,6},{12,10},{3,5},{7,9},{11,13},{5,3},... | collective-permute-start | bytes 786440 | tf_op jit(solution)/shard_map/ppermute | solution.py:306
  37.5 0.0 collective-permute-done.4.came
  37.5 0.0 copy-start.13
  37.5 0.8 %shard_map.151 = bf16[8,176,128]{2,1,0:T(8,128)(2,1)} custom-call(bf16[8,176,128]{2,1,0:T(8,128)(2,1)S(1)} %get-tuple-element.68.keep, bf16[8,128,128]{2,1,0:T(8,128)(2,1)S(1)} %collective-permute-done.4.came), custom_call_target="tpu_custom_call" | custom-call | flops 2000000000 | tf_op jit(solution)/shard_map/pallas_call | solution.py:289
  38.3 5.9 %all-to-all-start.1 = ((bf16[8,176,128]{2,1,0:T(8,128)(2,1)}), bf16[8,176,128]{2,1,0:T(8,128)(2,1)S(1)}, u32[]{:S(2)}, u32[]{:S(2)}) async-start(bf16[8,176,128]{2,1,0:T(8,128)(2,1)} %shard_map.151), calls=%async_computation.1 | async-start | bytes 720896 | tf_op jit(solution)/shard_map/all_to_all | solution.py:339
  44.3 0.0 copy-done.13
  44.3 2.1 %shard_map.152.partial = f32[512,256]{1,0:T(8,128)S(1)} custom-call(s32[3]{0:T(128)S(1)} %pad_add_fusion.info, bf16[512,256]{1,0:T(8,128)(2,1)S(1)} %get-tuple-element.71.own, s32[9,512]{1,0:T(8,128)S(1)} %get-tuple-element.43.neighbours, f32[9,256]{1,0:T(8,128)S(1)} %copy-done.13, bf16[8,512]{1,0:T(8,128)(2,1)S(1)} %get-tuple-element.72.grad, ...), custom_call_target="tpu_custom_call" | custom-call | flops 8000000000 | tf_op jit(solution)/shard_map/pallas_call | solution.py:289
  46.4 5.0 %collective-permute-done.6.tile = bf16[512,256]{1,0:T(8,128)(2,1)S(1)} collective-permute-done((bf16[512,256]{1,0:T(8,128)(2,1)S(1)}, bf16[512,256]{1,0:T(8,128)(2,1)S(1)}, u32[]{:S(2)}, u32[]{:S(2)}) %collective-permute-start.6) | collective-permute-done | bytes 262176 | tf_op jit(solution)/shard_map/ppermute | solution.py:306
  51.4 2.1 %shard_map.153.partial = f32[512,256]{1,0:T(8,128)S(1)} custom-call(s32[3]{0:T(128)S(1)} %pad_add_fusion.info, bf16[512,256]{1,0:T(8,128)(2,1)S(1)} %collective-permute-done.6.tile, s32[9,512]{1,0:T(8,128)S(1)} %get-tuple-element.43.neighbours, f32[9,256]{1,0:T(8,128)S(1)} %copy-done.13, f32[512,256]{1,0:T(8,128)S(1)} %shard_map.152.partial), custom_call_target="tpu_custom_call" | custom-call | flops 49999998976 | tf_op jit(solution)/shard_map/pallas_call | solution.py:289
  53.5 0.0 collective-permute-done.5.tile
  53.5 2.8 %shard_map.154 = bf16[512,256]{1,0:T(8,128)(2,1)} custom-call(s32[3]{0:T(128)S(1)} %pad_add_fusion.info, bf16[512,256]{1,0:T(8,128)(2,1)S(1)} %collective-permute-done.5.tile, s32[9,512]{1,0:T(8,128)S(1)} %get-tuple-element.43.neighbours, f32[9,256]{1,0:T(8,128)S(1)} %copy-done.13, f32[512,256]{1,0:T(8,128)S(1)} %shard_map.153.partial), custom_call_target="tpu_custom_call" | custom-call | flops 49999998976 | tf_op jit(solution)/shard_map/pallas_call | solution.py:289
  56.3 0.0 all-to-all-done.1.parts
  56.3 0.1 collective-permute-start.7
  56.4 1.3 %collective-permute-done.7.theirs = f32[176,128]{1,0:T(8,128)S(1)} collective-permute-done((f32[176,128]{1,0:T(8,128)S(1)}, f32[176,128]{1,0:T(8,128)S(1)}, u32[]{:S(2)}, u32[]{:S(2)}) %collective-permute-start.7) | collective-permute-done | bytes 90144 | tf_op jit(solution)/shard_map/ppermute | solution.py:310
  57.7 1.4 %shard_map.156 = (f32[1]{0:T(128)}, f32[128,256]{1,0:T(8,128)}, f32[128,256]{1,0:T(8,128)}, f32[9,256]{1,0:T(8,128)}, f32[8,256]{1,0:T(8,128)}) custom-call(s32[3]{0:T(128)S(1)} %pad_add_fusion.info, f32[176,128]{1,0:T(8,128)S(1)} %shard_map.155.ours, f32[176,128]{1,0:T(8,128)S(1)} %collective-permute-done.7.theirs, ...), custom_call_target="tpu_custom_call" | custom-call | flops 2000000000 | tf_op jit(solution)/shard_map/pallas_call | solution.py:289
  (6 shorter events, 0.1 us)
Async XLA Ops:
  0.6 16.3 %collective-permute-start.1 = (bf16[512,256]{1,0:T(8,128)(2,1)}, bf16[512,256]{1,0:T(8,128)(2,1)S(1)}, u32[]{:S(2)}, u32[]{:S(2)}) collective-permute-start(bf16[512,256]{1,0:T(8,128)(2,1)} %bitcast.12), channel_id=1, source_target_pairs={{0,2},{2,0},{4,6},{6,4},{8,10},{10,8},{12,14},{14,12},{1,3},{3,1},... | collective-permute-start | bytes 786440 | tf_op jit(solution)/shard_map/ppermute | solution.py:306
  3.6 16.1 %collective-permute-start = (bf16[512,256]{1,0:T(8,128)(2,1)}, bf16[512,256]{1,0:T(8,128)(2,1)S(1)}, u32[]{:S(2)}, u32[]{:S(2)}) collective-permute-start(bf16[512,256]{1,0:T(8,128)(2,1)} %bitcast.13), channel_id=1, source_target_pairs={{2,4},{6,8},{10,12},{4,2},{8,6},{12,10},{3,5},{7,9},{11,13},{5,3},... | collective-permute-start | bytes 786440 | tf_op jit(solution)/shard_map/ppermute | solution.py:306
  5.1 8.6 %copy-start = (bf16[1,512,256]{2,1,0:T(8,128)(2,1)S(1)}, bf16[1,512,256]{2,1,0:T(8,128)(2,1)}, u32[]{:S(2)}) copy-start(bf16[1,512,256]{2,1,0:T(8,128)(2,1)} %param.10) | copy-start | bytes 786436
  5.1 8.6 %copy-start.1 = (s32[9,512]{1,0:T(8,128)S(1)}, s32[9,512]{1,0:T(8,128)}, u32[]{:S(2)}) copy-start(s32[9,512]{1,0:T(8,128)} %neighbours_hbm.1) | copy-start | bytes 55300
  5.1 8.6 %copy-start.2 = (f32[9,256]{1,0:T(8,128)S(1)}, f32[9,256]{1,0:T(8,128)}, u32[]{:S(2)}) copy-start(f32[9,256]{1,0:T(8,128)} %weights_hbm.1) | copy-start | bytes 27652
  5.1 8.5 %copy-start.3 = (f32[8,512]{1,0:T(8,128)S(1)}, f32[8,512]{1,0:T(8,128)}, u32[]{:S(2)}) copy-start(f32[8,512]{1,0:T(8,128)} %target_hbm.1) | copy-start | bytes 49156
  5.1 8.5 %copy-start.4 = (bf16[8,256]{1,0:T(8,128)(2,1)S(1)}, bf16[8,256]{1,0:T(8,128)(2,1)}, u32[]{:S(2)}) copy-start(bf16[8,256]{1,0:T(8,128)(2,1)} %head_hbm.1) | copy-start | bytes 12292
  5.1 8.5 %copy-start.5 = (f32[1024]{0:T(1024)S(1)}, f32[1024]{0:T(1024)}, u32[]{:S(2)}) copy-start(f32[1024]{0:T(1024)} %param.16) | copy-start | bytes 12292
  5.2 8.5 %copy-start.6 = (f32[256]{0:T(256)S(1)}, f32[256]{0:T(256)}, u32[]{:S(2)}) copy-start(f32[256]{0:T(256)} %param.18) | copy-start | bytes 3076
  5.2 8.5 %copy-start.7 = (f32[256]{0:T(256)S(1)}, f32[256]{0:T(256)}, u32[]{:S(2)}) copy-start(f32[256]{0:T(256)} %param.14) | copy-start | bytes 3076
  6.0 21.5 %all-to-all-start = ((bf16[8,128,256]{2,1,0:T(8,128)(2,1)}), bf16[8,128,256]{2,1,0:T(8,128)(2,1)S(1)}, u32[]{:S(2)}, u32[]{:S(2)}) async-start(bf16[8,128,256]{2,1,0:T(8,128)(2,1)} %shard_map.145), calls=%async_computation | async-start | bytes 1048576 | tf_op jit(solution)/shard_map/all_to_all | solution.py:339
  16.2 0.7 %copy-start.10 = (bf16[512,256]{1,0:T(8,128)(2,1)}, bf16[512,256]{1,0:T(8,128)(2,1)S(1)}, u32[]{:S(2)}) copy-start(bf16[512,256]{1,0:T(8,128)(2,1)S(1)} %get-tuple-element.64.features) | copy-start | bytes 786436
  16.9 2.8 %copy-start.14 = (f32[8,512]{1,0:T(8,128)}, f32[8,512]{1,0:T(8,128)S(1)}, u32[]{:S(2)}) copy-start(f32[8,512]{1,0:T(8,128)S(1)} %get-tuple-element.58.target) | copy-start | bytes 49156
  16.9 2.8 %copy-start.12 = (f32[9,256]{1,0:T(8,128)}, f32[9,256]{1,0:T(8,128)S(1)}, u32[]{:S(2)}) copy-start(f32[9,256]{1,0:T(8,128)S(1)} %get-tuple-element.44.weights) | copy-start | bytes 27652
  16.9 2.8 %copy-start.16 = (f32[1,256]{1,0:T(1,128)}, f32[1,256]{1,0:T(1,128)S(1)}, u32[]{:S(2)}) copy-start(f32[1,256]{1,0:T(1,128)S(1)} %get-tuple-element.45.gain) | copy-start | bytes 3076
  22.7 0.8 %copy-start.8 = (f32[512,256]{1,0:T(8,128)}, f32[512,256]{1,0:T(8,128)S(1)}, u32[]{:S(2)}) copy-start(f32[512,256]{1,0:T(8,128)S(1)} %get-tuple-element.62.mixed) | copy-start | bytes 1572868
  27.5 1.9 %collective-permute-start.2 = (bf16[8,128,256]{2,1,0:T(8,128)(2,1)S(1)}, bf16[8,128,256]{2,1,0:T(8,128)(2,1)S(1)}, u32[]{:S(2)}, u32[]{:S(2)}) collective-permute-start(bf16[8,128,256]{2,1,0:T(8,128)(2,1)S(1)} %all-to-all-done.mine), channel_id=1, source_target_pairs={{0,1},{1,0},{2,3},{3,2},{4,5},{5,4},{6,7},{7,6},{8,9},{9,8},{10,11... | collective-permute-start | bytes 1572872 | tf_op jit(solution)/shard_map/ppermute | solution.py:310
  29.5 3.2 %copy-start.9 = (f32[512,256]{1,0:T(8,128)S(1)}, f32[512,256]{1,0:T(8,128)}, u32[]{:S(2)}) copy-start(f32[512,256]{1,0:T(8,128)} %copy-done.8) | copy-start | bytes 1572868
  29.5 3.2 %copy-start.11 = (bf16[512,256]{1,0:T(8,128)(2,1)S(1)}, bf16[512,256]{1,0:T(8,128)(2,1)}, u32[]{:S(2)}) copy-start(bf16[512,256]{1,0:T(8,128)(2,1)} %copy-done.10) | copy-start | bytes 786436
  29.5 3.2 %copy-start.15 = (f32[8,512]{1,0:T(8,128)S(1)}, f32[8,512]{1,0:T(8,128)}, u32[]{:S(2)}) copy-start(f32[8,512]{1,0:T(8,128)} %copy-done.14) | copy-start | bytes 49156
  29.5 3.2 %copy-start.17 = (f32[1,256]{1,0:T(1,128)S(1)}, f32[1,256]{1,0:T(1,128)}, u32[]{:S(2)}) copy-start(f32[1,256]{1,0:T(1,128)} %copy-done.16) | copy-start | bytes 3076
  31.5 1.2 %collective-permute-start.3 = (f32[8,512]{1,0:T(8,128)S(1)}, f32[8,512]{1,0:T(8,128)S(1)}, u32[]{:S(2)}, u32[]{:S(2)}) collective-permute-start(f32[8,512]{1,0:T(8,128)S(1)} %get-tuple-element.57.mine), channel_id=1, source_target_pairs={{0,1},{1,0},{2,3},{3,2},{4,5},{5,4},{6,7},{7,6},{8,9},{9,8},{10,11... | collective-permute-start | bytes 49160 | tf_op jit(solution)/shard_map/ppermute | solution.py:310
  35.2 2.3 %collective-permute-start.4 = (bf16[8,128,128]{2,1,0:T(8,128)(2,1)S(1)}, bf16[8,128,128]{2,1,0:T(8,128)(2,1)S(1)}, u32[]{:S(2)}, u32[]{:S(2)}) collective-permute-start(bf16[8,128,128]{2,1,0:T(8,128)(2,1)S(1)} %get-tuple-element.69), channel_id=1, source_target_pairs={{0,1},{1,0},{2,3},{3,2},{4,5},{5,4},{6,7},{7,6},{8,9},{9,8},{10,11... | collective-permute-start | bytes 786440 | tf_op jit(solution)/shard_map/ppermute | solution.py:310
  35.4 15.9 %collective-permute-start.6 = (bf16[512,256]{1,0:T(8,128)(2,1)S(1)}, bf16[512,256]{1,0:T(8,128)(2,1)S(1)}, u32[]{:S(2)}, u32[]{:S(2)}) collective-permute-start(bf16[512,256]{1,0:T(8,128)(2,1)S(1)} %get-tuple-element.71.own), channel_id=1, source_target_pairs={{0,2},{2,0},{4,6},{6,4},{8,10},{10,8},{12,14},{14,12},{1,3},{3,1},... | collective-permute-start | bytes 786440 | tf_op jit(solution)/shard_map/ppermute | solution.py:306
  36.8 16.6 %collective-permute-start.5 = (bf16[512,256]{1,0:T(8,128)(2,1)S(1)}, bf16[512,256]{1,0:T(8,128)(2,1)S(1)}, u32[]{:S(2)}, u32[]{:S(2)}) collective-permute-start(bf16[512,256]{1,0:T(8,128)(2,1)S(1)} %get-tuple-element.71.own), channel_id=1, source_target_pairs={{2,4},{6,8},{10,12},{4,2},{8,6},{12,10},{3,5},{7,9},{11,13},{5,3},... | collective-permute-start | bytes 786440 | tf_op jit(solution)/shard_map/ppermute | solution.py:306
  37.5 6.7 %copy-start.13 = (f32[9,256]{1,0:T(8,128)S(1)}, f32[9,256]{1,0:T(8,128)}, u32[]{:S(2)}) copy-start(f32[9,256]{1,0:T(8,128)} %copy-done.12) | copy-start | bytes 27652
  38.3 17.9 %all-to-all-start.1 = ((bf16[8,176,128]{2,1,0:T(8,128)(2,1)}), bf16[8,176,128]{2,1,0:T(8,128)(2,1)S(1)}, u32[]{:S(2)}, u32[]{:S(2)}) async-start(bf16[8,176,128]{2,1,0:T(8,128)(2,1)} %shard_map.151), calls=%async_computation.1 | async-start | bytes 720896 | tf_op jit(solution)/shard_map/all_to_all | solution.py:339
  56.3 1.4 %collective-permute-start.7 = (f32[176,128]{1,0:T(8,128)S(1)}, f32[176,128]{1,0:T(8,128)S(1)}, u32[]{:S(2)}, u32[]{:S(2)}) collective-permute-start(f32[176,128]{1,0:T(8,128)S(1)} %shard_map.155.ours), channel_id=1, source_target_pairs={{0,1},{1,0},{2,3},{3,2},{4,5},{5,4},{6,7},{7,6},{8,9},{9,8},{10,11... | collective-permute-start | bytes 270344 | tf_op jit(solution)/shard_map/ppermute | solution.py:310

commit v4 on v3

--- a/solution.py
+++ b/solution.py
@@ -60,9 +60,14 @@
 
 
 def tap_rows(places, source, tap):
-    column = lax.broadcasted_iota(jnp.int32, (places.shape[0], source.shape[0]), 1).astype(F32)
-    chosen = jnp.where(column == places[:, tap : tap + 1], 1.0, 0.0).astype(BF16)
-    return mul(chosen, source)
+    shape = (places.shape[0], 256)
+    column = lax.broadcasted_iota(jnp.int32, shape, 1).astype(F32).astype(BF16)
+    one, zero = jnp.ones((), BF16), jnp.zeros((), BF16)
+    chosen = []
+    for low_edge in range(0, source.shape[0], 256):
+        place = jnp.broadcast_to(places[:, tap : tap + 1] - float(low_edge), shape).astype(BF16)
+        chosen.append(jnp.where(column == place, one, zero))
+    return mul(jnp.concatenate(chosen, axis=1), source)
 
 
 def load(pairs, sems):
@@ -128,7 +133,7 @@
 
 def forward_kernel(
     info, normed, mine, other, bias, base, head, scale,
-    act_out, slope_out, forecast_out, up, down, reach,
+    act_out, slope_out, forecast_out, normed_t, up, down, reach,
 ):
     owners = mine.shape[0]
     half = mine.shape[1] // 2
@@ -141,11 +146,12 @@
     product = mul(jnp.concatenate([high, low], axis=0), down[...], NT)
     high, low = halves(product[:8] + product[8:])
     reach[...] = jnp.concatenate([high, low], axis=0)
-    forward(normed, up, reach, bias, base, act_out, slope_out, forecast_out)
-
-
-def forward(normed, up, reach, bias, base, act_out, slope_out, forecast_out):
+    forward(normed, up, reach, bias, base, act_out, slope_out, forecast_out, normed_t)
+
+
+def forward(normed, up, reach, bias, base, act_out, slope_out, forecast_out, normed_t):
     rows = normed[...]
+    normed_t[...] = turned(rows)
     total = base[...]
     for low_edge in range(0, up.shape[0], 256):
         piece = slice(low_edge, low_edge + 256)
@@ -185,11 +191,26 @@
     ).astype(BF16)
 
 
+def back_kernel(
+    info, mine, other, target, reach, slope, up, mixed, gain, normed_t,
+    mixed_grad, grad, send, pre_grad, loss, kept,
+):
+    backward_kernel(
+        mine, other, target, reach, slope, up, mixed, gain, mixed_grad, pre_grad, grad, loss
+    )
+    first = info[2] == 0
+    lower, higher = normed_t[:LANES, :], normed_t[LANES:, :]
+    kept[...] = jnp.where(first, lower, higher)
+    rows = jnp.where(first, higher, lower)
+    for block in range(send.shape[0]):
+        lanes = slice(block * LANES, (block + 1) * LANES)
+        send[block] = mul(rows, pre_grad[:, lanes]).astype(BF16)
+
+
 def weights_kernel(
-    info, pre_grad, normed, act, grad, features, down, scale, taken, mixed_grad, loss,
-    keep, send, small,
-):
-    normed_t = turned(normed[...])
+    pre_grad, kept, act, grad, features, down, scale, taken, mixed_grad, loss, came, joined
+):
+    rows = kept[...]
     summed = mul(grad[...], act[...])
     high, low = halves(summed)
     through = mul(jnp.concatenate([high, low], axis=0), down[...])
@@ -200,36 +221,13 @@
         for k in range(taken.shape[0])
     ]
     depth.insert(CENTRE, jnp.sum(features[...].astype(F32) * flow, axis=0, keepdims=True))
-    small[...] = jnp.concatenate([head_part] + depth + [loss[...]], axis=0)
-    first = info[2] == 0
-    for block in range(keep.shape[0]):
+    small = jnp.concatenate([head_part] + depth + [loss[...]], axis=0)
+    for block in range(joined.shape[0]):
         lanes = slice(block * LANES, (block + 1) * LANES)
-        up_part = mul(normed_t, pre_grad[:, lanes])
-        lower, higher = up_part[:LANES], up_part[LANES:]
-        keep[block, :LANES, :] = jnp.where(first, lower, higher).astype(BF16)
-        send[block, :, :] = jnp.where(first, higher, lower).astype(BF16)
+        main = mul(rows, pre_grad[:, lanes]) + came[block].astype(F32)
+        joined[block, :LANES, :] = main.astype(BF16)
         extra = [small[:, :LANES], small[:, LANES:], summed[:, lanes], jnp.zeros((4, LANES), F32)]
-        keep[block, LANES:, :] = jnp.concatenate(extra, axis=0).astype(BF16)
-
-
-def back_kernel(
-    info, mine, other, target, reach, slope, up, mixed, gain, normed, act, features, down, scale, taken,
-    mixed_grad, grad, keep, send, pre_grad, loss, small,
-):
-    backward_kernel(
-        mine, other, target, reach, slope, up, mixed, gain, mixed_grad, pre_grad, grad, loss
-    )
-    weights_kernel(
-        info, pre_grad, normed, act, grad, features, down, scale, taken, mixed_grad, loss,
-        keep, send, small,
-    )
-
-
-def join_kernel(keep, came, joined):
-    for block in range(keep.shape[0]):
-        main = keep[block, :LANES, :].astype(F32) + came[block].astype(F32)
-        joined[block, :LANES, :] = main.astype(BF16)
-        joined[block, LANES:, :] = keep[block, LANES:, :]
+        joined[block, LANES:, :] = jnp.concatenate(extra, axis=0).astype(BF16)
 
 
 def sum_kernel(parts, total):
@@ -385,34 +383,38 @@
         aliases={5: 0, 6: 1},
         flops=NEAR,
     )
-    outs = [((pixels, hidden), BF16), ((pixels, hidden), F32), ((8, pixels), F32)]
+    outs = [
+        ((pixels, hidden), BF16), ((pixels, hidden), F32), ((8, pixels), F32), ((channels, pixels), BF16)
+    ]
     if by_blocks:
         mine, normed = lax.optimization_barrier((mine, normed))
         other = swap(mine)
         whole = ((hidden, channels), BF16)
-        act, slope, forecast, up, down, reach = call(
+        act, slope, forecast, normed_t, up, down, reach = call(
             forward_kernel,
             outs + [whole, whole, ((16, hidden), BF16)],
             1,
             info, normed, mine, other, bias, base, head, scale,
         )
     else:
-        act, slope, forecast = call(forward, outs, 0, normed, up, reach, bias, base)
+        act, slope, forecast, normed_t = call(forward, outs, 0, normed, up, reach, bias, base)
     blocks = hidden // LANES
     full = ((blocks, LANES + EXTRA, LANES), BF16)
-    mixed_grad, grad, keep, send = call(
+    mixed_grad, grad, send, pre_grad, loss, kept = call(
         back_kernel,
-        [(tile, BF16), ((8, pixels), BF16), full, ((blocks, LANES, LANES), BF16)],
+        [(tile, BF16), ((8, pixels), BF16), ((blocks, LANES, LANES), BF16),
+         ((pixels, hidden), BF16), ((1, channels), F32), ((LANES, pixels), BF16)],
         1,
-        info, forecast, swap(forecast), target, reach, slope, up, mixed, gain,
-        normed, act, own, down, scale, taken,
-        scratch=[pltpu.VMEM((pixels, hidden), BF16), pltpu.VMEM((1, channels), F32),
-                 pltpu.VMEM((18, channels), F32)],
-        flops=NEAR,
+        info, forecast, swap(forecast), target, reach, slope, up, mixed, gain, normed_t,
     )
     came = swap(send)
     grad_pair, grad_side = pair_tiles(mixed_grad)
-    (joined,) = call(join_kernel, [full], 0, keep, came)
+    (joined,) = call(
+        weights_kernel,
+        [full],
+        0,
+        pre_grad, kept, act, grad, own, down, scale, taken, mixed_grad, loss, came,
+    )
     source, joined = lax.optimization_barrier((mixed_grad, joined))
     (partial,) = call(
         input_own_kernel, [(tile, F32)], 1, info, source, places, weights, grad, head, flops=OWN
@@ -453,11 +455,11 @@
     main = jnp.where(member == 0, main, main[::-1])
     rows = jnp.transpose(main, (1, 3, 0, 2)).reshape(hidden, channels)
     up_grad = lax.psum_scatter(rows, "pix", scatter_dimension=0, tiled=True)
-    summed = keep[:, LANES + 36 : LANES + 44].astype(F32)
+    summed = joined[:, LANES + 36 : LANES + 44].astype(F32)
     summed = jnp.transpose(summed + swap(summed), (0, 2, 1)).reshape(hidden, 8)
     summed = lax.psum_scatter(summed, "pix", scatter_dimension=0, tiled=True)
     down_grad = layer_scale * jnp.dot(summed, head_matrix.astype(F32), precision=exact)
-    small = keep[0, LANES : LANES + 36].astype(F32).reshape(2, 18, LANES)
+    small = joined[0, LANES : LANES + 36].astype(F32).reshape(2, 18, LANES)
     small = jnp.transpose(small, (1, 0, 2)).reshape(18, channels)
     small = lax.psum(small, ("pix", "mem"))
     return (

time: 59.7 us -> 59 us (0.988)
  Pallas kernels: 22.9 us -> 22.1 us
    pallas_call x12, Pallas kernels: 22.9 us -> 22.1 us  [call(): pl.pallas_call(kernel, out_shape=tuple((jax.ShapeDtypeStruct(shape, dtype...]
    all_to_all x2, waiting for transfers between devices: 4 us -> 4.69 us  [everywhere(): return lax.all_to_all(array, 'pix', split_axis=0, concat_axis=0)]
    unnamed x36 -> x32, local copies, waits for them, and re-layouts: 1.58 us -> 1.57 us
  transfers between devices with their start and end apart: 10 -> 10, of which waited for: 5 -> 5; matrix products, arithmetic and copies ran while one was open for 1% -> 1% of each run, Pallas kernels for 28% -> 29%
where the time goes in v4:
time: 59 us; the launch traced here: 58.6 us
  Pallas kernels  22.1 us (37%)
  starting transfers between devices  19.3 us (33%)
  waiting for transfers between devices  13.6 us (23%)
  local copies, waits for them, and re-layouts  1.57 us (3%)
  between operations  1.07 us (2%)
  other arithmetic  0.86 us (1%)
    pallas_call x12, Pallas kernels, call(): pl.pallas_call(kernel, out_shape=tuple((jax.ShapeDtypeStruct(shape, dtype...  22.1 us
    all_to_all x2, starting transfers between devices, everywhere(): return lax.all_to_all(array, 'pix', split_axis=0, concat_axis=0)  13.1 us
    ppermute x2, waiting for transfers between devices, pair_tiles(): lax.ppermute(array, 'pix', inner)  4.7 us
    all_to_all x2, waiting for transfers between devices, everywhere(): return lax.all_to_all(array, 'pix', split_axis=0, concat_axis=0)  4.69 us
    ppermute x2, starting transfers between devices, pair_tiles(): lax.ppermute(array, 'pix', inner)  4.42 us
    ppermute x4, waiting for transfers between devices, swap(): return lax.ppermute(array, 'mem', [(0, 1), (1, 0)])  4.23 us
    unnamed x32, local copies, waits for them, and re-layouts  1.57 us
    ppermute x2, starting transfers between devices, pair_tiles(): lax.ppermute(array, 'pix', outer)  1.33 us
  transfers between devices with their start and end apart: 10, of which 5 were waited for; matrix products, arithmetic and copies ran while one was open for 1% of the time, Pallas kernels for 29%

profile of v4, /device:TPU:0, one launch (start us, length us, event | category | flops | bytes accessed | tf_op | source)
XLA Modules:
  0.0 58.6 jit_solution(18420852732657426559)
XLA Ops:
  0.6 3.0 %collective-permute-start.1 = (bf16[512,256]{1,0:T(8,128)(2,1)}, bf16[512,256]{1,0:T(8,128)(2,1)S(1)}, u32[]{:S(2)}, u32[]{:S(2)}) collective-permute-start(bf16[512,256]{1,0:T(8,128)(2,1)} %bitcast.12), channel_id=1, source_target_pairs={{0,2},{2,0},{4,6},{6,4},{8,10},{10,8},{12,14},{14,12},{1,3},{3,1},... | collective-permute-start | bytes 786440 | tf_op jit(solution)/shard_map/ppermute | solution.py:304
  3.6 0.7 %collective-permute-start = (bf16[512,256]{1,0:T(8,128)(2,1)}, bf16[512,256]{1,0:T(8,128)(2,1)S(1)}, u32[]{:S(2)}, u32[]{:S(2)}) collective-permute-start(bf16[512,256]{1,0:T(8,128)(2,1)} %bitcast.13), channel_id=1, source_target_pairs={{2,4},{6,8},{10,12},{4,2},{8,6},{12,10},{3,5},{7,9},{11,13},{5,3},... | collective-permute-start | bytes 786440 | tf_op jit(solution)/shard_map/ppermute | solution.py:304
  4.3 0.8 %fusion = bf16[2,64,256]{2,1,0:T(8,128)(2,1)S(1)} fusion(s32[]{:T(128)S(6)} %select_n.11, bf16[1,128,256]{2,1,0:T(8,128)(2,1)} %bitcast.18, bf16[1,128,256]{2,1,0:T(8,128)(2,1)} %bitcast.19), kind=kLoop, calls=%fused_computation.2 | loop fusion | flops 131072 | bytes 196612 | tf_op jit(solution)/shard_map/stack | solution.py:342
  5.1 0.0 copy-start
  5.1 0.0 copy-start.1
  5.1 0.0 copy-start.2
  5.1 0.0 copy-start.3
  5.1 0.0 copy-start.4
  5.1 0.0 copy-start.5
  5.2 0.0 copy-start.6
  5.2 0.0 copy-start.7
  5.2 0.8 %shard_map.145 = bf16[8,128,256]{2,1,0:T(8,128)(2,1)} custom-call(bf16[128,256]{1,0:T(8,128)(2,1)S(1)} %bitcast.11), custom_call_target="tpu_custom_call" | custom-call | flops 8000000000 | tf_op jit(solution)/shard_map/pallas_call | solution.py:287
  6.0 7.6 %all-to-all-start = ((bf16[8,128,256]{2,1,0:T(8,128)(2,1)}), bf16[8,128,256]{2,1,0:T(8,128)(2,1)S(1)}, u32[]{:S(2)}, u32[]{:S(2)}) async-start(bf16[8,128,256]{2,1,0:T(8,128)(2,1)} %shard_map.145), calls=%async_computation | async-start | bytes 1048576 | tf_op jit(solution)/shard_map/all_to_all | solution.py:337
  13.6 0.1 pad_add_fusion.info
  13.7 0.0 copy-done
  13.7 0.0 copy-done.1
  13.7 0.0 copy-done.2
  13.7 0.0 copy-done.3
  13.7 0.0 copy-done.4
  13.7 0.0 copy-done.5
  13.7 0.0 copy-done.6
  13.7 0.0 copy-done.7
  13.7 2.3 %shard_map.146 = (bf16[512,256]{1,0:T(8,128)(2,1)S(1)}, f32[9,256]{1,0:T(8,128)S(1)}, bf16[8,256]{1,0:T(8,128)(2,1)S(1)}, f32[1,256]{1,0:T(1,128)S(1)}, f32[1,25...) custom-call(s32[3]{0:T(128)S(1)} %pad_add_fusion.info, ...), custom_call_target="tpu_custom_call" | custom-call | flops 8000000000 | tf_op jit(solution)/shard_map/pallas_call | solution.py:287
  16.0 0.0 copy-start.8
  16.0 0.7 %copy-done.8 = bf16[512,256]{1,0:T(8,128)(2,1)} copy-done((bf16[512,256]{1,0:T(8,128)(2,1)}, bf16[512,256]{1,0:T(8,128)(2,1)S(1)}, u32[]{:S(2)}) %copy-start.8) | copy-done | bytes 262168
  16.7 0.0 copy-start.12
  16.7 0.0 copy-start.14
  16.7 0.0 collective-permute-done.1.tile
  16.7 2.6 %shard_map.147 = (bf16[8,512,256]{2,1,0:T(8,128)(2,1)S(1)}, f32[512,256]{1,0:T(8,128)S(1)}) custom-call(s32[3]{0:T(128)S(1)} %pad_add_fusion.info, bf16[512,256]{1,0:T(8,128)(2,1)S(1)} %collective-permute-done.1.tile, s32[9,512]{1,0:T(8,128)S(1)} %get-tuple-element.46.neighbours, ...), custom_call_target="tpu_custom_call", output_to_operand_aliasing={{0}: (4, {}), {1}: (5, {})} | custom-call | flops 49999998976 | tf_op jit(solution)/shard_map/pallas_call | solution.py:287
  19.3 0.0 collective-permute-done.tile
  19.3 0.0 copy-done.12
  19.3 0.0 copy-done.14
  19.3 2.7 %shard_map.148 = (bf16[8,512,256]{2,1,0:T(8,128)(2,1)S(1)}, f32[512,256]{1,0:T(8,128)S(1)}, bf16[512,256]{1,0:T(8,128)(2,1)S(1)}) custom-call(s32[3]{0:T(128)S(1)} %pad_add_fusion.info, bf16[512,256]{1,0:T(8,128)(2,1)S(1)} %collective-permute-done.tile, s32[9,512]{1,0:T(8,128)S(1)} %get-tuple-element.46.neighbours, ...), custom_call_target="tpu_custom_call", output_to_operand_aliasing={{0}: (5, {}), {1}: (6, {})} | custom-call | flops 49999998976 | tf_op jit(solution)/shard_map/pallas_call | solution.py:287
  22.1 0.0 copy-start.10
  22.1 0.8 %copy-done.10 = f32[512,256]{1,0:T(8,128)} copy-done((f32[512,256]{1,0:T(8,128)}, f32[512,256]{1,0:T(8,128)S(1)}, u32[]{:S(2)}) %copy-start.10) | copy-done | bytes 524312
  22.9 4.7 %all-to-all-done.mine = bf16[8,128,256]{2,1,0:T(8,128)(2,1)S(1)} async-done(((bf16[8,128,256]{2,1,0:T(8,128)(2,1)}), bf16[8,128,256]{2,1,0:T(8,128)(2,1)S(1)}, u32[]{:S(2)}, u32[]{:S(2)}) %all-to-all-start) | async-done | bytes 524320 | tf_op jit(solution)/shard_map/all_to_all | solution.py:337
  27.5 0.0 collective-permute-start.2
  27.6 1.9 %collective-permute-done.2.other = bf16[8,128,256]{2,1,0:T(8,128)(2,1)S(1)} collective-permute-done((bf16[8,128,256]{2,1,0:T(8,128)(2,1)S(1)}, bf16[8,128,256]{2,1,0:T(8,128)(2,1)S(1)}, u32[]{:S(2)}, u32[]{:S(2)}) %collective-permute-start.2) | collective-permute-done | bytes 524320 | tf_op jit(solution)/shard_map/ppermute | solution.py:308
  29.5 0.0 copy-start.11
  29.5 2.0 %shard_map.149 = (bf16[512,1024]{1,0:T(8,128)(2,1)S(1)}, f32[512,1024]{1,0:T(8,128)S(1)}, f32[8,512]{1,0:T(8,128)S(1)}, bf16[256,512]{1,0:T(8,128)(2,1)S(1)}, bf...) custom-call(s32[3]{0:T(128)S(1)} %pad_add_fusion.info, ...), custom_call_target="tpu_custom_call" | custom-call | flops 2000000000 | tf_op jit(solution)/shard_map/pallas_call | solution.py:287
  31.5 0.2 collective-permute-start.3
  31.7 1.0 %collective-permute-done.3.other = f32[8,512]{1,0:T(8,128)S(1)} collective-permute-done((f32[8,512]{1,0:T(8,128)S(1)}, f32[8,512]{1,0:T(8,128)S(1)}, u32[]{:S(2)}, u32[]{:S(2)}) %collective-permute-start.3) | collective-permute-done | bytes 16416 | tf_op jit(solution)/shard_map/ppermute | solution.py:308
  32.7 0.0 copy-done.11
  32.7 1.8 %shard_map.150 = (bf16[512,256]{1,0:T(8,128)(2,1)S(1)}, bf16[8,512]{1,0:T(8,128)(2,1)S(1)}, bf16[8,128,128]{2,1,0:T(8,128)(2,1)S(1)}, bf16[512,1024]{1,0:T(8,128...) custom-call(s32[3]{0:T(128)S(1)} %pad_add_fusion.info, f32[8,512]{1,0:T(8,128)S(1)} %get-tuple-element.60.mine, ...), custom_call_target="tpu_custom_call" | custom-call | flops 2000000000 | tf_op jit(solution)/shard_map/pallas_call | solution.py:287
  34.5 0.2 collective-permute-start.4
  34.7 1.4 %collective-permute-start.6 = (bf16[512,256]{1,0:T(8,128)(2,1)S(1)}, bf16[512,256]{1,0:T(8,128)(2,1)S(1)}, u32[]{:S(2)}, u32[]{:S(2)}) collective-permute-start(bf16[512,256]{1,0:T(8,128)(2,1)S(1)} %get-tuple-element.78.mixed_grad.own), channel_id=1, source_target_pairs={{0,2},{2,0},{4,6},{6,4},{8,10},{10,8},{12,14},{14,12},{1,3},{3,1},... | collective-permute-start | bytes 786440 | tf_op jit(solution)/shard_map/ppermute | solution.py:304
  36.2 0.7 %collective-permute-start.5 = (bf16[512,256]{1,0:T(8,128)(2,1)S(1)}, bf16[512,256]{1,0:T(8,128)(2,1)S(1)}, u32[]{:S(2)}, u32[]{:S(2)}) collective-permute-start(bf16[512,256]{1,0:T(8,128)(2,1)S(1)} %get-tuple-element.78.mixed_grad.own), channel_id=1, source_target_pairs={{2,4},{6,8},{10,12},{4,2},{8,6},{12,10},{3,5},{7,9},{11,13},{5,3},... | collective-permute-start | bytes 786440 | tf_op jit(solution)/shard_map/ppermute | solution.py:304
  36.8 0.0 collective-permute-done.4.came
  36.9 0.0 copy-done.9
  36.9 0.0 copy-start.13
  36.9 0.0 copy-start.15
  36.9 1.5 %shard_map.151 = bf16[8,176,128]{2,1,0:T(8,128)(2,1)} custom-call(bf16[512,1024]{1,0:T(8,128)(2,1)S(1)} %get-tuple-element.68.pre_grad, bf16[128,512]{1,0:T(8,128)(2,1)S(1)} %get-tuple-element.69.kept, bf16[512,1024]{1,0:T(8,128)(2,1)S(1)} %get-tuple-element.70.act, bf16[8,512]{1,0:T(8,128)(2,1)S(1)} %get-tuple-element.71.grad, ...), custom_call_target="tpu_custom_call" | custom-call | flops 2000000000 | tf_op jit(solution)/shard_map/pallas_call | solution.py:287
  38.4 5.5 %all-to-all-start.1 = ((bf16[8,176,128]{2,1,0:T(8,128)(2,1)}), bf16[8,176,128]{2,1,0:T(8,128)(2,1)S(1)}, u32[]{:S(2)}, u32[]{:S(2)}) async-start(bf16[8,176,128]{2,1,0:T(8,128)(2,1)} %shard_map.151), calls=%async_computation.1 | async-start | bytes 720896 | tf_op jit(solution)/shard_map/all_to_all | solution.py:337
  43.9 0.0 copy-done.13
  43.9 0.0 copy-done.15
  43.9 2.1 %shard_map.152.partial = f32[512,256]{1,0:T(8,128)S(1)} custom-call(s32[3]{0:T(128)S(1)} %pad_add_fusion.info, bf16[512,256]{1,0:T(8,128)(2,1)S(1)} %get-tuple-element.78.mixed_grad.own, s32[9,512]{1,0:T(8,128)S(1)} %copy-done.13, f32[9,256]{1,0:T(8,128)S(1)} %copy-done.15, bf16[8,512]{1,0:T(8,128)(2,1)S(1)} %get-tuple-element.71.grad, ...), custom_call_target="tpu_custom_call" | custom-call | flops 8000000000 | tf_op jit(solution)/shard_map/pallas_call | solution.py:287
  46.0 4.7 %collective-permute-done.6.tile = bf16[512,256]{1,0:T(8,128)(2,1)S(1)} collective-permute-done((bf16[512,256]{1,0:T(8,128)(2,1)S(1)}, bf16[512,256]{1,0:T(8,128)(2,1)S(1)}, u32[]{:S(2)}, u32[]{:S(2)}) %collective-permute-start.6) | collective-permute-done | bytes 262176 | tf_op jit(solution)/shard_map/ppermute | solution.py:304
  50.7 2.1 %shard_map.153.partial = f32[512,256]{1,0:T(8,128)S(1)} custom-call(s32[3]{0:T(128)S(1)} %pad_add_fusion.info, bf16[512,256]{1,0:T(8,128)(2,1)S(1)} %collective-permute-done.6.tile, s32[9,512]{1,0:T(8,128)S(1)} %copy-done.13, f32[9,256]{1,0:T(8,128)S(1)} %copy-done.15, f32[512,256]{1,0:T(8,128)S(1)} %shard_map.152.partial), custom_call_target="tpu_custom_call" | custom-call | flops 49999998976 | tf_op jit(solution)/shard_map/pallas_call | solution.py:287
  52.8 0.0 collective-permute-done.5.tile
  52.8 2.8 %shard_map.154 = bf16[512,256]{1,0:T(8,128)(2,1)} custom-call(s32[3]{0:T(128)S(1)} %pad_add_fusion.info, bf16[512,256]{1,0:T(8,128)(2,1)S(1)} %collective-permute-done.5.tile, s32[9,512]{1,0:T(8,128)S(1)} %copy-done.13, f32[9,256]{1,0:T(8,128)S(1)} %copy-done.15, f32[512,256]{1,0:T(8,128)S(1)} %shard_map.153.partial), custom_call_target="tpu_custom_call" | custom-call | flops 49999998976 | tf_op jit(solution)/shard_map/pallas_call | solution.py:287
  55.6 0.0 all-to-all-done.1.parts
  55.6 0.1 collective-permute-start.7
  55.7 1.3 %collective-permute-done.7.theirs = f32[176,128]{1,0:T(8,128)S(1)} collective-permute-done((f32[176,128]{1,0:T(8,128)S(1)}, f32[176,128]{1,0:T(8,128)S(1)}, u32[]{:S(2)}, u32[]{:S(2)}) %collective-permute-start.7) | collective-permute-done | bytes 90144 | tf_op jit(solution)/shard_map/ppermute | solution.py:308
  57.0 1.4 %shard_map.156 = (f32[1]{0:T(128)}, f32[128,256]{1,0:T(8,128)}, f32[128,256]{1,0:T(8,128)}, f32[9,256]{1,0:T(8,128)}, f32[8,256]{1,0:T(8,128)}) custom-call(s32[3]{0:T(128)S(1)} %pad_add_fusion.info, f32[176,128]{1,0:T(8,128)S(1)} %shard_map.155.ours, f32[176,128]{1,0:T(8,128)S(1)} %collective-permute-done.7.theirs, ...), custom_call_target="tpu_custom_call" | custom-call | flops 2000000000 | tf_op jit(solution)/shard_map/pallas_call | solution.py:287
  (2 shorter events, 0.1 us)
Async XLA Ops:
  0.6 16.1 %collective-permute-start.1 = (bf16[512,256]{1,0:T(8,128)(2,1)}, bf16[512,256]{1,0:T(8,128)(2,1)S(1)}, u32[]{:S(2)}, u32[]{:S(2)}) collective-permute-start(bf16[512,256]{1,0:T(8,128)(2,1)} %bitcast.12), channel_id=1, source_target_pairs={{0,2},{2,0},{4,6},{6,4},{8,10},{10,8},{12,14},{14,12},{1,3},{3,1},... | collective-permute-start | bytes 786440 | tf_op jit(solution)/shard_map/ppermute | solution.py:304
  3.6 15.7 %collective-permute-start = (bf16[512,256]{1,0:T(8,128)(2,1)}, bf16[512,256]{1,0:T(8,128)(2,1)S(1)}, u32[]{:S(2)}, u32[]{:S(2)}) collective-permute-start(bf16[512,256]{1,0:T(8,128)(2,1)} %bitcast.13), channel_id=1, source_target_pairs={{2,4},{6,8},{10,12},{4,2},{8,6},{12,10},{3,5},{7,9},{11,13},{5,3},... | collective-permute-start | bytes 786440 | tf_op jit(solution)/shard_map/ppermute | solution.py:304
  5.1 8.6 %copy-start = (bf16[1,512,256]{2,1,0:T(8,128)(2,1)S(1)}, bf16[1,512,256]{2,1,0:T(8,128)(2,1)}, u32[]{:S(2)}) copy-start(bf16[1,512,256]{2,1,0:T(8,128)(2,1)} %param.10) | copy-start | bytes 786436
  5.1 8.6 %copy-start.1 = (s32[9,512]{1,0:T(8,128)S(1)}, s32[9,512]{1,0:T(8,128)}, u32[]{:S(2)}) copy-start(s32[9,512]{1,0:T(8,128)} %neighbours_hbm.1) | copy-start | bytes 55300
  5.1 8.6 %copy-start.2 = (f32[9,256]{1,0:T(8,128)S(1)}, f32[9,256]{1,0:T(8,128)}, u32[]{:S(2)}) copy-start(f32[9,256]{1,0:T(8,128)} %weights_hbm.1) | copy-start | bytes 27652
  5.1 8.5 %copy-start.3 = (f32[8,512]{1,0:T(8,128)S(1)}, f32[8,512]{1,0:T(8,128)}, u32[]{:S(2)}) copy-start(f32[8,512]{1,0:T(8,128)} %target_hbm.1) | copy-start | bytes 49156
  5.1 8.5 %copy-start.4 = (bf16[8,256]{1,0:T(8,128)(2,1)S(1)}, bf16[8,256]{1,0:T(8,128)(2,1)}, u32[]{:S(2)}) copy-start(bf16[8,256]{1,0:T(8,128)(2,1)} %head_hbm.1) | copy-start | bytes 12292
  5.1 8.5 %copy-start.5 = (f32[1024]{0:T(1024)S(1)}, f32[1024]{0:T(1024)}, u32[]{:S(2)}) copy-start(f32[1024]{0:T(1024)} %param.16) | copy-start | bytes 12292
  5.2 8.5 %copy-start.6 = (f32[256]{0:T(256)S(1)}, f32[256]{0:T(256)}, u32[]{:S(2)}) copy-start(f32[256]{0:T(256)} %param.18) | copy-start | bytes 3076
  5.2 8.5 %copy-start.7 = (f32[256]{0:T(256)S(1)}, f32[256]{0:T(256)}, u32[]{:S(2)}) copy-start(f32[256]{0:T(256)} %param.14) | copy-start | bytes 3076
  6.0 21.5 %all-to-all-start = ((bf16[8,128,256]{2,1,0:T(8,128)(2,1)}), bf16[8,128,256]{2,1,0:T(8,128)(2,1)S(1)}, u32[]{:S(2)}, u32[]{:S(2)}) async-start(bf16[8,128,256]{2,1,0:T(8,128)(2,1)} %shard_map.145), calls=%async_computation | async-start | bytes 1048576 | tf_op jit(solution)/shard_map/all_to_all | solution.py:337
  16.0 0.7 %copy-start.8 = (bf16[512,256]{1,0:T(8,128)(2,1)}, bf16[512,256]{1,0:T(8,128)(2,1)S(1)}, u32[]{:S(2)}) copy-start(bf16[512,256]{1,0:T(8,128)(2,1)S(1)} %get-tuple-element.72.features) | copy-start | bytes 786436
  16.7 2.6 %copy-start.12 = (s32[9,512]{1,0:T(8,128)}, s32[9,512]{1,0:T(8,128)S(1)}, u32[]{:S(2)}) copy-start(s32[9,512]{1,0:T(8,128)S(1)} %get-tuple-element.46.neighbours) | copy-start | bytes 55300
  16.7 2.6 %copy-start.14 = (f32[9,256]{1,0:T(8,128)}, f32[9,256]{1,0:T(8,128)S(1)}, u32[]{:S(2)}) copy-start(f32[9,256]{1,0:T(8,128)S(1)} %get-tuple-element.47.weights) | copy-start | bytes 27652
  22.1 0.8 %copy-start.10 = (f32[512,256]{1,0:T(8,128)}, f32[512,256]{1,0:T(8,128)S(1)}, u32[]{:S(2)}) copy-start(f32[512,256]{1,0:T(8,128)S(1)} %get-tuple-element.65.mixed) | copy-start | bytes 1572868
  27.5 1.9 %collective-permute-start.2 = (bf16[8,128,256]{2,1,0:T(8,128)(2,1)S(1)}, bf16[8,128,256]{2,1,0:T(8,128)(2,1)S(1)}, u32[]{:S(2)}, u32[]{:S(2)}) collective-permute-start(bf16[8,128,256]{2,1,0:T(8,128)(2,1)S(1)} %all-to-all-done.mine), channel_id=1, source_target_pairs={{0,1},{1,0},{2,3},{3,2},{4,5},{5,4},{6,7},{7,6},{8,9},{9,8},{10,11... | collective-permute-start | bytes 1572872 | tf_op jit(solution)/shard_map/ppermute | solution.py:308
  29.5 3.3 %copy-start.11 = (f32[512,256]{1,0:T(8,128)S(1)}, f32[512,256]{1,0:T(8,128)}, u32[]{:S(2)}) copy-start(f32[512,256]{1,0:T(8,128)} %copy-done.10) | copy-start | bytes 1572868
  31.5 1.2 %collective-permute-start.3 = (f32[8,512]{1,0:T(8,128)S(1)}, f32[8,512]{1,0:T(8,128)S(1)}, u32[]{:S(2)}, u32[]{:S(2)}) collective-permute-start(f32[8,512]{1,0:T(8,128)S(1)} %get-tuple-element.60.mine), channel_id=1, source_target_pairs={{0,1},{1,0},{2,3},{3,2},{4,5},{5,4},{6,7},{7,6},{8,9},{9,8},{10,11... | collective-permute-start | bytes 49160 | tf_op jit(solution)/shard_map/ppermute | solution.py:308
  32.7 4.1 %copy-start.9 = (bf16[512,256]{1,0:T(8,128)(2,1)S(1)}, bf16[512,256]{1,0:T(8,128)(2,1)}, u32[]{:S(2)}) copy-start(bf16[512,256]{1,0:T(8,128)(2,1)} %copy-done.8) | copy-start | bytes 786436
  34.5 2.3 %collective-permute-start.4 = (bf16[8,128,128]{2,1,0:T(8,128)(2,1)S(1)}, bf16[8,128,128]{2,1,0:T(8,128)(2,1)S(1)}, u32[]{:S(2)}, u32[]{:S(2)}) collective-permute-start(bf16[8,128,128]{2,1,0:T(8,128)(2,1)S(1)} %get-tuple-element.76), channel_id=1, source_target_pairs={{0,1},{1,0},{2,3},{3,2},{4,5},{5,4},{6,7},{7,6},{8,9},{9,8},{10,11... | collective-permute-start | bytes 786440 | tf_op jit(solution)/shard_map/ppermute | solution.py:308
  34.7 15.9 %collective-permute-start.6 = (bf16[512,256]{1,0:T(8,128)(2,1)S(1)}, bf16[512,256]{1,0:T(8,128)(2,1)S(1)}, u32[]{:S(2)}, u32[]{:S(2)}) collective-permute-start(bf16[512,256]{1,0:T(8,128)(2,1)S(1)} %get-tuple-element.78.mixed_grad.own), channel_id=1, source_target_pairs={{0,2},{2,0},{4,6},{6,4},{8,10},{10,8},{12,14},{14,12},{1,3},{3,1},... | collective-permute-start | bytes 786440 | tf_op jit(solution)/shard_map/ppermute | solution.py:304
  36.2 16.6 %collective-permute-start.5 = (bf16[512,256]{1,0:T(8,128)(2,1)S(1)}, bf16[512,256]{1,0:T(8,128)(2,1)S(1)}, u32[]{:S(2)}, u32[]{:S(2)}) collective-permute-start(bf16[512,256]{1,0:T(8,128)(2,1)S(1)} %get-tuple-element.78.mixed_grad.own), channel_id=1, source_target_pairs={{2,4},{6,8},{10,12},{4,2},{8,6},{12,10},{3,5},{7,9},{11,13},{5,3},... | collective-permute-start | bytes 786440 | tf_op jit(solution)/shard_map/ppermute | solution.py:304
  36.9 7.0 %copy-start.13 = (s32[9,512]{1,0:T(8,128)S(1)}, s32[9,512]{1,0:T(8,128)}, u32[]{:S(2)}) copy-start(s32[9,512]{1,0:T(8,128)} %copy-done.12) | copy-start | bytes 55300
  36.9 7.0 %copy-start.15 = (f32[9,256]{1,0:T(8,128)S(1)}, f32[9,256]{1,0:T(8,128)}, u32[]{:S(2)}) copy-start(f32[9,256]{1,0:T(8,128)} %copy-done.14) | copy-start | bytes 27652
  38.4 17.2 %all-to-all-start.1 = ((bf16[8,176,128]{2,1,0:T(8,128)(2,1)}), bf16[8,176,128]{2,1,0:T(8,128)(2,1)S(1)}, u32[]{:S(2)}, u32[]{:S(2)}) async-start(bf16[8,176,128]{2,1,0:T(8,128)(2,1)} %shard_map.151), calls=%async_computation.1 | async-start | bytes 720896 | tf_op jit(solution)/shard_map/all_to_all | solution.py:337
  55.6 1.4 %collective-permute-start.7 = (f32[176,128]{1,0:T(8,128)S(1)}, f32[176,128]{1,0:T(8,128)S(1)}, u32[]{:S(2)}, u32[]{:S(2)}) collective-permute-start(f32[176,128]{1,0:T(8,128)S(1)} %shard_map.155.ours), channel_id=1, source_target_pairs={{0,1},{1,0},{2,3},{3,2},{4,5},{5,4},{6,7},{7,6},{8,9},{9,8},{10,11... | collective-permute-start | bytes 270344 | tf_op jit(solution)/shard_map/ppermute | solution.py:308

commit v5 on v4

--- a/solution.py
+++ b/solution.py
@@ -83,16 +83,50 @@
         out[owner] = rows[...]
 
 
+def by_owner(split, first, mine, other):
+    if not split:
+        return mine + other
+    blocks = []
+    for a, b in zip(mine, other):
+        low, high = jnp.where(first, a, b), jnp.where(first, b, a)
+        left = lax.broadcasted_iota(jnp.int32, a.shape, 1) < LANES // 2
+        blocks.append(jnp.where(left, low, pltpu.roll(high, LANES // 2, 1)))
+        blocks.append(jnp.where(left, pltpu.roll(low, LANES // 2, 1), high))
+    return blocks
+
+
+def by_half(split, first, blocks):
+    if not split:
+        middle = len(blocks) // 2
+        return blocks[:middle], blocks[middle:]
+    mine, other = [], []
+    for a, b in zip(blocks[::2], blocks[1::2]):
+        left = lax.broadcasted_iota(jnp.int32, a.shape, 1) < LANES // 2
+        low = jnp.where(left, a, pltpu.roll(b, LANES // 2, 1))
+        high = jnp.where(left, pltpu.roll(a, LANES // 2, 1), b)
+        mine.append(jnp.where(first, low, high))
+        other.append(jnp.where(first, high, low))
+    return mine, other
+
+
+def lane_blocks(ref):
+    return [ref[:, low : low + LANES] for low in range(0, ref.shape[1], LANES)]
+
+
 def mix_own_kernel(
-    info, own_hbm, neighbours_hbm, weights_hbm, head_hbm, scale_hbm, gain_hbm, bias_hbm, target_hbm,
+    split, info, own_hbm, neighbours_hbm, weights_hbm, head_hbm, scale_hbm, gain_hbm, bias_hbm, target_hbm,
     own, weights, head, scale, gain, bias, target,
-    neighbours, taken, mixed_out, base_out, sems,
+    neighbours, taken, mixed_out, base_out, bias_mine, bias_other, sems,
 ):
     load(
         [(own_hbm, own), (neighbours_hbm, neighbours), (weights_hbm, weights), (head_hbm, head),
          (scale_hbm, scale), (gain_hbm, gain), (bias_hbm, bias), (target_hbm, target)],
         sems,
     )
+    whole = [jnp.broadcast_to(block, (8, LANES)) for block in lane_blocks(bias)]
+    mine, other = by_half(split, info[2] == 0, whole)
+    bias_mine[...] = jnp.concatenate(mine, axis=1)
+    bias_other[...] = jnp.concatenate(other, axis=1)
     source = own[...]
     places = relative_places(info, neighbours)
     base_out[...] = mul(head[...], source, NT)
@@ -132,41 +166,43 @@
 
 
 def forward_kernel(
-    info, normed, mine, other, bias, base, head, scale,
-    act_out, slope_out, forecast_out, normed_t, up, down, reach,
-):
-    owners = mine.shape[0]
-    half = mine.shape[1] // 2
+    normed, part, bias, base, head, scale, act_out, slope_out, forecast_out, up, down, reach
+):
+    owners, half = part.shape[0], part.shape[1] // 2
     for owner in range(owners):
-        for side in range(2):
-            rows = slice((2 * owner + side) * half, (2 * owner + side + 1) * half)
-            up[rows, :] = jnp.where(info[2] == side, mine[owner, :half], other[owner, :half])
-            down[rows, :] = jnp.where(info[2] == side, mine[owner, half:], other[owner, half:])
+        rows = slice(owner * half, (owner + 1) * half)
+        up[rows, :] = part[owner, :half]
+        down[rows, :] = part[owner, half:]
     high, low = halves(head[...].astype(F32) * scale[...])
     product = mul(jnp.concatenate([high, low], axis=0), down[...], NT)
     high, low = halves(product[:8] + product[8:])
     reach[...] = jnp.concatenate([high, low], axis=0)
-    forward(normed, up, reach, bias, base, act_out, slope_out, forecast_out, normed_t)
-
-
-def forward(normed, up, reach, bias, base, act_out, slope_out, forecast_out, normed_t):
     rows = normed[...]
-    normed_t[...] = turned(rows)
     total = base[...]
     for low_edge in range(0, up.shape[0], 256):
         piece = slice(low_edge, low_edge + 256)
-        pre = mul(rows, up[piece, :], NT) + bias[:, piece]
+        pre = mul(rows, up[piece, :], NT) + bias[:1, piece]
         phi = 0.5 + 0.5 * lax.erf(pre * 0.7071067811865476)
         act = (pre * phi).astype(BF16)
         act_out[:, piece] = act
         slope_out[:, piece] = phi + pre * jnp.exp(-0.5 * pre * pre) * 0.3989422804014327
-        part = mul(reach[:, piece], act, NT)
-        total = total + part[:8] + part[8:]
+        product = mul(reach[:, piece], act, NT)
+        total = total + product[:8] + product[8:]
     forecast_out[...] = total
 
 
+def first_kernel(
+    normed, part, bias, base, head, scale,
+    act_out, slope_out, forecast_out, up, down, reach, normed_t,
+):
+    normed_t[...] = turned(normed[...])
+    forward_kernel(
+        normed, part, bias, base, head, scale, act_out, slope_out, forecast_out, up, down, reach
+    )
+
+
 def backward_kernel(
-    mine, other, target, reach, slope, up, mixed, gain, mixed_grad, pre_out, grad_out, loss_out
+    mine, other, target, reaches, slopes, ups, mixed, gain, mixed_grad, pre_outs, grad_out, loss_out
 ):
     apart = mine[...] - target[...]
     spread = mine[...] - other[...]
@@ -176,11 +212,12 @@
     loss_out[...] = jnp.full(loss_out.shape, jnp.sum(0.5 * apart_abs - 0.25 * spread_abs), F32)
     twice = turned(jnp.concatenate([grad, grad], axis=0))
     normed_grad = jnp.zeros(mixed.shape, F32)
-    for low_edge in range(0, up.shape[0], 256):
-        piece = slice(low_edge, low_edge + 256)
-        pre = (mul(twice, reach[:, piece]) * slope[:, piece]).astype(BF16)
-        pre_out[:, piece] = pre
-        normed_grad = normed_grad + mul(pre, up[piece, :])
+    for reach, slope, up, pre_out in zip(reaches, slopes, ups, pre_outs):
+        for low_edge in range(0, up.shape[0], 256):
+            piece = slice(low_edge, low_edge + 256)
+            pre = (mul(twice, reach[:, piece]) * slope[:, piece]).astype(BF16)
+            pre_out[:, piece] = pre
+            normed_grad = normed_grad + mul(pre, up[piece, :])
     values = mixed[...]
     centred = values - row_mean(values)
     inverse = lax.rsqrt(row_mean(centred * centred) + 1e-06)
@@ -191,43 +228,57 @@
     ).astype(BF16)
 
 
+def up_blocks(split, first, rows, pre_grads):
+    products = [[mul(rows, block) for block in lane_blocks(pre)] for pre in pre_grads]
+    return by_owner(split, first, *products)
+
+
 def back_kernel(
-    info, mine, other, target, reach, slope, up, mixed, gain, normed_t,
-    mixed_grad, grad, send, pre_grad, loss, kept,
+    split, info, mine, other, target, reach_a, reach_b, slope_a, slope_b, up_a, up_b, mixed, gain, normed_t,
+    mixed_grad, grad, send, pre_a, pre_b, loss, kept,
 ):
     backward_kernel(
-        mine, other, target, reach, slope, up, mixed, gain, mixed_grad, pre_grad, grad, loss
+        mine, other, target, (reach_a, reach_b), (slope_a, slope_b), (up_a, up_b), mixed, gain,
+        mixed_grad, (pre_a, pre_b), grad, loss,
     )
     first = info[2] == 0
     lower, higher = normed_t[:LANES, :], normed_t[LANES:, :]
     kept[...] = jnp.where(first, lower, higher)
     rows = jnp.where(first, higher, lower)
-    for block in range(send.shape[0]):
-        lanes = slice(block * LANES, (block + 1) * LANES)
-        send[block] = mul(rows, pre_grad[:, lanes]).astype(BF16)
+    for block, value in enumerate(up_blocks(split, first, rows, (pre_a, pre_b))):
+        send[block] = value.astype(BF16)
 
 
 def weights_kernel(
-    pre_grad, kept, act, grad, features, down, scale, taken, mixed_grad, loss, came, joined
-):
-    rows = kept[...]
-    summed = mul(grad[...], act[...])
-    high, low = halves(summed)
-    through = mul(jnp.concatenate([high, low], axis=0), down[...])
-    head_part = mul(grad[...], features[...]) + scale[...] * (through[:8] + through[8:])
+    split, info, pre_a, pre_b, kept, act_a, act_b, grad, features, down_a, down_b, scale, taken, mixed_grad,
+    loss, came, joined
+):
+    first = info[2] == 0
+    sums, through = [], 0.0
+    for act, down in ((act_a, down_a), (act_b, down_b)):
+        summed = mul(grad[...], act[...])
+        high, low = halves(summed)
+        product = mul(jnp.concatenate([high, low], axis=0), down[...])
+        through = through + product[:8] + product[8:]
+        sums.append(lane_blocks(summed))
+    sums = by_owner(split, first, *sums)
+    head_part = mul(grad[...], features[...]) + scale[...] * through
     flow = mixed_grad[...].astype(F32)
     depth = [
         jnp.sum(taken[k].astype(F32) * flow, axis=0, keepdims=True)
         for k in range(taken.shape[0])
     ]
     depth.insert(CENTRE, jnp.sum(features[...].astype(F32) * flow, axis=0, keepdims=True))
-    small = jnp.concatenate([head_part] + depth + [loss[...]], axis=0)
-    for block in range(joined.shape[0]):
-        lanes = slice(block * LANES, (block + 1) * LANES)
-        main = mul(rows, pre_grad[:, lanes]) + came[block].astype(F32)
-        joined[block, :LANES, :] = main.astype(BF16)
-        extra = [small[:, :LANES], small[:, LANES:], summed[:, lanes], jnp.zeros((4, LANES), F32)]
-        joined[block, LANES:, :] = jnp.concatenate(extra, axis=0).astype(BF16)
+    rest = jnp.concatenate(depth + [loss[...]], axis=0)
+    small = jnp.concatenate(
+        [head_part[:, :LANES], head_part[:, LANES:], rest[:, :LANES], rest[:, LANES:],
+         jnp.zeros((4, LANES), F32)],
+        axis=0,
+    )
+    for block, value in enumerate(up_blocks(split, first, kept[...], (pre_a, pre_b))):
+        joined[block, :LANES, :] = (value + came[block].astype(F32)).astype(BF16)
+        extra = jnp.concatenate([sums[block], small], axis=0)
+        joined[block, LANES:, :] = extra.astype(BF16)
 
 
 def sum_kernel(parts, total):
@@ -243,11 +294,12 @@
     up[:, :LANES] = jnp.where(info[2] == 0, mine, other).T * factor
     up[:, LANES:] = jnp.where(info[2] == 0, other, mine).T * factor
     extra = ours[LANES:, :] + theirs[LANES:, :]
-    small = jnp.concatenate([extra[:18], extra[18:36]], axis=1)
-    head_out[...] = small[:8] * factor
-    depth[...] = small[8:17] * factor
-    mean[0] = jnp.sum(small[17:18, :1]) * loss_factor
-    high, low = halves(extra[36:44])
+    head_out[:, :LANES] = extra[8:16] * factor
+    head_out[:, LANES:] = extra[16:24] * factor
+    depth[:, :LANES] = extra[24:33] * factor
+    depth[:, LANES:] = extra[34:43] * factor
+    mean[0] = jnp.sum(extra[33:34, :1]) * loss_factor
+    high, low = halves(extra[:8])
     turn = jnp.concatenate([high, low], axis=0).astype(F32).T.astype(BF16)
     down[...] = mul(turn, jnp.concatenate([head[...], head[...]], axis=0)) * (scale[...] * factor)
 
@@ -352,15 +404,17 @@
     else:
         up = lax.all_gather(up_weight, "pix", axis=0, tiled=True)
         down = lax.all_gather(down_weight, "pix", axis=0, tiled=True)
-        reach = lax.dot_general(
-            head_matrix.astype(F32) * layer_scale, down.astype(F32), NT, precision=exact
-        )
-        reach = jnp.concatenate(halves(reach), axis=0)
-    own, weights, head, scale, gain, bias, target, places, taken, mixed, base = call(
-        mix_own_kernel,
+        part = (8, hidden // 16, channels)
+        mine, other = [
+            jnp.concatenate([up[rows].reshape(part), down[rows].reshape(part)], axis=1)
+            for rows in (slice(0, hidden // 2), slice(hidden // 2, hidden))
+        ]
+    short = ((8, hidden // 2), F32)
+    own, weights, head, scale, gain, _, target, places, taken, mixed, base, bias_mine, bias_other = call(
+        functools.partial(mix_own_kernel, by_blocks),
         [(tile, BF16), (depth_weight.shape, F32), (head_matrix.shape, BF16),
          ((1, channels), F32), ((1, channels), F32), ((1, hidden), F32), ((8, pixels), F32),
-         (neighbours.shape, jnp.int32), (many, BF16), (tile, F32), ((8, pixels), F32)],
+         (neighbours.shape, jnp.int32), (many, BF16), (tile, F32), ((8, pixels), F32), short, short],
         1,
         info, own, neighbours, depth_weight, head_matrix, scale, gain, bias, analysis_fields,
         hbm=8,
@@ -383,37 +437,41 @@
         aliases={5: 0, 6: 1},
         flops=NEAR,
     )
-    outs = [
-        ((pixels, hidden), BF16), ((pixels, hidden), F32), ((8, pixels), F32), ((channels, pixels), BF16)
-    ]
     if by_blocks:
         mine, normed = lax.optimization_barrier((mine, normed))
         other = swap(mine)
-        whole = ((hidden, channels), BF16)
-        act, slope, forecast, normed_t, up, down, reach = call(
-            forward_kernel,
-            outs + [whole, whole, ((16, hidden), BF16)],
-            1,
-            info, normed, mine, other, bias, base, head, scale,
-        )
-    else:
-        act, slope, forecast, normed_t = call(forward, outs, 0, normed, up, reach, bias, base)
+    whole = ((hidden // 2, channels), BF16)
+    outs = [
+        ((pixels, hidden // 2), BF16), ((pixels, hidden // 2), F32), ((8, pixels), F32),
+        whole, whole, ((16, hidden // 2), BF16),
+    ]
+    act_a, slope_a, base, up_a, down_a, reach_a, normed_t = call(
+        first_kernel,
+        outs + [((channels, pixels), BF16)],
+        0,
+        normed, mine, bias_mine, base, head, scale,
+    )
+    act_b, slope_b, forecast, up_b, down_b, reach_b = call(
+        forward_kernel, outs, 0, normed, other, bias_other, base, head, scale
+    )
     blocks = hidden // LANES
     full = ((blocks, LANES + EXTRA, LANES), BF16)
-    mixed_grad, grad, send, pre_grad, loss, kept = call(
-        back_kernel,
+    pre = ((pixels, hidden // 2), BF16)
+    mixed_grad, grad, send, pre_a, pre_b, loss, kept = call(
+        functools.partial(back_kernel, by_blocks),
         [(tile, BF16), ((8, pixels), BF16), ((blocks, LANES, LANES), BF16),
-         ((pixels, hidden), BF16), ((1, channels), F32), ((LANES, pixels), BF16)],
-        1,
-        info, forecast, swap(forecast), target, reach, slope, up, mixed, gain, normed_t,
+         pre, pre, ((1, channels), F32), ((LANES, pixels), BF16)],
+        1,
+        info, forecast, swap(forecast), target, reach_a, reach_b, slope_a, slope_b, up_a, up_b,
+        mixed, gain, normed_t,
     )
     came = swap(send)
     grad_pair, grad_side = pair_tiles(mixed_grad)
     (joined,) = call(
-        weights_kernel,
+        functools.partial(weights_kernel, by_blocks),
         [full],
-        0,
-        pre_grad, kept, act, grad, own, down, scale, taken, mixed_grad, loss, came,
+        1,
+        info, pre_a, pre_b, kept, act_a, act_b, grad, own, down_a, down_b, scale, taken, mixed_grad, loss, came,
     )
     source, joined = lax.optimization_barrier((mixed_grad, joined))
     (partial,) = call(
@@ -455,20 +513,21 @@
     main = jnp.where(member == 0, main, main[::-1])
     rows = jnp.transpose(main, (1, 3, 0, 2)).reshape(hidden, channels)
     up_grad = lax.psum_scatter(rows, "pix", scatter_dimension=0, tiled=True)
-    summed = joined[:, LANES + 36 : LANES + 44].astype(F32)
+    summed = joined[:, LANES : LANES + 8].astype(F32)
     summed = jnp.transpose(summed + swap(summed), (0, 2, 1)).reshape(hidden, 8)
     summed = lax.psum_scatter(summed, "pix", scatter_dimension=0, tiled=True)
     down_grad = layer_scale * jnp.dot(summed, head_matrix.astype(F32), precision=exact)
-    small = joined[0, LANES : LANES + 36].astype(F32).reshape(2, 18, LANES)
-    small = jnp.transpose(small, (1, 0, 2)).reshape(18, channels)
-    small = lax.psum(small, ("pix", "mem"))
+    small = joined[0, LANES + 8 : LANES + 44].astype(F32)
+    head_rows = jnp.concatenate([small[:8], small[8:16]], axis=1)
+    rest = jnp.concatenate([small[16:26], small[26:36]], axis=1)
+    head_rows, rest = lax.psum((head_rows, rest), ("pix", "mem"))
     return (
-        small[17, :1] * loss_scale,
+        rest[9, :1] * loss_scale,
         input_grad[None],
         up_grad * grad_scale,
         down_grad * grad_scale,
-        small[8:17] * grad_scale,
-        small[:8] * grad_scale,
+        rest[:9] * grad_scale,
+        head_rows * grad_scale,
     )
 
 

time: 59 us -> 57.8 us (0.980)
  waiting for transfers between devices: 13.6 us -> 12 us
    ppermute x2, waiting for transfers between devices: 4.7 us -> 3.67 us  [pair_tiles(): lax.ppermute(array, 'pix', inner)]
    ppermute x4, waiting for transfers between devices: 4.23 us -> 3.36 us  [swap(): return lax.ppermute(array, 'mem', [(0, 1), (1, 0)])]
    pallas_call x12 -> x13, Pallas kernels: 22.1 us -> 22.6 us  [call(): pl.pallas_call(kernel, out_shape=tuple((jax.ShapeDtypeStruct(shape, dtype...]
    unnamed x32 -> x36, local copies, waits for them, and re-layouts: 1.57 us -> 1.58 us
  transfers between devices with their start and end apart: 10 -> 10, of which waited for: 5 -> 6; matrix products, arithmetic and copies ran while one was open for 1% -> 1% of each run, Pallas kernels for 29% -> 32%
where the time goes in v5:
time: 57.8 us; the launch traced here: 57.4 us
  Pallas kernels  22.6 us (39%)
  starting transfers between devices  19.3 us (33%)
  waiting for transfers between devices  12 us (21%)
  local copies, waits for them, and re-layouts  1.58 us (3%)
  between operations  1.09 us (2%)
  other arithmetic  0.86 us (1%)
    pallas_call x13, Pallas kernels, call(): pl.pallas_call(kernel, out_shape=tuple((jax.ShapeDtypeStruct(shape, dtype...  22.6 us
    all_to_all x2, starting transfers between devices, everywhere(): return lax.all_to_all(array, 'pix', split_axis=0, concat_axis=0)  13.1 us
    all_to_all x2, waiting for transfers between devices, everywhere(): return lax.all_to_all(array, 'pix', split_axis=0, concat_axis=0)  4.96 us
    ppermute x2, starting transfers between devices, pair_tiles(): lax.ppermute(array, 'pix', inner)  4.43 us
    ppermute x2, waiting for transfers between devices, pair_tiles(): lax.ppermute(array, 'pix', inner)  3.67 us
    ppermute x4, waiting for transfers between devices, swap(): return lax.ppermute(array, 'mem', [(0, 1), (1, 0)])  3.36 us
    unnamed x36, local copies, waits for them, and re-layouts  1.58 us
    ppermute x2, starting transfers between devices, pair_tiles(): lax.ppermute(array, 'pix', outer)  1.33 us
  transfers between devices with their start and end apart: 10, of which 6 were waited for; matrix products, arithmetic and copies ran while one was open for 1% of the time, Pallas kernels for 32%

profile of v5, /device:TPU:0, one launch (start us, length us, event | category | flops | bytes accessed | tf_op | source)
XLA Modules:
  0.0 57.4 jit_solution(11296965356073530731)
XLA Ops:
  0.6 3.0 %collective-permute-start.1 = (bf16[512,256]{1,0:T(8,128)(2,1)}, bf16[512,256]{1,0:T(8,128)(2,1)S(1)}, u32[]{:S(2)}, u32[]{:S(2)}) collective-permute-start(bf16[512,256]{1,0:T(8,128)(2,1)} %bitcast.12), channel_id=1, source_target_pairs={{0,2},{2,0},{4,6},{6,4},{8,10},{10,8},{12,14},{14,12},{1,3},{3,1},... | collective-permute-start | bytes 786440 | tf_op jit(solution)/shard_map/ppermute | solution.py:356
  3.6 0.7 %collective-permute-start = (bf16[512,256]{1,0:T(8,128)(2,1)}, bf16[512,256]{1,0:T(8,128)(2,1)S(1)}, u32[]{:S(2)}, u32[]{:S(2)}) collective-permute-start(bf16[512,256]{1,0:T(8,128)(2,1)} %bitcast.13), channel_id=1, source_target_pairs={{2,4},{6,8},{10,12},{4,2},{8,6},{12,10},{3,5},{7,9},{11,13},{5,3},... | collective-permute-start | bytes 786440 | tf_op jit(solution)/shard_map/ppermute | solution.py:356
  4.3 0.8 %fusion = bf16[2,64,256]{2,1,0:T(8,128)(2,1)S(1)} fusion(s32[]{:T(128)S(6)} %select_n.11, bf16[1,128,256]{2,1,0:T(8,128)(2,1)} %bitcast.18, bf16[1,128,256]{2,1,0:T(8,128)(2,1)} %bitcast.19), kind=kLoop, calls=%fused_computation.2 | loop fusion | flops 131072 | bytes 196612 | tf_op jit(solution)/shard_map/stack | solution.py:394
  5.1 0.0 copy-start
  5.1 0.0 copy-start.2
  5.1 0.0 copy-start.3
  5.1 0.0 copy-start.4
  5.1 0.0 copy-start.5
  5.2 0.0 copy-start.6
  5.2 0.0 copy-start.7
  5.2 0.8 %shard_map.145 = bf16[8,128,256]{2,1,0:T(8,128)(2,1)} custom-call(bf16[128,256]{1,0:T(8,128)(2,1)S(1)} %bitcast.11), custom_call_target="tpu_custom_call" | custom-call | flops 8000000000 | tf_op jit(solution)/shard_map/pallas_call | solution.py:339
  6.0 7.6 %all-to-all-start = ((bf16[8,128,256]{2,1,0:T(8,128)(2,1)}), bf16[8,128,256]{2,1,0:T(8,128)(2,1)S(1)}, u32[]{:S(2)}, u32[]{:S(2)}) async-start(bf16[8,128,256]{2,1,0:T(8,128)(2,1)} %shard_map.145), calls=%async_computation | async-start | bytes 1048576 | tf_op jit(solution)/shard_map/all_to_all | solution.py:389
  13.6 0.1 pad_add_fusion.info
  13.7 0.0 copy-done
  13.7 0.0 copy-done.1
  13.7 0.0 copy-done.2
  13.7 0.0 copy-done.3
  13.7 0.0 copy-done.4
  13.7 0.0 copy-done.5
  13.7 0.0 copy-done.6
  13.7 0.0 copy-done.7
  13.7 2.3 %shard_map.146 = (bf16[512,256]{1,0:T(8,128)(2,1)S(1)}, f32[9,256]{1,0:T(8,128)S(1)}, bf16[8,256]{1,0:T(8,128)(2,1)S(1)}, f32[1,256]{1,0:T(1,128)S(1)}, f32[1,25...) custom-call(s32[3]{0:T(128)S(1)} %pad_add_fusion.info, ...), custom_call_target="tpu_custom_call" | custom-call | flops 8000000000 | tf_op jit(solution)/shard_map/pallas_call | solution.py:339
  16.0 0.0 copy-start.8
  16.0 0.7 %copy-done.8 = bf16[512,256]{1,0:T(8,128)(2,1)} copy-done((bf16[512,256]{1,0:T(8,128)(2,1)}, bf16[512,256]{1,0:T(8,128)(2,1)S(1)}, u32[]{:S(2)}) %copy-start.8) | copy-done | bytes 262168
  16.7 0.0 collective-permute-done.1.tile
  16.7 2.6 %shard_map.147 = (bf16[8,512,256]{2,1,0:T(8,128)(2,1)S(1)}, f32[512,256]{1,0:T(8,128)S(1)}) custom-call(s32[3]{0:T(128)S(1)} %pad_add_fusion.info, bf16[512,256]{1,0:T(8,128)(2,1)S(1)} %collective-permute-done.1.tile, s32[9,512]{1,0:T(8,128)S(1)} %get-tuple-element.54.neighbours, ...), custom_call_target="tpu_custom_call", output_to_operand_aliasing={{0}: (4, {}), {1}: (5, {})} | custom-call | flops 49999998976 | tf_op jit(solution)/shard_map/pallas_call | solution.py:339
  19.3 0.0 copy-done.12
  19.3 0.0 collective-permute-done.tile
  19.3 0.0 copy-done.14
  19.4 0.0 copy-done.16
  19.4 0.0 copy-start.13
  19.4 2.7 %shard_map.148 = (bf16[8,512,256]{2,1,0:T(8,128)(2,1)S(1)}, f32[512,256]{1,0:T(8,128)S(1)}, bf16[512,256]{1,0:T(8,128)(2,1)S(1)}) custom-call(s32[3]{0:T(128)S(1)} %pad_add_fusion.info, bf16[512,256]{1,0:T(8,128)(2,1)S(1)} %collective-permute-done.tile, s32[9,512]{1,0:T(8,128)S(1)} %get-tuple-element.54.neighbours, ...), custom_call_target="tpu_custom_call", output_to_operand_aliasing={{0}: (5, {}), {1}: (6, {})} | custom-call | flops 49999998976 | tf_op jit(solution)/shard_map/pallas_call | solution.py:339
  22.1 0.0 copy-start.10
  22.1 0.8 %copy-done.10 = f32[512,256]{1,0:T(8,128)} copy-done((f32[512,256]{1,0:T(8,128)}, f32[512,256]{1,0:T(8,128)S(1)}, u32[]{:S(2)}) %copy-start.10) | copy-done | bytes 524312
  22.9 4.6 %all-to-all-done.part = bf16[8,128,256]{2,1,0:T(8,128)(2,1)S(1)} async-done(((bf16[8,128,256]{2,1,0:T(8,128)(2,1)}), bf16[8,128,256]{2,1,0:T(8,128)(2,1)S(1)}, u32[]{:S(2)}, u32[]{:S(2)}) %all-to-all-start) | async-done | bytes 524320 | tf_op jit(solution)/shard_map/all_to_all | solution.py:389
  27.6 0.0 collective-permute-start.2
  27.6 0.0 copy-done.13
  27.6 0.9 %shard_map.149 = (bf16[512,512]{1,0:T(8,128)(2,1)S(1)}, f32[512,512]{1,0:T(8,128)S(1)}, f32[8,512]{1,0:T(8,128)S(1)}, bf16[512,256]{1,0:T(8,128)(2,1)S(1)}, bf16...) custom-call(bf16[512,256]{1,0:T(8,128)(2,1)S(1)} %get-tuple-element.62.normed, ...), custom_call_target="tpu_custom_call" | custom-call | flops 2000000000 | tf_op jit(solution)/shard_map/pallas_call | solution.py:339
  28.4 1.0 %collective-permute-done.2.part = bf16[8,128,256]{2,1,0:T(8,128)(2,1)S(1)} collective-permute-done((bf16[8,128,256]{2,1,0:T(8,128)(2,1)S(1)}, bf16[8,128,256]{2,1,0:T(8,128)(2,1)S(1)}, u32[]{:S(2)}, u32[]{:S(2)}) %collective-permute-start.2) | collective-permute-done | bytes 524320 | tf_op jit(solution)/shard_map/ppermute | solution.py:360
  29.5 0.9 %shard_map.150 = (bf16[512,512]{1,0:T(8,128)(2,1)S(1)}, f32[512,512]{1,0:T(8,128)S(1)}, f32[8,512]{1,0:T(8,128)S(1)}, bf16[512,256]{1,0:T(8,128)(2,1)S(1)}, bf16...) custom-call(bf16[512,256]{1,0:T(8,128)(2,1)S(1)} %get-tuple-element.62.normed, ...), custom_call_target="tpu_custom_call" | custom-call | flops 2000000000 | tf_op jit(solution)/shard_map/pallas_call | solution.py:339
  30.3 0.1 collective-permute-start.3
  30.5 1.0 %collective-permute-done.3.other = f32[8,512]{1,0:T(8,128)S(1)} collective-permute-done((f32[8,512]{1,0:T(8,128)S(1)}, f32[8,512]{1,0:T(8,128)S(1)}, u32[]{:S(2)}, u32[]{:S(2)}) %collective-permute-start.3) | collective-permute-done | bytes 16416 | tf_op jit(solution)/shard_map/ppermute | solution.py:360
  31.5 0.0 copy-done.11
  31.5 1.8 %shard_map.151 = (bf16[512,256]{1,0:T(8,128)(2,1)S(1)}, bf16[8,512]{1,0:T(8,128)(2,1)S(1)}, bf16[8,128,128]{2,1,0:T(8,128)(2,1)S(1)}, bf16[512,512]{1,0:T(8,128)...) custom-call(s32[3]{0:T(128)S(1)} %pad_add_fusion.info, ...), custom_call_target="tpu_custom_call" | custom-call | flops 2000000000 | tf_op jit(solution)/shard_map/pallas_call | solution.py:339
  33.3 0.2 collective-permute-start.4
  33.6 1.4 %collective-permute-start.6 = (bf16[512,256]{1,0:T(8,128)(2,1)S(1)}, bf16[512,256]{1,0:T(8,128)(2,1)S(1)}, u32[]{:S(2)}, u32[]{:S(2)}) collective-permute-start(bf16[512,256]{1,0:T(8,128)(2,1)S(1)} %get-tuple-element.94.mixed_grad.own), channel_id=1, source_target_pairs={{0,2},{2,0},{4,6},{6,4},{8,10},{10,8},{12,14},{14,12},{1,3},{3,1},... | collective-permute-start | bytes 786440 | tf_op jit(solution)/shard_map/ppermute | solution.py:356
  35.0 0.7 %collective-permute-start.5 = (bf16[512,256]{1,0:T(8,128)(2,1)S(1)}, bf16[512,256]{1,0:T(8,128)(2,1)S(1)}, u32[]{:S(2)}, u32[]{:S(2)}) collective-permute-start(bf16[512,256]{1,0:T(8,128)(2,1)S(1)} %get-tuple-element.94.mixed_grad.own), channel_id=1, source_target_pairs={{2,4},{6,8},{10,12},{4,2},{8,6},{12,10},{3,5},{7,9},{11,13},{5,3},... | collective-permute-start | bytes 786440 | tf_op jit(solution)/shard_map/ppermute | solution.py:356
  35.7 0.0 collective-permute-done.4.came
  35.7 0.0 copy-done.9
  35.7 0.0 copy-start.15
  35.7 0.0 copy-start.17
  35.7 2.2 %shard_map.152 = bf16[8,176,128]{2,1,0:T(8,128)(2,1)} custom-call(s32[3]{0:T(128)S(1)} %pad_add_fusion.info, bf16[512,512]{1,0:T(8,128)(2,1)S(1)} %get-tuple-element.81.pre_a, bf16[512,512]{1,0:T(8,128)(2,1)S(1)} %get-tuple-element.82.pre_b, bf16[128,512]{1,0:T(8,128)(2,1)S(1)} %get-tuple-element.83.kept, bf16[512,512]{1,0:T(8,128)(2,1)S(1)} %get-tuple-element.84.act_a, ...), custom_call_target="tpu_custom_call" | custom-call | flops 2000000000 | tf_op jit(solution)/shard_map/pallas_call | solution.py:339
  37.9 5.5 %all-to-all-start.1 = ((bf16[8,176,128]{2,1,0:T(8,128)(2,1)}), bf16[8,176,128]{2,1,0:T(8,128)(2,1)S(1)}, u32[]{:S(2)}, u32[]{:S(2)}) async-start(bf16[8,176,128]{2,1,0:T(8,128)(2,1)} %shard_map.152), calls=%async_computation.1 | async-start | bytes 720896 | tf_op jit(solution)/shard_map/all_to_all | solution.py:389
  43.4 0.0 copy-done.15
  43.4 0.0 copy-done.17
  43.4 2.1 %shard_map.153.partial = f32[512,256]{1,0:T(8,128)S(1)} custom-call(s32[3]{0:T(128)S(1)} %pad_add_fusion.info, bf16[512,256]{1,0:T(8,128)(2,1)S(1)} %get-tuple-element.94.mixed_grad.own, s32[9,512]{1,0:T(8,128)S(1)} %copy-done.15, f32[9,256]{1,0:T(8,128)S(1)} %copy-done.17, bf16[8,512]{1,0:T(8,128)(2,1)S(1)} %get-tuple-element.86.grad, ...), custom_call_target="tpu_custom_call" | custom-call | flops 8000000000 | tf_op jit(solution)/shard_map/pallas_call | solution.py:339
  45.5 3.7 %collective-permute-done.6.tile = bf16[512,256]{1,0:T(8,128)(2,1)S(1)} collective-permute-done((bf16[512,256]{1,0:T(8,128)(2,1)S(1)}, bf16[512,256]{1,0:T(8,128)(2,1)S(1)}, u32[]{:S(2)}, u32[]{:S(2)}) %collective-permute-start.6) | collective-permute-done | bytes 262176 | tf_op jit(solution)/shard_map/ppermute | solution.py:356
  49.2 2.1 %shard_map.154.partial = f32[512,256]{1,0:T(8,128)S(1)} custom-call(s32[3]{0:T(128)S(1)} %pad_add_fusion.info, bf16[512,256]{1,0:T(8,128)(2,1)S(1)} %collective-permute-done.6.tile, s32[9,512]{1,0:T(8,128)S(1)} %copy-done.15, f32[9,256]{1,0:T(8,128)S(1)} %copy-done.17, f32[512,256]{1,0:T(8,128)S(1)} %shard_map.153.partial), custom_call_target="tpu_custom_call" | custom-call | flops 49999998976 | tf_op jit(solution)/shard_map/pallas_call | solution.py:339
  51.3 0.0 collective-permute-done.5.tile
  51.3 2.8 %shard_map.155 = bf16[512,256]{1,0:T(8,128)(2,1)} custom-call(s32[3]{0:T(128)S(1)} %pad_add_fusion.info, bf16[512,256]{1,0:T(8,128)(2,1)S(1)} %collective-permute-done.5.tile, s32[9,512]{1,0:T(8,128)S(1)} %copy-done.15, f32[9,256]{1,0:T(8,128)S(1)} %copy-done.17, f32[512,256]{1,0:T(8,128)S(1)} %shard_map.154.partial), custom_call_target="tpu_custom_call" | custom-call | flops 49999998976 | tf_op jit(solution)/shard_map/pallas_call | solution.py:339
  54.1 0.3 all-to-all-done.1.parts
  54.4 0.1 collective-permute-start.7
  54.5 1.3 %collective-permute-done.7.theirs = f32[176,128]{1,0:T(8,128)S(1)} collective-permute-done((f32[176,128]{1,0:T(8,128)S(1)}, f32[176,128]{1,0:T(8,128)S(1)}, u32[]{:S(2)}, u32[]{:S(2)}) %collective-permute-start.7) | collective-permute-done | bytes 90144 | tf_op jit(solution)/shard_map/ppermute | solution.py:360
  55.8 1.4 %shard_map.157 = (f32[1]{0:T(128)}, f32[128,256]{1,0:T(8,128)}, f32[128,256]{1,0:T(8,128)}, f32[9,256]{1,0:T(8,128)}, f32[8,256]{1,0:T(8,128)}) custom-call(s32[3]{0:T(128)S(1)} %pad_add_fusion.info, f32[176,128]{1,0:T(8,128)S(1)} %shard_map.156.ours, f32[176,128]{1,0:T(8,128)S(1)} %collective-permute-done.7.theirs, ...), custom_call_target="tpu_custom_call" | custom-call | flops 2000000000 | tf_op jit(solution)/shard_map/pallas_call | solution.py:339
  (7 shorter events, 0.1 us)
Async XLA Ops:
  0.6 16.1 %collective-permute-start.1 = (bf16[512,256]{1,0:T(8,128)(2,1)}, bf16[512,256]{1,0:T(8,128)(2,1)S(1)}, u32[]{:S(2)}, u32[]{:S(2)}) collective-permute-start(bf16[512,256]{1,0:T(8,128)(2,1)} %bitcast.12), channel_id=1, source_target_pairs={{0,2},{2,0},{4,6},{6,4},{8,10},{10,8},{12,14},{14,12},{1,3},{3,1},... | collective-permute-start | bytes 786440 | tf_op jit(solution)/shard_map/ppermute | solution.py:356
  3.6 15.7 %collective-permute-start = (bf16[512,256]{1,0:T(8,128)(2,1)}, bf16[512,256]{1,0:T(8,128)(2,1)S(1)}, u32[]{:S(2)}, u32[]{:S(2)}) collective-permute-start(bf16[512,256]{1,0:T(8,128)(2,1)} %bitcast.13), channel_id=1, source_target_pairs={{2,4},{6,8},{10,12},{4,2},{8,6},{12,10},{3,5},{7,9},{11,13},{5,3},... | collective-permute-start | bytes 786440 | tf_op jit(solution)/shard_map/ppermute | solution.py:356
  5.1 8.6 %copy-start = (bf16[1,512,256]{2,1,0:T(8,128)(2,1)S(1)}, bf16[1,512,256]{2,1,0:T(8,128)(2,1)}, u32[]{:S(2)}) copy-start(bf16[1,512,256]{2,1,0:T(8,128)(2,1)} %param.10) | copy-start | bytes 786436
  5.1 8.6 %copy-start.1 = (s32[9,512]{1,0:T(8,128)S(1)}, s32[9,512]{1,0:T(8,128)}, u32[]{:S(2)}) copy-start(s32[9,512]{1,0:T(8,128)} %neighbours_hbm.1) | copy-start | bytes 55300
  5.1 8.6 %copy-start.2 = (f32[9,256]{1,0:T(8,128)S(1)}, f32[9,256]{1,0:T(8,128)}, u32[]{:S(2)}) copy-start(f32[9,256]{1,0:T(8,128)} %weights_hbm.1) | copy-start | bytes 27652
  5.1 8.6 %copy-start.3 = (f32[8,512]{1,0:T(8,128)S(1)}, f32[8,512]{1,0:T(8,128)}, u32[]{:S(2)}) copy-start(f32[8,512]{1,0:T(8,128)} %target_hbm.1) | copy-start | bytes 49156
  5.1 8.6 %copy-start.4 = (bf16[8,256]{1,0:T(8,128)(2,1)S(1)}, bf16[8,256]{1,0:T(8,128)(2,1)}, u32[]{:S(2)}) copy-start(bf16[8,256]{1,0:T(8,128)(2,1)} %head_hbm.1) | copy-start | bytes 12292
  5.1 8.6 %copy-start.5 = (f32[1024]{0:T(1024)S(1)}, f32[1024]{0:T(1024)}, u32[]{:S(2)}) copy-start(f32[1024]{0:T(1024)} %param.16) | copy-start | bytes 12292
  5.2 8.6 %copy-start.6 = (f32[256]{0:T(256)S(1)}, f32[256]{0:T(256)}, u32[]{:S(2)}) copy-start(f32[256]{0:T(256)} %param.18) | copy-start | bytes 3076
  5.2 8.5 %copy-start.7 = (f32[256]{0:T(256)S(1)}, f32[256]{0:T(256)}, u32[]{:S(2)}) copy-start(f32[256]{0:T(256)} %param.14) | copy-start | bytes 3076
  6.0 21.5 %all-to-all-start = ((bf16[8,128,256]{2,1,0:T(8,128)(2,1)}), bf16[8,128,256]{2,1,0:T(8,128)(2,1)S(1)}, u32[]{:S(2)}, u32[]{:S(2)}) async-start(bf16[8,128,256]{2,1,0:T(8,128)(2,1)} %shard_map.145), calls=%async_computation | async-start | bytes 1048576 | tf_op jit(solution)/shard_map/all_to_all | solution.py:389
  16.0 0.7 %copy-start.8 = (bf16[512,256]{1,0:T(8,128)(2,1)}, bf16[512,256]{1,0:T(8,128)(2,1)S(1)}, u32[]{:S(2)}) copy-start(bf16[512,256]{1,0:T(8,128)(2,1)S(1)} %get-tuple-element.87.features) | copy-start | bytes 786436
  16.7 2.6 %copy-start.12 = (f32[8,512]{1,0:T(8,128)}, f32[8,512]{1,0:T(8,128)S(1)}, u32[]{:S(2)}) copy-start(f32[8,512]{1,0:T(8,128)S(1)} %get-tuple-element.65.bias) | copy-start | bytes 49156
  16.7 2.6 %copy-start.14 = (s32[9,512]{1,0:T(8,128)}, s32[9,512]{1,0:T(8,128)S(1)}, u32[]{:S(2)}) copy-start(s32[9,512]{1,0:T(8,128)S(1)} %get-tuple-element.54.neighbours) | copy-start | bytes 55300
  16.7 2.6 %copy-start.16 = (f32[9,256]{1,0:T(8,128)}, f32[9,256]{1,0:T(8,128)S(1)}, u32[]{:S(2)}) copy-start(f32[9,256]{1,0:T(8,128)S(1)} %get-tuple-element.55.weights) | copy-start | bytes 27652
  19.4 8.2 %copy-start.13 = (f32[8,512]{1,0:T(8,128)S(1)}, f32[8,512]{1,0:T(8,128)}, u32[]{:S(2)}) copy-start(f32[8,512]{1,0:T(8,128)} %copy-done.12) | copy-start | bytes 49156
  22.1 0.8 %copy-start.10 = (f32[512,256]{1,0:T(8,128)}, f32[512,256]{1,0:T(8,128)S(1)}, u32[]{:S(2)}) copy-start(f32[512,256]{1,0:T(8,128)S(1)} %get-tuple-element.78.mixed) | copy-start | bytes 1572868
  27.6 1.9 %collective-permute-start.2 = (bf16[8,128,256]{2,1,0:T(8,128)(2,1)S(1)}, bf16[8,128,256]{2,1,0:T(8,128)(2,1)S(1)}, u32[]{:S(2)}, u32[]{:S(2)}) collective-permute-start(bf16[8,128,256]{2,1,0:T(8,128)(2,1)S(1)} %all-to-all-done.part), channel_id=1, source_target_pairs={{0,1},{1,0},{2,3},{3,2},{4,5},{5,4},{6,7},{7,6},{8,9},{9,8},{10,11... | collective-permute-start | bytes 1572872 | tf_op jit(solution)/shard_map/ppermute | solution.py:360
  29.5 2.1 %copy-start.11 = (f32[512,256]{1,0:T(8,128)S(1)}, f32[512,256]{1,0:T(8,128)}, u32[]{:S(2)}) copy-start(f32[512,256]{1,0:T(8,128)} %copy-done.10) | copy-start | bytes 1572868
  30.3 1.2 %collective-permute-start.3 = (f32[8,512]{1,0:T(8,128)S(1)}, f32[8,512]{1,0:T(8,128)S(1)}, u32[]{:S(2)}, u32[]{:S(2)}) collective-permute-start(f32[8,512]{1,0:T(8,128)S(1)} %get-tuple-element.70.mine), channel_id=1, source_target_pairs={{0,1},{1,0},{2,3},{3,2},{4,5},{5,4},{6,7},{7,6},{8,9},{9,8},{10,11... | collective-permute-start | bytes 49160 | tf_op jit(solution)/shard_map/ppermute | solution.py:360
  31.5 4.1 %copy-start.9 = (bf16[512,256]{1,0:T(8,128)(2,1)S(1)}, bf16[512,256]{1,0:T(8,128)(2,1)}, u32[]{:S(2)}) copy-start(bf16[512,256]{1,0:T(8,128)(2,1)} %copy-done.8) | copy-start | bytes 786436
  33.3 2.3 %collective-permute-start.4 = (bf16[8,128,128]{2,1,0:T(8,128)(2,1)S(1)}, bf16[8,128,128]{2,1,0:T(8,128)(2,1)S(1)}, u32[]{:S(2)}, u32[]{:S(2)}) collective-permute-start(bf16[8,128,128]{2,1,0:T(8,128)(2,1)S(1)} %get-tuple-element.92), channel_id=1, source_target_pairs={{0,1},{1,0},{2,3},{3,2},{4,5},{5,4},{6,7},{7,6},{8,9},{9,8},{10,11... | collective-permute-start | bytes 786440 | tf_op jit(solution)/shard_map/ppermute | solution.py:360
  33.6 15.7 %collective-permute-start.6 = (bf16[512,256]{1,0:T(8,128)(2,1)S(1)}, bf16[512,256]{1,0:T(8,128)(2,1)S(1)}, u32[]{:S(2)}, u32[]{:S(2)}) collective-permute-start(bf16[512,256]{1,0:T(8,128)(2,1)S(1)} %get-tuple-element.94.mixed_grad.own), channel_id=1, source_target_pairs={{0,2},{2,0},{4,6},{6,4},{8,10},{10,8},{12,14},{14,12},{1,3},{3,1},... | collective-permute-start | bytes 786440 | tf_op jit(solution)/shard_map/ppermute | solution.py:356
  35.0 16.3 %collective-permute-start.5 = (bf16[512,256]{1,0:T(8,128)(2,1)S(1)}, bf16[512,256]{1,0:T(8,128)(2,1)S(1)}, u32[]{:S(2)}, u32[]{:S(2)}) collective-permute-start(bf16[512,256]{1,0:T(8,128)(2,1)S(1)} %get-tuple-element.94.mixed_grad.own), channel_id=1, source_target_pairs={{2,4},{6,8},{10,12},{4,2},{8,6},{12,10},{3,5},{7,9},{11,13},{5,3},... | collective-permute-start | bytes 786440 | tf_op jit(solution)/shard_map/ppermute | solution.py:356
  35.7 7.7 %copy-start.15 = (s32[9,512]{1,0:T(8,128)S(1)}, s32[9,512]{1,0:T(8,128)}, u32[]{:S(2)}) copy-start(s32[9,512]{1,0:T(8,128)} %copy-done.14) | copy-start | bytes 55300
  35.7 7.7 %copy-start.17 = (f32[9,256]{1,0:T(8,128)S(1)}, f32[9,256]{1,0:T(8,128)}, u32[]{:S(2)}) copy-start(f32[9,256]{1,0:T(8,128)} %copy-done.16) | copy-start | bytes 27652
  37.9 16.5 %all-to-all-start.1 = ((bf16[8,176,128]{2,1,0:T(8,128)(2,1)}), bf16[8,176,128]{2,1,0:T(8,128)(2,1)S(1)}, u32[]{:S(2)}, u32[]{:S(2)}) async-start(bf16[8,176,128]{2,1,0:T(8,128)(2,1)} %shard_map.152), calls=%async_computation.1 | async-start | bytes 720896 | tf_op jit(solution)/shard_map/all_to_all | solution.py:389
  54.4 1.4 %collective-permute-start.7 = (f32[176,128]{1,0:T(8,128)S(1)}, f32[176,128]{1,0:T(8,128)S(1)}, u32[]{:S(2)}, u32[]{:S(2)}) collective-permute-start(f32[176,128]{1,0:T(8,128)S(1)} %shard_map.156.ours), channel_id=1, source_target_pairs={{0,1},{1,0},{2,3},{3,2},{4,5},{5,4},{6,7},{7,6},{8,9},{9,8},{10,11... | collective-permute-start | bytes 270344 | tf_op jit(solution)/shard_map/ppermute | solution.py:360

commit v6 on v5

--- a/solution.py
+++ b/solution.py
@@ -57,6 +57,15 @@
 def side_places(info, neighbours):
     pixels = neighbours.shape[1]
     return relative_places(info, neighbours) + jnp.where(info[1] == 0, pixels, -pixels).astype(F32)
+
+
+def outer_places(info, neighbours):
+    relative = relative_places(info, neighbours)
+    pixels = float(neighbours.shape[1])
+    after, before = relative >= pixels, relative < 0
+    even = jnp.where(after, relative - pixels, jnp.where(before, relative + 2 * pixels, FAR))
+    odd = jnp.where(before, relative + pixels, jnp.where(after, relative, FAR))
+    return jnp.where(info[1] == 0, even, odd)
 
 
 def tap_rows(places, source, tap):
@@ -114,15 +123,16 @@
 
 
 def mix_own_kernel(
-    split, info, own_hbm, neighbours_hbm, weights_hbm, head_hbm, scale_hbm, gain_hbm, bias_hbm, target_hbm,
+    split, info, own_hbm, neighbours_hbm, weights_hbm, scale_hbm, gain_hbm, bias_hbm, target_hbm, head_in,
     own, weights, head, scale, gain, bias, target,
     neighbours, taken, mixed_out, base_out, bias_mine, bias_other, sems,
 ):
     load(
-        [(own_hbm, own), (neighbours_hbm, neighbours), (weights_hbm, weights), (head_hbm, head),
-         (scale_hbm, scale), (gain_hbm, gain), (bias_hbm, bias), (target_hbm, target)],
+        [(own_hbm, own), (neighbours_hbm, neighbours), (weights_hbm, weights), (scale_hbm, scale),
+         (gain_hbm, gain), (bias_hbm, bias), (target_hbm, target)],
         sems,
     )
+    head[...] = head_in[...]
     whole = [jnp.broadcast_to(block, (8, LANES)) for block in lane_blocks(bias)]
     mine, other = by_half(split, info[2] == 0, whole)
     bias_mine[...] = jnp.concatenate(mine, axis=1)
@@ -320,12 +330,9 @@
     out[...] = back_taps(total, source, relative_places(info, neighbours), weights)
 
 
-def input_pair_kernel(info, tile, neighbours, weights, partial, out):
-    out[...] = back_taps(partial[...], tile[...], pair_places(info, neighbours), weights)
-
-
-def input_side_kernel(info, tile, neighbours, weights, partial, out):
-    total = back_taps(partial[...], tile[...], side_places(info, neighbours), weights)
+def input_outer_kernel(info, side, pair, neighbours, weights, partial, out):
+    source = jnp.concatenate([pair[...], side[...]], axis=0)
+    total = back_taps(partial[...], source, outer_places(info, neighbours), weights)
     out[...] = total.astype(BF16)
 
 
@@ -416,9 +423,9 @@
          ((1, channels), F32), ((1, channels), F32), ((1, hidden), F32), ((8, pixels), F32),
          (neighbours.shape, jnp.int32), (many, BF16), (tile, F32), ((8, pixels), F32), short, short],
         1,
-        info, own, neighbours, depth_weight, head_matrix, scale, gain, bias, analysis_fields,
-        hbm=8,
-        scratch=[pltpu.SemaphoreType.DMA((8,))],
+        info, own, neighbours, depth_weight, scale, gain, bias, analysis_fields, head_matrix,
+        hbm=7,
+        scratch=[pltpu.SemaphoreType.DMA((7,))],
         flops=OWN,
     )
     taken, mixed = call(
@@ -477,18 +484,11 @@
     (partial,) = call(
         input_own_kernel, [(tile, F32)], 1, info, source, places, weights, grad, head, flops=OWN
     )
-    (partial,) = call(
-        input_pair_kernel,
-        [(tile, F32)],
-        1,
-        info, grad_pair, places, weights, partial,
-        flops=NEAR,
-    )
     (input_grad,) = call(
-        input_side_kernel,
+        input_outer_kernel,
         [(tile, BF16)],
         1,
-        info, grad_side, places, weights, partial,
+        info, grad_side, grad_pair, places, weights, partial,
         flops=NEAR,
         last=True,
     )

time: 57.8 us -> 57.8 us (level)
  Pallas kernels: 22.6 us -> 21.7 us
  waiting for transfers between devices: 12 us -> 12.9 us
    all_to_all x2, waiting for transfers between devices: 4.96 us -> 5.86 us  [everywhere(): return lax.all_to_all(array, 'pix', split_axis=0, concat_axis=0)]
    pallas_call x13 -> x12, Pallas kernels: 22.6 us -> 21.7 us  [call(): pl.pallas_call(kernel, out_shape=tuple((jax.ShapeDtypeStruct(shape, dtype...]
  transfers between devices with their start and end apart: 10 -> 10, of which waited for: 6 -> 6; matrix products, arithmetic and copies ran while one was open for 1% -> 1% of each run, Pallas kernels for 32% -> 31%
where the time goes in v6:
time: 57.8 us; the launch traced here: 57.4 us
  Pallas kernels  21.7 us (38%)
  starting transfers between devices  19.3 us (33%)
  waiting for transfers between devices  12.9 us (22%)
  local copies, waits for them, and re-layouts  1.58 us (3%)
  between operations  1.07 us (2%)
  other arithmetic  0.86 us (1%)
    pallas_call x12, Pallas kernels, call(): pl.pallas_call(kernel, out_shape=tuple((jax.ShapeDtypeStruct(shape, dtype...  21.7 us
    all_to_all x2, starting transfers between devices, everywhere(): return lax.all_to_all(array, 'pix', split_axis=0, concat_axis=0)  13.1 us
    all_to_all x2, waiting for transfers between devices, everywhere(): return lax.all_to_all(array, 'pix', split_axis=0, concat_axis=0)  5.86 us
    ppermute x2, starting transfers between devices, pair_tiles(): lax.ppermute(array, 'pix', inner)  4.43 us
    ppermute x2, waiting for transfers between devices, pair_tiles(): lax.ppermute(array, 'pix', inner)  3.67 us
    ppermute x4, waiting for transfers between devices, swap(): return lax.ppermute(array, 'mem', [(0, 1), (1, 0)])  3.36 us
    unnamed x36, local copies, waits for them, and re-layouts  1.58 us
    ppermute x2, starting transfers between devices, pair_tiles(): lax.ppermute(array, 'pix', outer)  1.33 us
  transfers between devices with their start and end apart: 10, of which 6 were waited for; matrix products, arithmetic and copies ran while one was open for 1% of the time, Pallas kernels for 31%

profile of v6, /device:TPU:0, one launch (start us, length us, event | category | flops | bytes accessed | tf_op | source)
XLA Modules:
  0.0 57.4 jit_solution(12046426056345832851)
XLA Ops:
  0.6 3.0 %collective-permute-start.1 = (bf16[512,256]{1,0:T(8,128)(2,1)}, bf16[512,256]{1,0:T(8,128)(2,1)S(1)}, u32[]{:S(2)}, u32[]{:S(2)}) collective-permute-start(bf16[512,256]{1,0:T(8,128)(2,1)} %bitcast.12), channel_id=1, source_target_pairs={{0,2},{2,0},{4,6},{6,4},{8,10},{10,8},{12,14},{14,12},{1,3},{3,1},... | collective-permute-start | bytes 786440 | tf_op jit(solution)/shard_map/ppermute | solution.py:363
  3.6 0.7 %collective-permute-start = (bf16[512,256]{1,0:T(8,128)(2,1)}, bf16[512,256]{1,0:T(8,128)(2,1)S(1)}, u32[]{:S(2)}, u32[]{:S(2)}) collective-permute-start(bf16[512,256]{1,0:T(8,128)(2,1)} %bitcast.13), channel_id=1, source_target_pairs={{2,4},{6,8},{10,12},{4,2},{8,6},{12,10},{3,5},{7,9},{11,13},{5,3},... | collective-permute-start | bytes 786440 | tf_op jit(solution)/shard_map/ppermute | solution.py:363
  4.3 0.8 %fusion = bf16[2,64,256]{2,1,0:T(8,128)(2,1)S(1)} fusion(s32[]{:T(128)S(6)} %select_n.11, bf16[1,128,256]{2,1,0:T(8,128)(2,1)} %bitcast.18, bf16[1,128,256]{2,1,0:T(8,128)(2,1)} %bitcast.19), kind=kLoop, calls=%fused_computation.2 | loop fusion | flops 131072 | bytes 196612 | tf_op jit(solution)/shard_map/stack | solution.py:401
  5.1 0.0 copy-start
  5.1 0.0 copy-start.1
  5.1 0.0 copy-start.2
  5.1 0.0 copy-start.3
  5.1 0.0 copy-start.4
  5.1 0.0 copy-start.5
  5.2 0.0 copy-start.6
  5.2 0.0 copy-start.7
  5.2 0.8 %shard_map.145 = bf16[8,128,256]{2,1,0:T(8,128)(2,1)} custom-call(bf16[128,256]{1,0:T(8,128)(2,1)S(1)} %bitcast.11), custom_call_target="tpu_custom_call" | custom-call | flops 8000000000 | tf_op jit(solution)/shard_map/pallas_call | solution.py:346
  6.0 7.6 %all-to-all-start = ((bf16[8,128,256]{2,1,0:T(8,128)(2,1)}), bf16[8,128,256]{2,1,0:T(8,128)(2,1)S(1)}, u32[]{:S(2)}, u32[]{:S(2)}) async-start(bf16[8,128,256]{2,1,0:T(8,128)(2,1)} %shard_map.145), calls=%async_computation | async-start | bytes 1048576 | tf_op jit(solution)/shard_map/all_to_all | solution.py:396
  13.6 0.1 pad_add_fusion.info
  13.7 0.0 copy-done
  13.7 0.0 copy-done.1
  13.7 0.0 copy-done.2
  13.7 0.0 copy-done.3
  13.7 0.0 copy-done.4
  13.7 0.0 copy-done.5
  13.7 0.0 copy-done.6
  13.7 0.0 copy-done.7
  13.7 2.3 %shard_map.146 = (bf16[512,256]{1,0:T(8,128)(2,1)S(1)}, f32[9,256]{1,0:T(8,128)S(1)}, bf16[8,256]{1,0:T(8,128)(2,1)S(1)}, f32[1,256]{1,0:T(1,128)S(1)}, f32[1,25...) custom-call(s32[3]{0:T(128)S(1)} %pad_add_fusion.info, ...), custom_call_target="tpu_custom_call" | custom-call | flops 8000000000 | tf_op jit(solution)/shard_map/pallas_call | solution.py:346
  16.0 0.0 copy-start.8
  16.0 0.7 %copy-done.8 = bf16[512,256]{1,0:T(8,128)(2,1)} copy-done((bf16[512,256]{1,0:T(8,128)(2,1)}, bf16[512,256]{1,0:T(8,128)(2,1)S(1)}, u32[]{:S(2)}) %copy-start.8) | copy-done | bytes 262168
  16.7 0.0 collective-permute-done.1.tile
  16.7 2.6 %shard_map.147 = (bf16[8,512,256]{2,1,0:T(8,128)(2,1)S(1)}, f32[512,256]{1,0:T(8,128)S(1)}) custom-call(s32[3]{0:T(128)S(1)} %pad_add_fusion.info, bf16[512,256]{1,0:T(8,128)(2,1)S(1)} %collective-permute-done.1.tile, s32[9,512]{1,0:T(8,128)S(1)} %get-tuple-element.54.neighbours, ...), custom_call_target="tpu_custom_call", output_to_operand_aliasing={{0}: (4, {}), {1}: (5, {})} | custom-call | flops 49999998976 | tf_op jit(solution)/shard_map/pallas_call | solution.py:346
  19.3 0.0 copy-done.12
  19.3 0.0 collective-permute-done.tile
  19.3 0.0 copy-done.14
  19.3 0.0 copy-done.16
  19.3 0.0 copy-start.13
  19.4 2.7 %shard_map.148 = (bf16[8,512,256]{2,1,0:T(8,128)(2,1)S(1)}, f32[512,256]{1,0:T(8,128)S(1)}, bf16[512,256]{1,0:T(8,128)(2,1)S(1)}) custom-call(s32[3]{0:T(128)S(1)} %pad_add_fusion.info, bf16[512,256]{1,0:T(8,128)(2,1)S(1)} %collective-permute-done.tile, s32[9,512]{1,0:T(8,128)S(1)} %get-tuple-element.54.neighbours, ...), custom_call_target="tpu_custom_call", output_to_operand_aliasing={{0}: (5, {}), {1}: (6, {})} | custom-call | flops 49999998976 | tf_op jit(solution)/shard_map/pallas_call | solution.py:346
  22.1 0.0 copy-start.10
  22.1 0.8 %copy-done.10 = f32[512,256]{1,0:T(8,128)} copy-done((f32[512,256]{1,0:T(8,128)}, f32[512,256]{1,0:T(8,128)S(1)}, u32[]{:S(2)}) %copy-start.10) | copy-done | bytes 524312
  22.9 4.7 %all-to-all-done.part = bf16[8,128,256]{2,1,0:T(8,128)(2,1)S(1)} async-done(((bf16[8,128,256]{2,1,0:T(8,128)(2,1)}), bf16[8,128,256]{2,1,0:T(8,128)(2,1)S(1)}, u32[]{:S(2)}, u32[]{:S(2)}) %all-to-all-start) | async-done | bytes 524320 | tf_op jit(solution)/shard_map/all_to_all | solution.py:396
  27.6 0.0 collective-permute-start.2
  27.6 0.0 copy-done.13
  27.6 0.9 %shard_map.149 = (bf16[512,512]{1,0:T(8,128)(2,1)S(1)}, f32[512,512]{1,0:T(8,128)S(1)}, f32[8,512]{1,0:T(8,128)S(1)}, bf16[512,256]{1,0:T(8,128)(2,1)S(1)}, bf16...) custom-call(bf16[512,256]{1,0:T(8,128)(2,1)S(1)} %get-tuple-element.62.normed, ...), custom_call_target="tpu_custom_call" | custom-call | flops 2000000000 | tf_op jit(solution)/shard_map/pallas_call | solution.py:346
  28.4 1.0 %collective-permute-done.2.part = bf16[8,128,256]{2,1,0:T(8,128)(2,1)S(1)} collective-permute-done((bf16[8,128,256]{2,1,0:T(8,128)(2,1)S(1)}, bf16[8,128,256]{2,1,0:T(8,128)(2,1)S(1)}, u32[]{:S(2)}, u32[]{:S(2)}) %collective-permute-start.2) | collective-permute-done | bytes 524320 | tf_op jit(solution)/shard_map/ppermute | solution.py:367
  29.5 0.9 %shard_map.150 = (bf16[512,512]{1,0:T(8,128)(2,1)S(1)}, f32[512,512]{1,0:T(8,128)S(1)}, f32[8,512]{1,0:T(8,128)S(1)}, bf16[512,256]{1,0:T(8,128)(2,1)S(1)}, bf16...) custom-call(bf16[512,256]{1,0:T(8,128)(2,1)S(1)} %get-tuple-element.62.normed, ...), custom_call_target="tpu_custom_call" | custom-call | flops 2000000000 | tf_op jit(solution)/shard_map/pallas_call | solution.py:346
  30.3 0.1 collective-permute-start.3
  30.5 1.0 %collective-permute-done.3.other = f32[8,512]{1,0:T(8,128)S(1)} collective-permute-done((f32[8,512]{1,0:T(8,128)S(1)}, f32[8,512]{1,0:T(8,128)S(1)}, u32[]{:S(2)}, u32[]{:S(2)}) %collective-permute-start.3) | collective-permute-done | bytes 16416 | tf_op jit(solution)/shard_map/ppermute | solution.py:367
  31.5 0.0 copy-done.11
  31.5 1.8 %shard_map.151 = (bf16[512,256]{1,0:T(8,128)(2,1)S(1)}, bf16[8,512]{1,0:T(8,128)(2,1)S(1)}, bf16[8,128,128]{2,1,0:T(8,128)(2,1)S(1)}, bf16[512,512]{1,0:T(8,128)...) custom-call(s32[3]{0:T(128)S(1)} %pad_add_fusion.info, ...), custom_call_target="tpu_custom_call" | custom-call | flops 2000000000 | tf_op jit(solution)/shard_map/pallas_call | solution.py:346
  33.3 0.2 collective-permute-start.4
  33.6 1.4 %collective-permute-start.6 = (bf16[512,256]{1,0:T(8,128)(2,1)S(1)}, bf16[512,256]{1,0:T(8,128)(2,1)S(1)}, u32[]{:S(2)}, u32[]{:S(2)}) collective-permute-start(bf16[512,256]{1,0:T(8,128)(2,1)S(1)} %get-tuple-element.94.mixed_grad.own), channel_id=1, source_target_pairs={{0,2},{2,0},{4,6},{6,4},{8,10},{10,8},{12,14},{14,12},{1,3},{3,1},... | collective-permute-start | bytes 786440 | tf_op jit(solution)/shard_map/ppermute | solution.py:363
  35.0 0.7 %collective-permute-start.5 = (bf16[512,256]{1,0:T(8,128)(2,1)S(1)}, bf16[512,256]{1,0:T(8,128)(2,1)S(1)}, u32[]{:S(2)}, u32[]{:S(2)}) collective-permute-start(bf16[512,256]{1,0:T(8,128)(2,1)S(1)} %get-tuple-element.94.mixed_grad.own), channel_id=1, source_target_pairs={{2,4},{6,8},{10,12},{4,2},{8,6},{12,10},{3,5},{7,9},{11,13},{5,3},... | collective-permute-start | bytes 786440 | tf_op jit(solution)/shard_map/ppermute | solution.py:363
  35.7 0.0 collective-permute-done.4.came
  35.7 0.0 copy-done.9
  35.7 0.0 copy-start.15
  35.7 0.0 copy-start.17
  35.7 2.2 %shard_map.152 = bf16[8,176,128]{2,1,0:T(8,128)(2,1)} custom-call(s32[3]{0:T(128)S(1)} %pad_add_fusion.info, bf16[512,512]{1,0:T(8,128)(2,1)S(1)} %get-tuple-element.81.pre_a, bf16[512,512]{1,0:T(8,128)(2,1)S(1)} %get-tuple-element.82.pre_b, bf16[128,512]{1,0:T(8,128)(2,1)S(1)} %get-tuple-element.83.kept, bf16[512,512]{1,0:T(8,128)(2,1)S(1)} %get-tuple-element.84.act_a, ...), custom_call_target="tpu_custom_call" | custom-call | flops 2000000000 | tf_op jit(solution)/shard_map/pallas_call | solution.py:346
  37.9 5.5 %all-to-all-start.1 = ((bf16[8,176,128]{2,1,0:T(8,128)(2,1)}), bf16[8,176,128]{2,1,0:T(8,128)(2,1)S(1)}, u32[]{:S(2)}, u32[]{:S(2)}) async-start(bf16[8,176,128]{2,1,0:T(8,128)(2,1)} %shard_map.152), calls=%async_computation.1 | async-start | bytes 720896 | tf_op jit(solution)/shard_map/all_to_all | solution.py:396
  43.4 0.0 copy-done.15
  43.4 0.0 copy-done.17
  43.4 2.1 %shard_map.153.partial = f32[512,256]{1,0:T(8,128)S(1)} custom-call(s32[3]{0:T(128)S(1)} %pad_add_fusion.info, bf16[512,256]{1,0:T(8,128)(2,1)S(1)} %get-tuple-element.94.mixed_grad.own, s32[9,512]{1,0:T(8,128)S(1)} %copy-done.15, f32[9,256]{1,0:T(8,128)S(1)} %copy-done.17, bf16[8,512]{1,0:T(8,128)(2,1)S(1)} %get-tuple-element.86.grad, ...), custom_call_target="tpu_custom_call" | custom-call | flops 8000000000 | tf_op jit(solution)/shard_map/pallas_call | solution.py:346
  45.5 3.7 %collective-permute-done.6.pair = bf16[512,256]{1,0:T(8,128)(2,1)S(1)} collective-permute-done((bf16[512,256]{1,0:T(8,128)(2,1)S(1)}, bf16[512,256]{1,0:T(8,128)(2,1)S(1)}, u32[]{:S(2)}, u32[]{:S(2)}) %collective-permute-start.6) | collective-permute-done | bytes 262176 | tf_op jit(solution)/shard_map/ppermute | solution.py:363
  49.2 0.0 collective-permute-done.5.side
  49.2 4.0 %shard_map.154 = bf16[512,256]{1,0:T(8,128)(2,1)} custom-call(s32[3]{0:T(128)S(1)} %pad_add_fusion.info, bf16[512,256]{1,0:T(8,128)(2,1)S(1)} %collective-permute-done.5.side, bf16[512,256]{1,0:T(8,128)(2,1)S(1)} %collective-permute-done.6.pair, s32[9,512]{1,0:T(8,128)S(1)} %copy-done.15, f32[9,256]{1,0:T(8,128)S(1)} %copy-done.17, ...), custom_call_target="tpu_custom_call" | custom-call | flops 49999998976 | tf_op jit(solution)/shard_map/pallas_call | solution.py:346
  53.2 1.2 %all-to-all-done.1.parts = bf16[8,176,128]{2,1,0:T(8,128)(2,1)S(1)} async-done(((bf16[8,176,128]{2,1,0:T(8,128)(2,1)}), bf16[8,176,128]{2,1,0:T(8,128)(2,1)S(1)}, u32[]{:S(2)}, u32[]{:S(2)}) %all-to-all-start.1) | async-done | bytes 360480 | tf_op jit(solution)/shard_map/all_to_all | solution.py:396
  54.4 0.1 collective-permute-start.7
  54.5 1.3 %collective-permute-done.7.theirs = f32[176,128]{1,0:T(8,128)S(1)} collective-permute-done((f32[176,128]{1,0:T(8,128)S(1)}, f32[176,128]{1,0:T(8,128)S(1)}, u32[]{:S(2)}, u32[]{:S(2)}) %collective-permute-start.7) | collective-permute-done | bytes 90144 | tf_op jit(solution)/shard_map/ppermute | solution.py:367
  55.8 1.4 %shard_map.156 = (f32[1]{0:T(128)}, f32[128,256]{1,0:T(8,128)}, f32[128,256]{1,0:T(8,128)}, f32[9,256]{1,0:T(8,128)}, f32[8,256]{1,0:T(8,128)}) custom-call(s32[3]{0:T(128)S(1)} %pad_add_fusion.info, f32[176,128]{1,0:T(8,128)S(1)} %shard_map.155.ours, f32[176,128]{1,0:T(8,128)S(1)} %collective-permute-done.7.theirs, ...), custom_call_target="tpu_custom_call" | custom-call | flops 2000000000 | tf_op jit(solution)/shard_map/pallas_call | solution.py:346
  (6 shorter events, 0.1 us)
Async XLA Ops:
  0.6 16.1 %collective-permute-start.1 = (bf16[512,256]{1,0:T(8,128)(2,1)}, bf16[512,256]{1,0:T(8,128)(2,1)S(1)}, u32[]{:S(2)}, u32[]{:S(2)}) collective-permute-start(bf16[512,256]{1,0:T(8,128)(2,1)} %bitcast.12), channel_id=1, source_target_pairs={{0,2},{2,0},{4,6},{6,4},{8,10},{10,8},{12,14},{14,12},{1,3},{3,1},... | collective-permute-start | bytes 786440 | tf_op jit(solution)/shard_map/ppermute | solution.py:363
  3.6 15.7 %collective-permute-start = (bf16[512,256]{1,0:T(8,128)(2,1)}, bf16[512,256]{1,0:T(8,128)(2,1)S(1)}, u32[]{:S(2)}, u32[]{:S(2)}) collective-permute-start(bf16[512,256]{1,0:T(8,128)(2,1)} %bitcast.13), channel_id=1, source_target_pairs={{2,4},{6,8},{10,12},{4,2},{8,6},{12,10},{3,5},{7,9},{11,13},{5,3},... | collective-permute-start | bytes 786440 | tf_op jit(solution)/shard_map/ppermute | solution.py:363
  5.1 8.6 %copy-start = (bf16[1,512,256]{2,1,0:T(8,128)(2,1)S(1)}, bf16[1,512,256]{2,1,0:T(8,128)(2,1)}, u32[]{:S(2)}) copy-start(bf16[1,512,256]{2,1,0:T(8,128)(2,1)} %param.10) | copy-start | bytes 786436
  5.1 8.6 %copy-start.1 = (s32[9,512]{1,0:T(8,128)S(1)}, s32[9,512]{1,0:T(8,128)}, u32[]{:S(2)}) copy-start(s32[9,512]{1,0:T(8,128)} %neighbours_hbm.1) | copy-start | bytes 55300
  5.1 8.6 %copy-start.2 = (f32[9,256]{1,0:T(8,128)S(1)}, f32[9,256]{1,0:T(8,128)}, u32[]{:S(2)}) copy-start(f32[9,256]{1,0:T(8,128)} %weights_hbm.1) | copy-start | bytes 27652
  5.1 8.6 %copy-start.3 = (f32[8,512]{1,0:T(8,128)S(1)}, f32[8,512]{1,0:T(8,128)}, u32[]{:S(2)}) copy-start(f32[8,512]{1,0:T(8,128)} %target_hbm.1) | copy-start | bytes 49156
  5.1 8.6 %copy-start.4 = (f32[1024]{0:T(1024)S(1)}, f32[1024]{0:T(1024)}, u32[]{:S(2)}) copy-start(f32[1024]{0:T(1024)} %param.16) | copy-start | bytes 12292
  5.1 8.6 %copy-start.5 = (bf16[8,256]{1,0:T(8,128)(2,1)S(1)}, bf16[8,256]{1,0:T(8,128)(2,1)}, u32[]{:S(2)}) copy-start(bf16[8,256]{1,0:T(8,128)(2,1)} %head_in.1) | copy-start | bytes 12292
  5.2 8.6 %copy-start.6 = (f32[256]{0:T(256)S(1)}, f32[256]{0:T(256)}, u32[]{:S(2)}) copy-start(f32[256]{0:T(256)} %param.18) | copy-start | bytes 3076
  5.2 8.5 %copy-start.7 = (f32[256]{0:T(256)S(1)}, f32[256]{0:T(256)}, u32[]{:S(2)}) copy-start(f32[256]{0:T(256)} %param.14) | copy-start | bytes 3076
  6.0 21.5 %all-to-all-start = ((bf16[8,128,256]{2,1,0:T(8,128)(2,1)}), bf16[8,128,256]{2,1,0:T(8,128)(2,1)S(1)}, u32[]{:S(2)}, u32[]{:S(2)}) async-start(bf16[8,128,256]{2,1,0:T(8,128)(2,1)} %shard_map.145), calls=%async_computation | async-start | bytes 1048576 | tf_op jit(solution)/shard_map/all_to_all | solution.py:396
  16.0 0.7 %copy-start.8 = (bf16[512,256]{1,0:T(8,128)(2,1)}, bf16[512,256]{1,0:T(8,128)(2,1)S(1)}, u32[]{:S(2)}) copy-start(bf16[512,256]{1,0:T(8,128)(2,1)S(1)} %get-tuple-element.87.features) | copy-start | bytes 786436
  16.7 2.6 %copy-start.12 = (f32[8,512]{1,0:T(8,128)}, f32[8,512]{1,0:T(8,128)S(1)}, u32[]{:S(2)}) copy-start(f32[8,512]{1,0:T(8,128)S(1)} %get-tuple-element.65.bias) | copy-start | bytes 49156
  16.7 2.6 %copy-start.14 = (s32[9,512]{1,0:T(8,128)}, s32[9,512]{1,0:T(8,128)S(1)}, u32[]{:S(2)}) copy-start(s32[9,512]{1,0:T(8,128)S(1)} %get-tuple-element.54.neighbours) | copy-start | bytes 55300
  16.7 2.6 %copy-start.16 = (f32[9,256]{1,0:T(8,128)}, f32[9,256]{1,0:T(8,128)S(1)}, u32[]{:S(2)}) copy-start(f32[9,256]{1,0:T(8,128)S(1)} %get-tuple-element.55.weights) | copy-start | bytes 27652
  19.3 8.2 %copy-start.13 = (f32[8,512]{1,0:T(8,128)S(1)}, f32[8,512]{1,0:T(8,128)}, u32[]{:S(2)}) copy-start(f32[8,512]{1,0:T(8,128)} %copy-done.12) | copy-start | bytes 49156
  22.1 0.8 %copy-start.10 = (f32[512,256]{1,0:T(8,128)}, f32[512,256]{1,0:T(8,128)S(1)}, u32[]{:S(2)}) copy-start(f32[512,256]{1,0:T(8,128)S(1)} %get-tuple-element.78.mixed) | copy-start | bytes 1572868
  27.6 1.9 %collective-permute-start.2 = (bf16[8,128,256]{2,1,0:T(8,128)(2,1)S(1)}, bf16[8,128,256]{2,1,0:T(8,128)(2,1)S(1)}, u32[]{:S(2)}, u32[]{:S(2)}) collective-permute-start(bf16[8,128,256]{2,1,0:T(8,128)(2,1)S(1)} %all-to-all-done.part), channel_id=1, source_target_pairs={{0,1},{1,0},{2,3},{3,2},{4,5},{5,4},{6,7},{7,6},{8,9},{9,8},{10,11... | collective-permute-start | bytes 1572872 | tf_op jit(solution)/shard_map/ppermute | solution.py:367
  29.5 2.1 %copy-start.11 = (f32[512,256]{1,0:T(8,128)S(1)}, f32[512,256]{1,0:T(8,128)}, u32[]{:S(2)}) copy-start(f32[512,256]{1,0:T(8,128)} %copy-done.10) | copy-start | bytes 1572868
  30.3 1.2 %collective-permute-start.3 = (f32[8,512]{1,0:T(8,128)S(1)}, f32[8,512]{1,0:T(8,128)S(1)}, u32[]{:S(2)}, u32[]{:S(2)}) collective-permute-start(f32[8,512]{1,0:T(8,128)S(1)} %get-tuple-element.70.mine), channel_id=1, source_target_pairs={{0,1},{1,0},{2,3},{3,2},{4,5},{5,4},{6,7},{7,6},{8,9},{9,8},{10,11... | collective-permute-start | bytes 49160 | tf_op jit(solution)/shard_map/ppermute | solution.py:367
  31.5 4.1 %copy-start.9 = (bf16[512,256]{1,0:T(8,128)(2,1)S(1)}, bf16[512,256]{1,0:T(8,128)(2,1)}, u32[]{:S(2)}) copy-start(bf16[512,256]{1,0:T(8,128)(2,1)} %copy-done.8) | copy-start | bytes 786436
  33.3 2.3 %collective-permute-start.4 = (bf16[8,128,128]{2,1,0:T(8,128)(2,1)S(1)}, bf16[8,128,128]{2,1,0:T(8,128)(2,1)S(1)}, u32[]{:S(2)}, u32[]{:S(2)}) collective-permute-start(bf16[8,128,128]{2,1,0:T(8,128)(2,1)S(1)} %get-tuple-element.92), channel_id=1, source_target_pairs={{0,1},{1,0},{2,3},{3,2},{4,5},{5,4},{6,7},{7,6},{8,9},{9,8},{10,11... | collective-permute-start | bytes 786440 | tf_op jit(solution)/shard_map/ppermute | solution.py:367
  33.6 15.7 %collective-permute-start.6 = (bf16[512,256]{1,0:T(8,128)(2,1)S(1)}, bf16[512,256]{1,0:T(8,128)(2,1)S(1)}, u32[]{:S(2)}, u32[]{:S(2)}) collective-permute-start(bf16[512,256]{1,0:T(8,128)(2,1)S(1)} %get-tuple-element.94.mixed_grad.own), channel_id=1, source_target_pairs={{0,2},{2,0},{4,6},{6,4},{8,10},{10,8},{12,14},{14,12},{1,3},{3,1},... | collective-permute-start | bytes 786440 | tf_op jit(solution)/shard_map/ppermute | solution.py:363
  35.0 14.2 %collective-permute-start.5 = (bf16[512,256]{1,0:T(8,128)(2,1)S(1)}, bf16[512,256]{1,0:T(8,128)(2,1)S(1)}, u32[]{:S(2)}, u32[]{:S(2)}) collective-permute-start(bf16[512,256]{1,0:T(8,128)(2,1)S(1)} %get-tuple-element.94.mixed_grad.own), channel_id=1, source_target_pairs={{2,4},{6,8},{10,12},{4,2},{8,6},{12,10},{3,5},{7,9},{11,13},{5,3},... | collective-permute-start | bytes 786440 | tf_op jit(solution)/shard_map/ppermute | solution.py:363
  35.7 7.7 %copy-start.15 = (s32[9,512]{1,0:T(8,128)S(1)}, s32[9,512]{1,0:T(8,128)}, u32[]{:S(2)}) copy-start(s32[9,512]{1,0:T(8,128)} %copy-done.14) | copy-start | bytes 55300
  35.7 7.7 %copy-start.17 = (f32[9,256]{1,0:T(8,128)S(1)}, f32[9,256]{1,0:T(8,128)}, u32[]{:S(2)}) copy-start(f32[9,256]{1,0:T(8,128)} %copy-done.16) | copy-start | bytes 27652
  37.9 16.5 %all-to-all-start.1 = ((bf16[8,176,128]{2,1,0:T(8,128)(2,1)}), bf16[8,176,128]{2,1,0:T(8,128)(2,1)S(1)}, u32[]{:S(2)}, u32[]{:S(2)}) async-start(bf16[8,176,128]{2,1,0:T(8,128)(2,1)} %shard_map.152), calls=%async_computation.1 | async-start | bytes 720896 | tf_op jit(solution)/shard_map/all_to_all | solution.py:396
  54.4 1.4 %collective-permute-start.7 = (f32[176,128]{1,0:T(8,128)S(1)}, f32[176,128]{1,0:T(8,128)S(1)}, u32[]{:S(2)}, u32[]{:S(2)}) collective-permute-start(f32[176,128]{1,0:T(8,128)S(1)} %shard_map.155.ours), channel_id=1, source_target_pairs={{0,1},{1,0},{2,3},{3,2},{4,5},{5,4},{6,7},{7,6},{8,9},{9,8},{10,11... | collective-permute-start | bytes 270344 | tf_op jit(solution)/shard_map/ppermute | solution.py:367
